TPU v7x, 32 devices: a whole 2x2x4 slice. The times are simulated.
32 devices in a mesh: lat: 8 (over z, core), vec: 4 (over y, x).
Axes of the slice: x: 2, y: 2, z: 4, core: 2. Of those that a mesh axis runs over, the one named last changes fastest.
Arguments:
- vectors: bfloat16 [4, 64, 128, 1024], P(None, 'vec', 'lat'), may hold values from -6 to 6
- classical_spins: float32 [3, 128, 1024], P(None, 'lat'), may hold values from -1 to 1, as said below
- coefficients: float32 [5], replicated, may hold values from 0.4 to 1.6
Outputs:
- rotated_spins: float32 [3, 128, 1024], P(None, 'lat')
- local_fields: float32 [3, 128, 1024], P(None, 'lat')
Inputs may be any that keep to these rules, and one draw needn't show every extreme that they name: `classical_spins`: each site's spin has unit length.
All inputs are finite; a program needn't handle non-finite values.
Results may differ from a plain program's by a relative error of at most 0.0003.
Values sent between devices are 32-bit elements; how exact they have to be, the bound alone decides.
No kernel may reach another device: no remote copies, remote signals or barrier semaphores. Data moves between devices by JAX's collectives and lax.ppermute only.
A program may use at most 64 MiB of HBM per device.

v0:
```python
import jax
import jax.numpy as jnp
from jax import lax
from jax.sharding import PartitionSpec as P

STEPS = 4


coupling = 2.0
hopping = 1.0
inverse_bound = 1.0 / 6.5
time_step = 1.0


def with_halo(block, sides, width):
    for axis, dim in sides:
        count = lax.axis_size(axis)
        forward = [(i, i + 1) for i in range(count - 1)]
        forward.append((count - 1, 0))
        backward = [(target, source) for source, target in forward]
        low = lax.ppermute(
            lax.slice_in_dim(block, block.shape[dim] - width, None, axis=dim), axis, forward
        )
        high = lax.ppermute(lax.slice_in_dim(block, 0, width, axis=dim), axis, backward)
        block = jnp.concatenate([low, block, high], axis=dim)
    return block


def exchange_term(states, spins_here):
    spin_x = spins_here[0][None]
    spin_y = spins_here[1][None]
    spin_z = spins_here[2][None]
    up_real, up_imag, down_real, down_imag = (states[0], states[1], states[2], states[3])
    return jnp.stack(
        [
            spin_z * up_real + spin_x * down_real + spin_y * down_imag,
            spin_z * up_imag + spin_x * down_imag - spin_y * down_real,
            spin_x * up_real - spin_y * up_imag - spin_z * down_real,
            spin_x * up_imag + spin_y * up_real - spin_z * down_imag,
        ]
    )


def spin_density(probes, weighted):
    along_x = jnp.sum(
        probes[0] * weighted[2]
        + probes[1] * weighted[3]
        + probes[2] * weighted[0]
        + probes[3] * weighted[1],
        axis=0,
    )
    along_y = jnp.sum(
        probes[0] * weighted[3]
        - probes[1] * weighted[2]
        - probes[2] * weighted[1]
        + probes[3] * weighted[0],
        axis=0,
    )
    along_z = jnp.sum(
        probes[0] * weighted[0]
        + probes[1] * weighted[1]
        - probes[2] * weighted[2]
        - probes[3] * weighted[3],
        axis=0,
    )
    return jnp.stack([along_x, along_y, along_z])


def rotate_spins(spins_now, fields):
    magnitude = jnp.sqrt(jnp.sum(fields * fields, axis=0))
    rotation_angle = time_step * magnitude
    cosine = jnp.cos(rotation_angle)
    sine_ratio = jnp.sinc(rotation_angle / jnp.pi)
    half_ratio = 0.5 * jnp.sinc(rotation_angle / (2.0 * jnp.pi)) ** 2
    torque = jnp.cross(fields, spins_now, axis=0)
    projection = jnp.sum(fields * spins_now, axis=0)
    return (
        cosine * spins_now
        + time_step * sine_ratio * torque
        + time_step * time_step * half_ratio * projection * fields
    )


def apply_hamiltonian(padded, spins_here):
    middle = padded[:, :, 1:-1]
    neighbours = (
        padded[:, :, 2:] + padded[:, :, :-2] + jnp.roll(middle, 1, 3) + jnp.roll(middle, -1, 3)
    )
    return inverse_bound * (coupling * exchange_term(middle, spins_here) - hopping * neighbours)


def shards(vectors, classical_spins, coefficients):
    probes = vectors.astype(jnp.float32)
    count_all = vectors.shape[1] * lax.axis_size("vec")
    moments = coefficients[0] * probes
    previous = probes
    current = probes
    for degree in range(STEPS):
        padded = with_halo(current, (("lat", 2),), 1)
        following = apply_hamiltonian(padded, classical_spins)
        if degree > 0:
            following = 2.0 * following - previous
        moments = moments + coefficients[degree + 1] * following
        previous = current
        current = following
    partial_value = spin_density(probes, moments) * (coupling / count_all)
    summed_share = lax.psum_scatter(partial_value, "vec", scatter_dimension=2, tiled=True)
    share_width = summed_share.shape[2]
    spin_share = lax.dynamic_slice_in_dim(
        classical_spins, lax.axis_index("vec") * share_width, share_width, 2
    )
    turned = rotate_spins(spin_share, summed_share)
    rotated, fields = (
        lax.all_gather(turned, "vec", axis=2, tiled=True),
        lax.all_gather(summed_share, "vec", axis=2, tiled=True),
    )
    return (rotated, fields)


def solution(mesh):
    placed = (P(None, "vec", "lat", None), P(None, "lat", None), P())
    return jax.shard_map(
        shards,
        mesh=mesh,
        in_specs=placed,
        out_specs=(P(None, "lat", None), P(None, "lat", None)),
        check_vma=False,
    )
```

profile of v0, /device:TPU:0, one launch (start us, length us, event | category | flops | bytes accessed | tf_op | source)
XLA Modules:
  0.0 148.7 jit_solution(7484465507345490147)
XLA Ops:
  7.2 0.0 reduce-scatter.2.cloned.1.call-start
  7.2 2.8 %copy_convert_fusion = f32[4,16,16,1024]{3,1,2,0:T(8,128)S(1)} fusion(bf16[4,16,16,1024]{3,2,1,0:T(8,128)(2,1)} %param.4), kind=kLoop, calls=%fused_computation.36 | loop fusion | flops 1048576 | bytes 6291456 | tf_op jit(solution)/shard_map/convert_element_type | solution.py:93
  10.1 0.5 collective-permute-start.1
  10.6 0.0 copy-start.2
  10.6 0.0 copy-start.3
  10.6 4.1 %collective-permute-start = (f32[4,16,1,1024]{3,1,2,0:T(8,128)S(1)}, f32[4,16,1,1024]{3,1,2,0:T(8,128)S(1)}, u32[]{:S(2)}, u32[]{:S(2)}) collective-permute-start(f32[4,16,1,1024]{3,1,2,0:T(8,128)S(1)} %get-tuple-element.44), channel_id=1, source_target_pairs={{4,0},{8,4},{12,8},{16,12},{20,16},{24,20},{28,24},{0,28},{5,1},{9... | collective-permute-start | bytes 786440 | tf_op jit(solution)/shard_map/ppermute | solution.py:24
  14.7 1.7 %fusion.65 = (f32[4,16,16,1023]{3,1,2,0:T(8,128)S(1)}, f32[4,16,16,1023]{3,1,2,0:T(8,128)S(1)}) fusion(f32[4,16,16,1024]{3,1,2,0:T(8,128)S(1)} %copy_convert_fusion), kind=kLoop, calls=%fused_computation.131 | loop fusion | bytes 16760832 | tf_op jit(solution)/shard_map/jit(_roll_static)/slice | solution.py:87
  16.4 0.0 copy-done.2
  16.4 0.0 copy-done.3
  16.4 0.6 fusion.66
  17.6 0.9 multiply_add_fusion.3
  18.5 0.2 fusion.64
  18.7 0.1 collective-permute-done.1
  18.9 0.5 collective-permute-done
  19.4 4.2 %broadcast_multiply_fusion = (f32[4,16,16,1024]{3,1,2,0:T(8,128)S(1)}, f32[4,16,16,1024]{3,1,2,0:T(8,128)}) fusion(f32[4,16,16,1]{3,1,2,0:T(8,128)S(1)} %get-tuple-element.47, f32[4,16,16,1023]{3,1,2,0:T(8,128)S(1)} %get-tuple-element.49, f32[4,16,16,1023]{3,1,2,0:T(8,128)S(1)} %get-tuple-element.48, f32[4,16,16,1]{3,1,2,0:T(8,128)S(1)} %get-tuple-element.46, ...), kind=kLoop, calls=%fused_computation.37 | loop fusion | flops 13631488 | bytes 25690112 | tf_op jit(solution)/shard_map/mul | solution.py:89
  23.6 2.1 %multiply_add_fusion.2 = (f32[1,16,16,1024]{3,1,2,0:T(8,128)S(1)}, f32[1,16,16,1024]{3,1,2,0:T(8,128)S(1)}, f32[1,16,16,1024]{3,1,2,0:T(8,128)}, f32[1,16,16,1024]{3,1,2,0:T(8,128)}) fusion(f32[4,16,16,1024]{3,1,2,0:T(8,128)S(1)} %get-tuple-element.7, f32[16,1024]{1,0:T(8,128)S(1)} %get-tuple-element.53, f32[16,1024]{1,0:T(8,128)S(1)} %get-tuple-element.52, ...), kind=kLoop, calls=%fused_computation.52 | loop fusion | flops 5242880 | bytes 8585216 | tf_op jit(solution)/shard_map/add | solution.py:36
  25.7 0.0 copy-start.1
  25.7 3.4 %fusion.60 = (f32[4,16,16,1023]{3,1,2,0:T(8,128)S(1)}, f32[4,16,16,1023]{3,1,2,0:T(8,128)}) fusion(f32[4,16,16,1024]{3,1,2,0:T(8,128)S(1)} %get-tuple-element.7), kind=kLoop, calls=%fused_computation.126 | loop fusion | bytes 16760832 | tf_op jit(solution)/shard_map/jit(_roll_static)/slice | solution.py:87
  29.1 2.0 %collective-permute-start.3 = (f32[4,16,1,1024]{3,1,2,0:T(8,128)S(1)}, f32[4,16,1,1024]{3,1,2,0:T(8,128)S(1)}, u32[]{:S(2)}, u32[]{:S(2)}) collective-permute-start(f32[4,16,1,1024]{3,1,2,0:T(8,128)S(1)} %get-tuple-element.43), channel_id=1, source_target_pairs={{0,4},{4,8},{8,12},{12,16},{16,20},{20,24},{24,28},{28,0},{1,5},{5... | collective-permute-start | bytes 786440 | tf_op jit(solution)/shard_map/ppermute | solution.py:21
  31.1 1.8 %collective-permute-start.2 = (f32[4,16,1,1024]{3,1,2,0:T(8,128)S(1)}, f32[4,16,1,1024]{3,1,2,0:T(8,128)S(1)}, u32[]{:S(2)}, u32[]{:S(2)}) collective-permute-start(f32[4,16,1,1024]{3,1,2,0:T(8,128)S(1)} %get-tuple-element.42), channel_id=1, source_target_pairs={{4,0},{8,4},{12,8},{16,12},{20,16},{24,20},{28,24},{0,28},{5,1},{9... | collective-permute-start | bytes 786440 | tf_op jit(solution)/shard_map/ppermute | solution.py:24
  33.0 0.2 fusion.61
  33.2 4.0 %collective-permute-done.3 = f32[4,16,1,1024]{3,1,2,0:T(8,128)S(1)} collective-permute-done((f32[4,16,1,1024]{3,1,2,0:T(8,128)S(1)}, f32[4,16,1,1024]{3,1,2,0:T(8,128)S(1)}, u32[]{:S(2)}, u32[]{:S(2)}) %collective-permute-start.3) | collective-permute-done | bytes 262176 | tf_op jit(solution)/shard_map/ppermute | solution.py:21
  37.2 0.0 collective-permute-done.2
  37.2 0.0 copy-done.1
  37.2 5.5 %fusion.19 = f32[4,16,16,1024]{3,1,2,0:T(8,128)S(1)} fusion(f32[4,16,16,1024]{3,1,2,0:T(8,128)S(1)} %get-tuple-element.7, f32[4,16,1,1024]{3,1,2,0:T(8,128)S(1)} %collective-permute-done.3, f32[4,16,1,1024]{3,1,2,0:T(8,128)S(1)} %collective-permute-done.2, f32[1,16,16,1024]{3,1,2,0:T(8,128)} %get-tuple-element.21, f32[1,16,16,1024]{3,1,2,0:T(8,128)} %get-tuple-element.20, ...), kind=kLoop, calls=%fused_computation.24 | loop fusion | flops 15728640 | bytes 23592960 | tf_op jit(solution)/shard_map/sub | solution.py:102
  42.7 0.7 multiply_add_fusion.1
  43.4 0.0 copy-start
  43.4 4.7 %fusion.57 = (f32[4,16,16,1023]{3,1,2,0:T(8,128)}, f32[4,16,16,1023]{3,1,2,0:T(8,128)}) fusion(f32[4,16,16,1024]{3,1,2,0:T(8,128)S(1)} %fusion.19), kind=kLoop, calls=%fused_computation.123 | loop fusion | bytes 16760832 | tf_op jit(solution)/shard_map/jit(_roll_static)/slice | solution.py:87
  48.1 2.5 %collective-permute-start.5 = (f32[4,16,1,1024]{3,1,2,0:T(8,128)S(1)}, f32[4,16,1,1024]{3,1,2,0:T(8,128)S(1)}, u32[]{:S(2)}, u32[]{:S(2)}) collective-permute-start(f32[4,16,1,1024]{3,1,2,0:T(8,128)S(1)} %get-tuple-element.37), channel_id=1, source_target_pairs={{0,4},{4,8},{8,12},{12,16},{16,20},{20,24},{24,28},{28,0},{1,5},{5... | collective-permute-start | bytes 786440 | tf_op jit(solution)/shard_map/ppermute | solution.py:21
  50.6 1.4 collective-permute-start.4
  51.9 0.2 fusion.58
  52.1 4.0 %collective-permute-done.5 = f32[4,16,1,1024]{3,1,2,0:T(8,128)S(1)} collective-permute-done((f32[4,16,1,1024]{3,1,2,0:T(8,128)S(1)}, f32[4,16,1,1024]{3,1,2,0:T(8,128)S(1)}, u32[]{:S(2)}, u32[]{:S(2)}) %collective-permute-start.5) | collective-permute-done | bytes 262176 | tf_op jit(solution)/shard_map/ppermute | solution.py:21
  56.1 0.5 collective-permute-done.4
  56.6 0.0 copy-done
  56.6 5.4 %fusion.13 = f32[4,16,16,1024]{3,1,2,0:T(8,128)S(1)} fusion(f32[4,16,16,1024]{3,1,2,0:T(8,128)S(1)} %fusion.19, f32[4,16,1,1024]{3,1,2,0:T(8,128)S(1)} %collective-permute-done.5, f32[4,16,1,1024]{3,1,2,0:T(8,128)S(1)} %collective-permute-done.4, f32[1,16,16,1024]{3,1,2,0:T(8,128)S(1)} %get-tuple-element.17, f32[1,16,16,1024]{3,1,2,0:T(8,128)S(1)} %get-tuple-element.16, ...), kind=kLoop, calls=%fused_computation.16 | loop fusion | flops 15728640 | bytes 25690112 | tf_op jit(solution)/shard_map/sub | solution.py:102
  62.0 2.4 %multiply_add_fusion = (f32[1,16,16,1024]{3,1,2,0:T(8,128)S(1)}, f32[1,16,16,1024]{3,1,2,0:T(8,128)}, f32[1,16,16,1024]{3,1,2,0:T(8,128)}, f32[1,16,16,1024]{3,1,2,0:T(8,128)}) fusion(f32[4,16,16,1024]{3,1,2,0:T(8,128)S(1)} %fusion.13, f32[16,1024]{1,0:T(8,128)S(1)} %get-tuple-element.53, f32[16,1024]{1,0:T(8,128)S(1)} %get-tuple-element.52, ...), kind=kLoop, calls=%fused_computation.44 | loop fusion | flops 5242880 | bytes 8585216 | tf_op jit(solution)/shard_map/add | solution.py:36
  64.5 4.7 %fusion.54 = (f32[4,16,16,1023]{3,1,2,0:T(8,128)}, f32[4,16,16,1023]{3,1,2,0:T(8,128)}) fusion(f32[4,16,16,1024]{3,1,2,0:T(8,128)S(1)} %fusion.13), kind=kLoop, calls=%fused_computation.120 | loop fusion | bytes 16760832 | tf_op jit(solution)/shard_map/jit(_roll_static)/slice | solution.py:87
  69.1 2.0 %collective-permute-start.7 = (f32[4,16,1,1024]{3,1,2,0:T(8,128)S(1)}, f32[4,16,1,1024]{3,1,2,0:T(8,128)S(1)}, u32[]{:S(2)}, u32[]{:S(2)}) collective-permute-start(f32[4,16,1,1024]{3,1,2,0:T(8,128)S(1)} %get-tuple-element.31), channel_id=1, source_target_pairs={{0,4},{4,8},{8,12},{12,16},{16,20},{20,24},{24,28},{28,0},{1,5},{5... | collective-permute-start | bytes 786440 | tf_op jit(solution)/shard_map/ppermute | solution.py:21
  71.1 1.8 %collective-permute-start.6 = (f32[4,16,1,1024]{3,1,2,0:T(8,128)S(1)}, f32[4,16,1,1024]{3,1,2,0:T(8,128)}, u32[]{:S(2)}, u32[]{:S(2)}) collective-permute-start(f32[4,16,1,1024]{3,1,2,0:T(8,128)S(1)} %get-tuple-element.30), channel_id=1, source_target_pairs={{4,0},{8,4},{12,8},{16,12},{20,16},{24,20},{28,24},{0,28},{5,1},{9... | collective-permute-start | bytes 786440 | tf_op jit(solution)/shard_map/ppermute | solution.py:24
  72.9 1.0 fusion.55
  73.9 3.2 %collective-permute-done.7 = f32[4,16,1,1024]{3,1,2,0:T(8,128)S(1)} collective-permute-done((f32[4,16,1,1024]{3,1,2,0:T(8,128)S(1)}, f32[4,16,1,1024]{3,1,2,0:T(8,128)S(1)}, u32[]{:S(2)}, u32[]{:S(2)}) %collective-permute-start.7) | collective-permute-done | bytes 262176 | tf_op jit(solution)/shard_map/ppermute | solution.py:21
  77.1 0.0 collective-permute-done.6
  77.2 12.2 %fusion.7 = f32[4,16,16,1024]{3,1,2,0:T(8,128)} fusion(f32[4,16,16,1024]{3,1,2,0:T(8,128)S(1)} %fusion.19, f32[4,16,16,1024]{3,1,2,0:T(8,128)S(1)} %fusion.13, f32[4,16,1,1024]{3,1,2,0:T(8,128)S(1)} %collective-permute-done.7, f32[4,16,1,1024]{3,1,2,0:T(8,128)} %collective-permute-done.6, f32[1,16,16,1024]{3,1,2,0:T(8,128)} %get-tuple-element.13, ...), kind=kLoop, calls=%fused_computation.8 | loop fusion | flops 25165824 | bytes 31981588 | tf_op jit(solution)/shard_map/add | solution.py:103
  89.4 3.5 %add_reduce_fusion.1 = (f32[16,1024]{1,0:T(8,128)S(1)}, f32[16,1024]{1,0:T(8,128)S(1)}, f32[16,1024]{1,0:T(8,128)S(1)}) fusion(f32[4,16,16,1024]{3,1,2,0:T(8,128)} %fusion.7, f32[4,16,16,1024]{3,1,2,0:T(8,128)S(1)} %copy_convert_fusion), kind=kLoop, calls=%fused_computation.40 | loop fusion | flops 6242304 | bytes 8585216 | tf_op jit(solution)/shard_map/reduce_sum | solution.py:45
  92.9 0.7 maximum_multiply_fusion.4
  93.6 0.0 reduce-scatter.2.cloned.1.call-update
  93.6 27.5 %reduce-scatter.2.cloned.1.call-done = f32[3,16,256]{2,1,0:T(8,128)} async-done(((f32[3,16,1024]{2,1,0:T(8,128)}), f32[3,16,256]{2,1,0:T(8,128)}) %reduce-scatter.2.cloned.1.call-update) | async-done | bytes 49168 | tf_op jit(solution)/shard_map/reduce_scatter | solution.py:107
  121.1 0.8 multiply_reduce_fusion.1
  121.9 0.8 subtract_bitcast_fusion.2
  122.7 0.1 sqrt_cosine_fusion
  122.8 0.8 fusion.25
  123.6 8.9 %all_gather.6 = f32[3,16,1024]{2,1,0:T(8,128)S(1)} all-gather(f32[3,16,256]{2,1,0:T(8,128)S(1)} %fusion.25), channel_id=1, replica_groups=mesh['lat'=8,'vec'=4] {'vec'}, dimensions={2}, use_global_device_ids=true | all-gather | bytes 245760 | tf_op jit(solution)/shard_map/all_gather | solution.py:114
  132.5 8.0 %all_gather.7 = f32[3,16,1024]{2,1,0:T(8,128)S(1)} all-gather(f32[3,16,256]{2,1,0:T(8,128)} %reduce-scatter.2.cloned.1.call-done), channel_id=1, replica_groups=mesh['lat'=8,'vec'=4] {'vec'}, dimensions={2}, use_global_device_ids=true | all-gather | bytes 245760 | tf_op jit(solution)/shard_map/all_gather | solution.py:115
  140.5 0.7 copy.13
  141.2 0.7 copy.14
  (5 shorter events, 0.2 us)
Async XLA Ops:
  7.2 113.9 %reduce-scatter.2.cloned.1.call-start = ((), (), s32[]{:S(2)}) async-start(), calls=%async_computation.1 | async-start | bytes 245760 | tf_op jit(solution)/shard_map/reduce_scatter | solution.py:107
  10.1 8.8 %collective-permute-start.1 = (f32[4,16,1,1024]{3,1,2,0:T(8,128)S(1)}, f32[4,16,1,1024]{3,1,2,0:T(8,128)S(1)}, u32[]{:S(2)}, u32[]{:S(2)}) collective-permute-start(f32[4,16,1,1024]{3,1,2,0:T(8,128)S(1)} %get-tuple-element.45), channel_id=1, source_target_pairs={{0,4},{4,8},{8,12},{12,16},{16,20},{20,24},{24,28},{28,0},{1,5},{5... | collective-permute-start | bytes 786440 | tf_op jit(solution)/shard_map/ppermute | solution.py:21
  10.6 5.8 %copy-start.2 = (f32[3,16,1024]{2,1,0:T(8,128)S(1)}, f32[3,16,1024]{2,1,0:T(8,128)}, u32[]{:S(2)}) copy-start(f32[3,16,1024]{2,1,0:T(8,128)} %param.5) | copy-start | bytes 589828
  10.6 5.8 %copy-start.3 = (f32[5]{0:T(128)S(1)}, f32[5]{0:T(128)}, u32[]{:S(2)}) copy-start(f32[5]{0:T(128)} %param.6) | copy-start | bytes 64
  10.6 8.7 %collective-permute-start = (f32[4,16,1,1024]{3,1,2,0:T(8,128)S(1)}, f32[4,16,1,1024]{3,1,2,0:T(8,128)S(1)}, u32[]{:S(2)}, u32[]{:S(2)}) collective-permute-start(f32[4,16,1,1024]{3,1,2,0:T(8,128)S(1)} %get-tuple-element.44), channel_id=1, source_target_pairs={{4,0},{8,4},{12,8},{16,12},{20,16},{24,20},{28,24},{0,28},{5,1},{9... | collective-permute-start | bytes 786440 | tf_op jit(solution)/shard_map/ppermute | solution.py:24
  25.7 11.4 %copy-start.1 = (bf16[4,16,16,1024]{3,2,1,0:T(8,128)(2,1)S(1)}, bf16[4,16,16,1024]{3,2,1,0:T(8,128)(2,1)}, u32[]{:S(2)}) copy-start(bf16[4,16,16,1024]{3,2,1,0:T(8,128)(2,1)} %param.4) | copy-start | bytes 6291460
  29.1 8.0 %collective-permute-start.3 = (f32[4,16,1,1024]{3,1,2,0:T(8,128)S(1)}, f32[4,16,1,1024]{3,1,2,0:T(8,128)S(1)}, u32[]{:S(2)}, u32[]{:S(2)}) collective-permute-start(f32[4,16,1,1024]{3,1,2,0:T(8,128)S(1)} %get-tuple-element.43), channel_id=1, source_target_pairs={{0,4},{4,8},{8,12},{12,16},{16,20},{20,24},{24,28},{28,0},{1,5},{5... | collective-permute-start | bytes 786440 | tf_op jit(solution)/shard_map/ppermute | solution.py:21
  31.1 6.1 %collective-permute-start.2 = (f32[4,16,1,1024]{3,1,2,0:T(8,128)S(1)}, f32[4,16,1,1024]{3,1,2,0:T(8,128)S(1)}, u32[]{:S(2)}, u32[]{:S(2)}) collective-permute-start(f32[4,16,1,1024]{3,1,2,0:T(8,128)S(1)} %get-tuple-element.42), channel_id=1, source_target_pairs={{4,0},{8,4},{12,8},{16,12},{20,16},{24,20},{28,24},{0,28},{5,1},{9... | collective-permute-start | bytes 786440 | tf_op jit(solution)/shard_map/ppermute | solution.py:24
  43.4 13.2 %copy-start = (f32[4,16,16,1024]{3,1,2,0:T(8,128)S(1)}, f32[4,16,16,1024]{3,1,2,0:T(8,128)}, u32[]{:S(2)}) copy-start(f32[4,16,16,1024]{3,1,2,0:T(8,128)} %get-tuple-element.8) | copy-start | bytes 12582916
  48.1 8.0 %collective-permute-start.5 = (f32[4,16,1,1024]{3,1,2,0:T(8,128)S(1)}, f32[4,16,1,1024]{3,1,2,0:T(8,128)S(1)}, u32[]{:S(2)}, u32[]{:S(2)}) collective-permute-start(f32[4,16,1,1024]{3,1,2,0:T(8,128)S(1)} %get-tuple-element.37), channel_id=1, source_target_pairs={{0,4},{4,8},{8,12},{12,16},{16,20},{20,24},{24,28},{28,0},{1,5},{5... | collective-permute-start | bytes 786440 | tf_op jit(solution)/shard_map/ppermute | solution.py:21
  50.6 6.1 %collective-permute-start.4 = (f32[4,16,1,1024]{3,1,2,0:T(8,128)S(1)}, f32[4,16,1,1024]{3,1,2,0:T(8,128)S(1)}, u32[]{:S(2)}, u32[]{:S(2)}) collective-permute-start(f32[4,16,1,1024]{3,1,2,0:T(8,128)S(1)} %get-tuple-element.36), channel_id=1, source_target_pairs={{4,0},{8,4},{12,8},{16,12},{20,16},{24,20},{28,24},{0,28},{5,1},{9... | collective-permute-start | bytes 786440 | tf_op jit(solution)/shard_map/ppermute | solution.py:24
  69.1 8.0 %collective-permute-start.7 = (f32[4,16,1,1024]{3,1,2,0:T(8,128)S(1)}, f32[4,16,1,1024]{3,1,2,0:T(8,128)S(1)}, u32[]{:S(2)}, u32[]{:S(2)}) collective-permute-start(f32[4,16,1,1024]{3,1,2,0:T(8,128)S(1)} %get-tuple-element.31), channel_id=1, source_target_pairs={{0,4},{4,8},{8,12},{12,16},{16,20},{20,24},{24,28},{28,0},{1,5},{5... | collective-permute-start | bytes 786440 | tf_op jit(solution)/shard_map/ppermute | solution.py:21
  71.1 6.1 %collective-permute-start.6 = (f32[4,16,1,1024]{3,1,2,0:T(8,128)S(1)}, f32[4,16,1,1024]{3,1,2,0:T(8,128)}, u32[]{:S(2)}, u32[]{:S(2)}) collective-permute-start(f32[4,16,1,1024]{3,1,2,0:T(8,128)S(1)} %get-tuple-element.30), channel_id=1, source_target_pairs={{4,0},{8,4},{12,8},{16,12},{20,16},{24,20},{28,24},{0,28},{5,1},{9... | collective-permute-start | bytes 786440 | tf_op jit(solution)/shard_map/ppermute | solution.py:24
Sparse Core Ops, SparseCore 0:
  93.7 27.3 reduce-scatter.1
where the time goes:
time: 149 us
  other arithmetic  43 us (29%)
  waiting for transfers between devices  39.8 us (27%)
  local copies, waits for them, and re-layouts  18.1 us (12%)
  blocking collectives  16.9 us (11%)
  starting transfers between devices  16.1 us (11%)
  between operations  14.7 us (10%)
    reduce_scatter x1, waiting for transfers between devices, shards(): lax.psum_scatter(partial_value, 'vec', scatter_dimension=2, tiled=True)  27.5 us
    slice x6, local copies, waits for them, and re-layouts, apply_hamiltonian(): jnp.roll(middle, -1, 3)  14.1 us
    add x1, other arithmetic, shards(): moments = moments + coefficients[degree + 1] * following  12.2 us
    ppermute x4, waiting for transfers between devices, with_halo(): lax.ppermute(lax.slice_in_dim(block, block.shape[dim] - width, None, axis...  11.3 us
    sub x2, other arithmetic, shards(): following = 2.0 * following - previous  10.8 us
    ppermute x4, starting transfers between devices, with_halo(): lax.ppermute(lax.slice_in_dim(block, 0, width, axis=dim), axis, backward)  9.16 us
    all_gather x1, blocking collectives, shards(): lax.all_gather(turned, 'vec', axis=2, tiled=True)  8.93 us
    all_gather x1, blocking collectives, shards(): lax.all_gather(summed_share, 'vec', axis=2, tiled=True)  7.98 us
  transfers between devices with their start and end apart: 9, of which 7 were waited for; matrix products, arithmetic and copies ran while one was open for 3% of the time, Pallas kernels for 0%

commit v1 on v0

v1 whole, which is shorter than its diff:
```python
import functools

import jax
import jax.numpy as jnp
from jax import lax
from jax.experimental import pallas as pl
from jax.experimental.pallas import tpu as pltpu
from jax.sharding import PartitionSpec as P

coupling = 2.0
hopping = 1.0
inverse_bound = 1.0 / 6.5
time_step = 1.0

LANES = 8
REACH = 4
HALO = 2


def scale_of(coefs, count):
    step = -hopping * inverse_bound
    return 8.0 * coefs[4] * step**4 * (coupling / count)


def ratios(coefs):
    step = -hopping * inverse_bound
    c = [jnp.full((LANES, 128), coefs[k], jnp.float32) for k in range(5)]
    top = 1.0 / (c[4] * (8.0 * step**4))
    return [
        (c[0] - c[2] + c[4]) * top,
        (c[1] - 3.0 * c[3]) * step * top,
        (2.0 * c[2] - 8.0 * c[4]) * step**2 * top,
        4.0 * c[3] * step**3 * top,
    ]


def wide(row, width):
    return jnp.concatenate([row] * (width // 128), axis=1)


def sideways(state):
    return [pltpu.roll(x, 1, 1) + pltpu.roll(x, x.shape[1] - 1, 1) for x in state]


def plus(*states):
    return [functools.reduce(lambda a, b: a + b, parts) for parts in zip(*states)]


def on_site(state, spins, ratio=None):
    sx, sy, sz = spins
    ur, ui, dr, di = state
    zp, zm = (sz, sz) if ratio is None else (sz + ratio, sz - ratio)
    return [
        zp * ur + sx * dr + sy * di,
        zp * ui + sx * di - sy * dr,
        sx * ur - sy * ui - zm * dr,
        sx * ui + sy * ur - zm * di,
    ]


def flat(state, spins, ratio=None):
    return plus(sideways(state), on_site(state, spins, ratio))


def density(r, w):
    return [
        r[0] * w[2] + r[1] * w[3] + r[2] * w[0] + r[3] * w[1],
        r[0] * w[3] - r[1] * w[2] - r[2] * w[1] + r[3] * w[0],
        r[0] * w[0] + r[1] * w[1] - r[2] * w[2] - r[3] * w[3],
    ]


def times(ratio, state):
    return [ratio * x for x in state]


def load(ref, *at):
    return [ref[(*at, k)] for k in range(ref.shape[len(at)])]


def save(ref, at, state):
    for k, x in enumerate(state):
        ref[(*at, k)] = x


def unroll(v_ref, comp, rows_ref):
    tiles, length, _ = rows_ref.shape
    states = v_ref[comp].astype(jnp.float32).reshape(length, tiles * 128)
    for t in range(tiles):
        rows_ref[t] = states[:, t * 128 : (t + 1) * 128]


def row_of(rows_ref, y, rows):
    tiles = rows_ref.shape[0]
    return jnp.concatenate([rows_ref[t, pl.ds(y, LANES, stride=rows), :] for t in range(tiles)], axis=1)


def edges_kernel(v_ref, low_ref, high_ref, rows_ref):
    rows, width = v_ref.shape[2:]
    for comp in range(4):
        unroll(v_ref, comp, rows_ref)
        for i in range(HALO):
            low_ref[i, comp] = row_of(rows_ref, i, rows)
            high_ref[i, comp] = row_of(rows_ref, rows - 1 - i, rows)


def edge_rows(vectors):
    _, count, rows, width = vectors.shape
    out = jax.ShapeDtypeStruct((HALO, 4, count, width), jnp.float32)
    spec = pl.BlockSpec((HALO, 4, LANES, width), lambda g: (0, 0, g, 0))
    return pl.pallas_call(
        edges_kernel,
        grid=(count // LANES,),
        in_specs=[pl.BlockSpec((4, LANES, rows, width), lambda g: (0, g, 0, 0))],
        out_specs=[spec, spec],
        out_shape=[out, out],
        scratch_shapes=[pltpu.VMEM((width // 128, LANES * rows, 128), jnp.float32)],
        compiler_params=pltpu.CompilerParams(vmem_limit_bytes=24 << 20),
        name="edge_rows",
    )(vectors)


def inner_kernel(coef_ref, v_ref, s_ref, f_ref, low_ref, high_ref, rows_ref, r_ref, sp_ref, a_ref, b_ref, acc_ref):
    rows, width = v_ref.shape[2:]
    step = pl.program_id(0)
    last = pl.num_programs(0) - 1
    rho = [wide(x, width) for x in ratios(coef_ref)]
    field = -(coupling / hopping)

    @pl.when(step == 0)
    def _():
        for y in range(rows + 2):
            for k in range(3):
                sp_ref[y, k] = jnp.broadcast_to(s_ref[k, y : y + 1, :] * field, (LANES, width))

    for comp in range(4):
        unroll(v_ref, comp, rows_ref)
        for y in range(rows):
            r_ref[y, comp] = row_of(rows_ref, y, rows)
        for i in range(REACH):
            low_ref[i, comp] = r_ref[i, comp]
            high_ref[i, comp] = r_ref[rows - 1 - i, comp]

    save(a_ref, (1,), load(r_ref, 0))
    save(a_ref, (rows + 2,), load(r_ref, rows - 1))

    def one(y, above, below):
        here = load(r_ref, y)
        out = flat(here, load(sp_ref, y + 1), rho[3])
        for other in above + below:
            out = plus(out, load(r_ref, other))
        save(a_ref, (y + 2,), out)

    one(0, [], [1])

    @pl.loop(1, rows - 1)
    def _(y):
        one(y, [y - 1], [y + 1])

    one(rows - 1, [rows - 2], [])

    save(b_ref, (0,), load(a_ref, 1))
    save(b_ref, (rows + 3,), load(a_ref, rows + 2))
    save(b_ref, (1,), plus(flat(load(a_ref, 1), load(sp_ref, 0)), load(a_ref, 2)))
    save(b_ref, (rows + 2,), plus(flat(load(a_ref, rows + 2), load(sp_ref, rows + 1)), load(a_ref, rows + 1)))

    def further(src, y, ratio):
        here = load(src, y + 2)
        out = flat(here, load(sp_ref, y + 1))
        out = plus(out, load(src, y + 1), load(src, y + 3))
        if ratio is not None:
            out = plus(out, times(ratio, load(r_ref, y)))
        return out

    @pl.loop(0, rows)
    def _(y):
        save(b_ref, (y + 2,), further(a_ref, y, rho[2]))

    save(a_ref, (1,), further(b_ref, -1, None))
    save(a_ref, (rows + 2,), further(b_ref, rows, None))

    @pl.loop(0, rows)
    def _(y):
        save(a_ref, (y + 2,), further(b_ref, y, rho[1]))

    @pl.loop(0, rows)
    def _(y):
        here = density(load(r_ref, y), further(a_ref, y, rho[0]))

        @pl.when(step == 0)
        def _():
            save(acc_ref, (y,), here)

        @pl.when(step > 0)
        def _():
            save(acc_ref, (y,), plus(here, load(acc_ref, y)))

    @pl.when(step == last)
    def _():
        for y in range(rows):
            for k in range(3):
                f_ref[k, y : y + 1, :] = jnp.sum(acc_ref[y, k], axis=0, keepdims=True)


def inner(coefficients, vectors, spins):
    _, count, rows, width = vectors.shape
    edge = jax.ShapeDtypeStruct((REACH, 4, count, width), jnp.float32)
    edge_spec = pl.BlockSpec((REACH, 4, LANES, width), lambda g: (0, 0, g, 0))
    f32 = jnp.float32
    return pl.pallas_call(
        inner_kernel,
        grid=(count // LANES,),
        in_specs=[
            pl.BlockSpec(memory_space=pltpu.SMEM),
            pl.BlockSpec((4, LANES, rows, width), lambda g: (0, g, 0, 0)),
            pl.BlockSpec((3, rows + 2, width), lambda g: (0, 0, 0)),
        ],
        out_specs=[pl.BlockSpec((3, rows, width), lambda g: (0, 0, 0)), edge_spec, edge_spec],
        out_shape=[jax.ShapeDtypeStruct((3, rows, width), f32), edge, edge],
        scratch_shapes=[
            pltpu.VMEM((width // 128, LANES * rows, 128), f32),
            pltpu.VMEM((rows, 4, LANES, width), f32),
            pltpu.VMEM((rows + 2, 3, LANES, width), f32),
            pltpu.VMEM((rows + 4, 4, LANES, width), f32),
            pltpu.VMEM((rows + 4, 4, LANES, width), f32),
            pltpu.VMEM((rows, 3, LANES, width), f32),
        ],
        compiler_params=pltpu.CompilerParams(vmem_limit_bytes=48 << 20),
        cost_estimate=pl.CostEstimate(flops=240 * vectors.size, bytes_accessed=8 << 20, transcendentals=0),
        name="inner",
    )(coefficients, vectors, spins)


def outer_kernel(coef_ref, own_ref, halo_ref, s_ref, f_ref, g_ref, sp_ref, facc_ref, gacc_ref):
    width = own_ref.shape[-1]
    step = pl.program_id(1)
    last = pl.num_programs(1) - 1
    rho = [wide(x, width) for x in ratios(coef_ref)]
    field = -(coupling / hopping)

    @pl.when(step == 0)
    def _():
        for y in range(5):
            for k in range(3):
                sp_ref[y, k] = jnp.broadcast_to(s_ref[0, k, y : y + 1, :] * field, (LANES, width))

    def spin(name):
        return load(sp_ref, ("B2", "B1", "A1", "A2", "A3").index(name))

    own = lambda i: load(own_ref, 0, i - 1)
    halo = lambda j: load(halo_ref, 0, j - 1)
    b1, b2 = halo(1), halo(2)

    a_b2 = plus(flat(b2, spin("B2"), rho[3]), b1)
    a_b1 = plus(flat(b1, spin("B1"), rho[3]), b2)
    b_b2 = plus(flat(a_b2, spin("B2")), a_b1, b2, times(rho[2], b2))
    b_b1 = plus(flat(a_b1, spin("B1")), a_b2, b1, times(rho[2], b1))
    b_a1 = plus(flat(b1, spin("A1")), a_b1)
    c_b1 = plus(flat(b_b1, spin("B1")), b_b2, b_a1, times(rho[1], b1))
    c_a1 = plus(flat(b_a1, spin("A1")), b_b1, b1)
    c_a2 = plus(flat(b1, spin("A2")), b_a1)
    w = [
        plus(flat(c_a1, spin("A1")), c_b1, c_a2),
        plus(flat(c_a2, spin("A2")), c_a1, b1),
        plus(flat(b1, spin("A3")), c_a2),
        b1,
    ]
    f = [density(own(i + 1), w[i]) for i in range(REACH)]
    a3 = own(3)
    spins = plus(*[spin(name) for name in ("A3", "A2", "A1", "B1")])
    w_b1 = plus(on_site(a3, spins, rho[3]), times(4.0, sideways(a3)), own(4))
    g = [density(b1, w_b1), density(b2, a3)]

    @pl.when(step == 0)
    def _():
        for i, x in enumerate(f):
            save(facc_ref, (i,), x)
        for i, x in enumerate(g):
            save(gacc_ref, (i,), x)

    @pl.when(step > 0)
    def _():
        for i, x in enumerate(f):
            save(facc_ref, (i,), plus(x, load(facc_ref, i)))
        for i, x in enumerate(g):
            save(gacc_ref, (i,), plus(x, load(gacc_ref, i)))

    @pl.when(step == last)
    def _():
        for acc, out, n in ((facc_ref, f_ref, REACH), (gacc_ref, g_ref, HALO)):
            for i in range(n):
                for k in range(3):
                    out[0, k, i : i + 1, :] = jnp.sum(acc[i, k], axis=0, keepdims=True)


def outer(coefficients, own, halo, spins):
    _, _, _, count, width = own.shape
    f32 = jnp.float32
    return pl.pallas_call(
        outer_kernel,
        grid=(2, count // LANES),
        in_specs=[
            pl.BlockSpec(memory_space=pltpu.SMEM),
            pl.BlockSpec((1, REACH, 4, LANES, width), lambda e, g: (e, 0, 0, g, 0)),
            pl.BlockSpec((1, HALO, 4, LANES, width), lambda e, g: (e, 0, 0, g, 0)),
            pl.BlockSpec((1, 3, 5, width), lambda e, g: (e, 0, 0, 0)),
        ],
        out_specs=[
            pl.BlockSpec((1, 3, REACH, width), lambda e, g: (e, 0, 0, 0)),
            pl.BlockSpec((1, 3, HALO, width), lambda e, g: (e, 0, 0, 0)),
        ],
        out_shape=[
            jax.ShapeDtypeStruct((2, 3, REACH, width), f32),
            jax.ShapeDtypeStruct((2, 3, HALO, width), f32),
        ],
        scratch_shapes=[
            pltpu.VMEM((5, 3, LANES, width), f32),
            pltpu.VMEM((REACH, 3, LANES, width), f32),
            pltpu.VMEM((HALO, 3, LANES, width), f32),
        ],
        compiler_params=pltpu.CompilerParams(vmem_limit_bytes=48 << 20),
        cost_estimate=pl.CostEstimate(flops=80 * own.size, bytes_accessed=4 << 20, transcendentals=0),
        name="outer",
    )(coefficients, own, halo, spins)


def rotate_spins(spins_now, fields):
    magnitude = jnp.sqrt(jnp.sum(fields * fields, axis=0))
    rotation_angle = time_step * magnitude
    cosine = jnp.cos(rotation_angle)
    sine_ratio = jnp.sinc(rotation_angle / jnp.pi)
    half_ratio = 0.5 * jnp.sinc(rotation_angle / (2.0 * jnp.pi)) ** 2
    torque = jnp.cross(fields, spins_now, axis=0)
    projection = jnp.sum(fields * spins_now, axis=0)
    return (
        cosine * spins_now
        + time_step * sine_ratio * torque
        + time_step * time_step * half_ratio * projection * fields
    )


def summed_over(part, axis):
    count = lax.axis_size(axis)
    if count & (count - 1):
        return lax.psum(part, axis)
    apart = 1
    while apart < count:
        part = part + lax.ppermute(part, axis, [(i, i ^ apart) for i in range(count)])
        apart *= 2
    return part


def shards(vectors, classical_spins, coefficients):
    count_all = vectors.shape[1] * lax.axis_size("vec")
    rows = vectors.shape[2]
    number = lax.axis_size("lat")
    forward = [(i, (i + 1) % number) for i in range(number)]
    backward = [(b, a) for a, b in forward]
    down = lambda x: lax.ppermute(x, "lat", forward)
    up = lambda x: lax.ppermute(x, "lat", backward)

    spin_low = down(classical_spins[:, rows - HALO :])
    spin_high = up(classical_spins[:, :HALO])
    low, high = edge_rows(vectors)
    halo_low, halo_high = down(high), up(low)

    spins_wide = jnp.concatenate([spin_low, classical_spins, spin_high], axis=1)
    f_in, own_low, own_high = inner(coefficients, vectors, spins_wide[:, HALO - 1 : rows + HALO + 1])
    own = jnp.stack([own_low, own_high])
    spin_edges = jnp.stack([spins_wide[:, :5], jnp.flip(spins_wide[:, -5:], 1)])
    f_out, g_out = outer(coefficients, own, jnp.stack([halo_low, halo_high]), spin_edges)

    total = f_in.at[:, :REACH].add(f_out[0]).at[:, rows - REACH :].add(jnp.flip(f_out[1], 1))
    total, given = summed_over((total), "vec"), summed_over(g_out, "vec")
    from_low, from_high = down(given[1]), up(given[0])
    total = total.at[:, :HALO].add(from_low).at[:, rows - HALO :].add(jnp.flip(from_high, 1))
    fields = total * scale_of(coefficients, count_all)
    return rotate_spins(classical_spins, fields), fields


def solution(mesh):
    placed = (P(None, "vec", "lat", None), P(None, "lat", None), P())
    return jax.shard_map(
        shards,
        mesh=mesh,
        in_specs=placed,
        out_specs=(P(None, "lat", None), P(None, "lat", None)),
        check_vma=False,
    )
```

time: 149 us -> 65.7 us (0.44)
  other arithmetic: 43 us -> 4.64 us
  waiting for transfers between devices: 39.8 us -> 10.6 us
  Pallas kernels: 0 us -> 28.3 us
  blocking collectives: 16.9 us -> 0 us
  between operations: 14.7 us -> 1.5 us
  local copies, waits for them, and re-layouts: 18.1 us -> 6.16 us
  starting transfers between devices: 16.1 us -> 14.2 us
    pallas_call x0 -> x3, Pallas kernels: none -> 28.3 us  [the longest x1 22.4 us: inner(): pl.pallas_call(inner_kernel, grid=(count // LANES,), in_specs=[pl.BlockSp...]
    reduce_scatter x1 -> x0, waiting for transfers between devices: 27.5 us -> none  [shards(): lax.psum_scatter(partial_value, 'vec', scatter_dimension=2, tiled=True)]
    add x5 -> x4, other arithmetic: 18.4 us -> 0.11 us  [summed_over(): part + lax.ppermute(part, axis, [(i, i ^ apart) for i in range(count)])]
    all_gather x2 -> x0, blocking collectives: 16.9 us -> none  [the longest x1 8.93 us: shards(): lax.all_gather(turned, 'vec', axis=2, tiled=True)]
    slice x13 -> x2, local copies, waits for them, and re-layouts: 16.8 us -> 1.55 us  [the longest x1 0.96 us: shards(): spin_low = down(classical_spins[:, rows - HALO:])]
    sub x2 -> x0, other arithmetic: 10.8 us -> none  [shards(): following = 2.0 * following - previous]
    mul x2 -> x0, other arithmetic: 4.92 us -> none  [the longest x1 4.23 us: apply_hamiltonian(): inverse_bound * (coupling * exchange_term(middle, spins_here) - hopping *...]
    reduce_sum x1 -> x0, other arithmetic: 3.5 us -> none  [spin_density(): jnp.sum(probes[0] * weighted[2] + probes[1] * weighted[3] + probes[2] * w...]
  transfers between devices with their start and end apart: 9 -> 10, of which waited for: 7 -> 5; matrix products, arithmetic and copies ran while one was open for 3% -> 8% of each run, Pallas kernels for 0% -> 36%
where the time goes in v1:
time: 65.7 us; the launch traced here: 65.4 us
  Pallas kernels  28.3 us (43%)
  starting transfers between devices  14.2 us (22%)
  waiting for transfers between devices  10.6 us (16%)
  local copies, waits for them, and re-layouts  6.16 us (9%)
  other arithmetic  4.64 us (7%)
  between operations  1.5 us (2%)
    pallas_call x1, Pallas kernels, inner(): pl.pallas_call(inner_kernel, grid=(count // LANES,), in_specs=[pl.BlockSp...  22.4 us
    ppermute x3, starting transfers between devices, shards(): up = lambda x: lax.ppermute(x, 'lat', backward)  8.89 us
    ppermute x4, waiting for transfers between devices, summed_over(): lax.ppermute(part, axis, [(i, i ^ apart) for i in range(count)])  8.68 us
    ppermute x4, starting transfers between devices, summed_over(): lax.ppermute(part, axis, [(i, i ^ apart) for i in range(count)])  5.26 us
    pallas_call x1, Pallas kernels, outer(): pl.pallas_call(outer_kernel, grid=(2, count // LANES), in_specs=[pl.Block...  5.06 us
    rev x1, local copies, waits for them, and re-layouts, shards(): spin_edges = jnp.stack([spins_wide[:, :5], jnp.flip(spins_wide[:, -5:], 1)])  2.45 us
    another operation x2, other arithmetic, shards(): spin_edges = jnp.stack([spins_wide[:, :5], jnp.flip(spins_wide[:, -5:], 1)])  1.65 us
    ppermute x3, waiting for transfers between devices, shards(): down = lambda x: lax.ppermute(x, 'lat', forward)  1.64 us
  transfers between devices with their start and end apart: 10, of which 5 were waited for; matrix products, arithmetic and copies ran while one was open for 8% of the time, Pallas kernels for 36%

profile of v1, /device:TPU:0, one launch (start us, length us, event | category | flops | bytes accessed | tf_op | source)
XLA Modules:
  0.0 65.4 jit_solution(10910143683523672330)
XLA Ops:
  0.6 0.0 copy-start.2
  0.6 1.0 %fusion.34 = (f32[3,2,1024]{2,1,0:T(2,128)S(1)}, f32[3,2,1024]{2,1,0:T(2,128)S(1)}) fusion(f32[3,16,1024]{2,1,0:T(8,128)} %param.13), kind=kLoop, calls=%fused_computation.78 | loop fusion | bytes 98304 | tf_op jit(solution)/shard_map/slice | solution.py:362
  1.6 4.5 %collective-permute-start.1 = (f32[3,2,1024]{2,1,0:T(2,128)S(1)}, f32[3,2,1024]{2,1,0:T(2,128)S(1)}, u32[]{:S(2)}, u32[]{:S(2)}) collective-permute-start(f32[3,2,1024]{2,1,0:T(2,128)S(1)} %get-tuple-element.74), channel_id=1, source_target_pairs={{4,0},{8,4},{12,8},{16,12},{20,16},{24,20},{28,24},{0,28},{5,1},{9... | collective-permute-start | bytes 73736 | tf_op jit(solution)/shard_map/ppermute | solution.py:360
  6.1 0.0 collective-permute-start
  6.2 0.0 copy-start
  6.2 1.6 %copy-done = bf16[4,16,16,1024]{3,2,1,0:T(8,128)(2,1)S(1)} copy-done((bf16[4,16,16,1024]{3,2,1,0:T(8,128)(2,1)S(1)}, bf16[4,16,16,1024]{3,2,1,0:T(8,128)(2,1)}, u32[]{:S(2)}) %copy-start) | copy-done | bytes 2097176
  7.7 0.0 copy-start.3
  7.7 0.0 copy-start.1
  7.7 0.8 %edge_rows.1 = (f32[2,4,16,1024]{3,2,1,0:T(8,128)S(1)}, f32[2,4,16,1024]{3,2,1,0:T(8,128)S(1)}) custom-call(bf16[4,16,16,1024]{3,2,1,0:T(8,128)(2,1)S(1)} %copy-done), custom_call_target="tpu_custom_call" | custom-call | tf_op jit(solution)/shard_map/edge_rows/pallas_call | solution.py:111
  8.6 3.6 %collective-permute-start.3 = (f32[2,4,16,1024]{3,2,1,0:T(8,128)S(1)}, f32[2,4,16,1024]{3,2,1,0:T(8,128)}, u32[]{:S(2)}, u32[]{:S(2)}) collective-permute-start(f32[2,4,16,1024]{3,2,1,0:T(8,128)S(1)} %get-tuple-element.62), channel_id=1, source_target_pairs={{4,0},{8,4},{12,8},{16,12},{20,16},{24,20},{28,24},{0,28},{5,1},{9... | collective-permute-start | bytes 1572872 | tf_op jit(solution)/shard_map/ppermute | solution.py:360
  12.2 0.0 collective-permute-start.2
  12.2 0.0 collective-permute-done.1
  12.2 0.0 collective-permute-done
  12.2 1.6 %fusion.2 = (f32[1,3,5,1024]{3,2,1,0:T(8,128)}, f32[3,5,1024]{2,1,0:T(8,128)S(1)}) fusion(f32[3,16,1024]{2,1,0:T(8,128)} %param.13, f32[3,2,1024]{2,1,0:T(2,128)S(1)} %collective-permute-done, f32[3,2,1024]{2,1,0:T(2,128)S(1)} %collective-permute-done.1), kind=kLoop, calls=%fused_computation.12 | loop fusion | flops 30720 | bytes 368640 | tf_op jit(solution)/shard_map/stack | solution.py:370
  13.8 2.4 %rev.12 = f32[3,5,1024]{2,1,0:T(8,128)} reverse(f32[3,5,1024]{2,1,0:T(8,128)S(1)} %get-tuple-element.72), dimensions={1} | reverse | bytes 122880 | tf_op jit(solution)/shard_map/jit(_flip)/rev | solution.py:370
  16.3 0.0 copy-done.3
  16.3 0.0 copy-start.5
  16.3 0.0 copy-start.6
  16.3 0.1 pad_maximum_fusion.2.s_ref
  16.3 0.0 copy-done.2
  16.3 0.0 copy-done.1
  16.4 22.4 %inner.1 = (f32[3,16,1024]{2,1,0:T(8,128)S(1)}, f32[4,4,16,1024]{3,2,1,0:T(8,128)S(1)}, f32[4,4,16,1024]{3,2,1,0:T(8,128)S(1)}) custom-call(f32[5]{0:T(128)S(1)} %copy-done.2, bf16[4,16,16,1024]{3,2,1,0:T(8,128)(2,1)S(1)} %copy-done.1, f32[3,18,1024]{2,1,0:T(8,128)S(1)} %pad_maximum_fusion.2.s_ref), custom_call_target="tpu_custom_call" | custom-call | flops 251658240 | bytes 8388608 | tf_op jit(solution)/shard_map/inner/pallas_call | solution.py:210
  38.8 0.0 copy-done.5
  38.8 0.0 copy-done.6
  38.9 0.2 pad_maximum_fusion.own_ref
  39.1 0.0 collective-permute-done.3
  39.1 0.0 collective-permute-done.2
  39.1 1.3 %pad_maximum_fusion.1.halo_ref = f32[2,2,4,16,1024]{4,3,2,1,0:T(8,128)S(1)} fusion(f32[1,2,4,16,1024]{4,3,2,1,0:T(8,128)} %bitcast.3, f32[1,2,4,16,1024]{4,3,2,1,0:T(8,128)} %bitcast.2), kind=kLoop, calls=%fused_computation.1 | loop fusion | flops 262144 | bytes 2097152 | tf_op jit(solution)/shard_map/stack | solution.py:371
  40.4 5.1 %outer.1 = (f32[2,3,4,1024]{3,2,1,0:T(4,128)S(1)}, f32[2,3,2,1024]{3,2,1,0:T(2,128)S(1)}) custom-call(f32[5]{0:T(128)S(1)} %copy-done.2, f32[2,4,4,16,1024]{4,3,2,1,0:T(8,128)S(1)} %pad_maximum_fusion.own_ref, f32[2,2,4,16,1024]{4,3,2,1,0:T(8,128)S(1)} %pad_maximum_fusion.1.halo_ref, f32[2,3,5,1024]{3,2,1,0:T(8,128)S(1)} %pad_maximum_fusion.4.s_ref), custom_call_target="tpu_custom_call" | custom-call | flops 41943040 | bytes 4194304 | tf_op jit(solution)/shard_map/outer/pallas_call | solution.py:299
  45.6 0.3 rev.13
  45.9 1.6 %collective-permute-start.4 = (f32[3,16,1024]{2,1,0:T(8,128)S(1)}, f32[3,16,1024]{2,1,0:T(8,128)S(1)}, u32[]{:S(2)}, u32[]{:S(2)}) collective-permute-start(f32[3,16,1024]{2,1,0:T(8,128)S(1)} %fusion.30), channel_id=1, source_target_pairs={{0,1},{1,0},{2,3},{3,2},{4,5},{5,4},{6,7},{7,6},{8,9},{9,8},{10,11... | collective-permute-start | bytes 589832 | tf_op jit(solution)/shard_map/ppermute | solution.py:348
  47.4 0.5 collective-permute-start.6
  48.0 4.2 %collective-permute-done.6 = f32[2,3,2,1024]{3,2,1,0:T(2,128)S(1)} collective-permute-done((f32[2,3,2,1024]{3,2,1,0:T(2,128)S(1)}, f32[2,3,2,1024]{3,2,1,0:T(2,128)S(1)}, u32[]{:S(2)}, u32[]{:S(2)}) %collective-permute-start.6) | collective-permute-done | bytes 49184 | tf_op jit(solution)/shard_map/ppermute | solution.py:348
  52.2 1.6 %collective-permute-start.7 = (f32[2,3,2,1024]{3,2,1,0:T(2,128)S(1)}, f32[2,3,2,1024]{3,2,1,0:T(2,128)S(1)}, u32[]{:S(2)}, u32[]{:S(2)}) collective-permute-start(f32[2,3,2,1024]{3,2,1,0:T(2,128)S(1)} %add.89), channel_id=1, source_target_pairs={{0,2},{1,3},{2,0},{3,1},{4,6},{5,7},{6,4},{7,5},{8,10},{9,11},{10,... | collective-permute-start | bytes 147464 | tf_op jit(solution)/shard_map/ppermute | solution.py:348
  53.8 2.9 %collective-permute-done.7 = f32[2,3,2,1024]{3,2,1,0:T(2,128)S(1)} collective-permute-done((f32[2,3,2,1024]{3,2,1,0:T(2,128)S(1)}, f32[2,3,2,1024]{3,2,1,0:T(2,128)S(1)}, u32[]{:S(2)}, u32[]{:S(2)}) %collective-permute-start.7) | collective-permute-done | bytes 49184 | tf_op jit(solution)/shard_map/ppermute | solution.py:348
  56.7 0.0 collective-permute-done.4
  56.7 1.6 %collective-permute-start.5 = (f32[3,16,1024]{2,1,0:T(8,128)S(1)}, f32[3,16,1024]{2,1,0:T(8,128)S(1)}, u32[]{:S(2)}, u32[]{:S(2)}) collective-permute-start(f32[3,16,1024]{2,1,0:T(8,128)S(1)} %add.87), channel_id=1, source_target_pairs={{0,2},{1,3},{2,0},{3,1},{4,6},{5,7},{6,4},{7,5},{8,10},{9,11},{10,... | collective-permute-start | bytes 589832 | tf_op jit(solution)/shard_map/ppermute | solution.py:348
  58.3 0.8 %collective-permute-start.9 = (f32[3,2,1024]{2,1,0:T(2,128)S(1)}, f32[3,2,1024]{2,1,0:T(2,128)S(1)}, u32[]{:S(2)}, u32[]{:S(2)}) collective-permute-start(f32[3,2,1024]{2,1,0:T(2,128)S(1)} %get-tuple-element.78), channel_id=1, source_target_pairs={{4,0},{8,4},{12,8},{16,12},{20,16},{24,20},{28,24},{0,28},{5,1},{9... | collective-permute-start | bytes 73736 | tf_op jit(solution)/shard_map/ppermute | solution.py:360
  59.1 0.0 collective-permute-start.8
  59.1 0.6 slice.165
  60.3 0.3 collective-permute-done.9
  60.6 0.3 rev.14
  60.9 1.6 %collective-permute-done.5 = f32[3,16,1024]{2,1,0:T(8,128)S(1)} collective-permute-done((f32[3,16,1024]{2,1,0:T(8,128)S(1)}, f32[3,16,1024]{2,1,0:T(8,128)S(1)}, u32[]{:S(2)}, u32[]{:S(2)}) %collective-permute-start.5) | collective-permute-done | bytes 196640 | tf_op jit(solution)/shard_map/ppermute | solution.py:348
  62.5 1.6 %collective-permute-done.8 = f32[3,2,1024]{2,1,0:T(2,128)S(1)} collective-permute-done((f32[3,2,1024]{2,1,0:T(2,128)S(1)}, f32[3,2,1024]{2,1,0:T(2,128)S(1)}, u32[]{:S(2)}, u32[]{:S(2)}) %collective-permute-start.8) | collective-permute-done | bytes 24608 | tf_op jit(solution)/shard_map/ppermute | solution.py:359
  64.2 0.0 copy-start.4
  64.3 0.4 sqrt_cosine_fusion
  64.7 0.7 %fusion.1 = f32[3,16,1024]{2,1,0:T(8,128)} fusion(f32[1,16,1024]{2,1,0:T(8,128)S(1)} %get-tuple-element.70, f32[1,16,1024]{2,1,0:T(8,128)S(1)} %get-tuple-element.69, f32[1,16,1024]{2,1,0:T(8,128)S(1)} %get-tuple-element.68, f32[3,16,1024]{2,1,0:T(8,128)S(1)} %get-tuple-element.67, f32[3,16,1024]{2,1,0:T(8,128)S(1)} %copy-done.3, ...), kind=kLoop, calls=%fused_computation.7 | loop fusion | flops 344064 | bytes 983040 | tf_op jit(solution)/shard_map/add | solution.py:336
  65.4 0.0 copy-done.4
  (13 shorter events, 0.3 us)
Async XLA Ops:
  0.6 15.7 %copy-start.2 = (f32[5]{0:T(128)S(1)}, f32[5]{0:T(128)}, u32[]{:S(2)}) copy-start(f32[5]{0:T(128)} %coef_ref.3) | copy-start | bytes 64
  1.6 10.6 %collective-permute-start.1 = (f32[3,2,1024]{2,1,0:T(2,128)S(1)}, f32[3,2,1024]{2,1,0:T(2,128)S(1)}, u32[]{:S(2)}, u32[]{:S(2)}) collective-permute-start(f32[3,2,1024]{2,1,0:T(2,128)S(1)} %get-tuple-element.74), channel_id=1, source_target_pairs={{4,0},{8,4},{12,8},{16,12},{20,16},{24,20},{28,24},{0,28},{5,1},{9... | collective-permute-start | bytes 73736 | tf_op jit(solution)/shard_map/ppermute | solution.py:360
  6.1 6.0 %collective-permute-start = (f32[3,2,1024]{2,1,0:T(2,128)S(1)}, f32[3,2,1024]{2,1,0:T(2,128)S(1)}, u32[]{:S(2)}, u32[]{:S(2)}) collective-permute-start(f32[3,2,1024]{2,1,0:T(2,128)S(1)} %get-tuple-element.73), channel_id=1, source_target_pairs={{0,4},{4,8},{8,12},{12,16},{16,20},{20,24},{24,28},{28,0},{1,5},{5... | collective-permute-start | bytes 73736 | tf_op jit(solution)/shard_map/ppermute | solution.py:359
  6.2 1.6 %copy-start = (bf16[4,16,16,1024]{3,2,1,0:T(8,128)(2,1)S(1)}, bf16[4,16,16,1024]{3,2,1,0:T(8,128)(2,1)}, u32[]{:S(2)}) copy-start(bf16[4,16,16,1024]{3,2,1,0:T(8,128)(2,1)} %v_ref.3) | copy-start | bytes 6291460
  7.7 8.5 %copy-start.3 = (f32[3,16,1024]{2,1,0:T(8,128)S(1)}, f32[3,16,1024]{2,1,0:T(8,128)}, u32[]{:S(2)}) copy-start(f32[3,16,1024]{2,1,0:T(8,128)} %param.13) | copy-start | bytes 589828
  7.7 8.6 %copy-start.1 = (bf16[4,16,16,1024]{3,2,1,0:T(8,128)(2,1)S(1)}, bf16[4,16,16,1024]{3,2,1,0:T(8,128)(2,1)}, u32[]{:S(2)}) copy-start(bf16[4,16,16,1024]{3,2,1,0:T(8,128)(2,1)} %v_ref.3) | copy-start | bytes 6291460
  8.6 30.5 %collective-permute-start.3 = (f32[2,4,16,1024]{3,2,1,0:T(8,128)S(1)}, f32[2,4,16,1024]{3,2,1,0:T(8,128)}, u32[]{:S(2)}, u32[]{:S(2)}) collective-permute-start(f32[2,4,16,1024]{3,2,1,0:T(8,128)S(1)} %get-tuple-element.62), channel_id=1, source_target_pairs={{4,0},{8,4},{12,8},{16,12},{20,16},{24,20},{28,24},{0,28},{5,1},{9... | collective-permute-start | bytes 1572872 | tf_op jit(solution)/shard_map/ppermute | solution.py:360
  12.2 26.9 %collective-permute-start.2 = (f32[2,4,16,1024]{3,2,1,0:T(8,128)S(1)}, f32[2,4,16,1024]{3,2,1,0:T(8,128)}, u32[]{:S(2)}, u32[]{:S(2)}) collective-permute-start(f32[2,4,16,1024]{3,2,1,0:T(8,128)S(1)} %get-tuple-element.61), channel_id=1, source_target_pairs={{0,4},{4,8},{8,12},{12,16},{16,20},{20,24},{24,28},{28,0},{1,5},{5... | collective-permute-start | bytes 1572872 | tf_op jit(solution)/shard_map/ppermute | solution.py:359
  16.3 22.5 %copy-start.5 = (f32[1,3,5,1024]{3,2,1,0:T(8,128)S(1)}, f32[1,3,5,1024]{3,2,1,0:T(8,128)}, u32[]{:S(2)}) copy-start(f32[1,3,5,1024]{3,2,1,0:T(8,128)} %get-tuple-element.71) | copy-start | bytes 184324
  16.3 22.5 %copy-start.6 = (f32[3,5,1024]{2,1,0:T(8,128)S(1)}, f32[3,5,1024]{2,1,0:T(8,128)}, u32[]{:S(2)}) copy-start(f32[3,5,1024]{2,1,0:T(8,128)} %rev.12) | copy-start | bytes 184324
  45.9 10.8 %collective-permute-start.4 = (f32[3,16,1024]{2,1,0:T(8,128)S(1)}, f32[3,16,1024]{2,1,0:T(8,128)S(1)}, u32[]{:S(2)}, u32[]{:S(2)}) collective-permute-start(f32[3,16,1024]{2,1,0:T(8,128)S(1)} %fusion.30), channel_id=1, source_target_pairs={{0,1},{1,0},{2,3},{3,2},{4,5},{5,4},{6,7},{7,6},{8,9},{9,8},{10,11... | collective-permute-start | bytes 589832 | tf_op jit(solution)/shard_map/ppermute | solution.py:348
  47.4 4.7 %collective-permute-start.6 = (f32[2,3,2,1024]{3,2,1,0:T(2,128)S(1)}, f32[2,3,2,1024]{3,2,1,0:T(2,128)S(1)}, u32[]{:S(2)}, u32[]{:S(2)}) collective-permute-start(f32[2,3,2,1024]{3,2,1,0:T(2,128)S(1)} %get-tuple-element.64), channel_id=1, source_target_pairs={{0,1},{1,0},{2,3},{3,2},{4,5},{5,4},{6,7},{7,6},{8,9},{9,8},{10,11... | collective-permute-start | bytes 147464 | tf_op jit(solution)/shard_map/ppermute | solution.py:348
  52.2 4.5 %collective-permute-start.7 = (f32[2,3,2,1024]{3,2,1,0:T(2,128)S(1)}, f32[2,3,2,1024]{3,2,1,0:T(2,128)S(1)}, u32[]{:S(2)}, u32[]{:S(2)}) collective-permute-start(f32[2,3,2,1024]{3,2,1,0:T(2,128)S(1)} %add.89), channel_id=1, source_target_pairs={{0,2},{1,3},{2,0},{3,1},{4,6},{5,7},{6,4},{7,5},{8,10},{9,11},{10,... | collective-permute-start | bytes 147464 | tf_op jit(solution)/shard_map/ppermute | solution.py:348
  56.7 5.7 %collective-permute-start.5 = (f32[3,16,1024]{2,1,0:T(8,128)S(1)}, f32[3,16,1024]{2,1,0:T(8,128)S(1)}, u32[]{:S(2)}, u32[]{:S(2)}) collective-permute-start(f32[3,16,1024]{2,1,0:T(8,128)S(1)} %add.87), channel_id=1, source_target_pairs={{0,2},{1,3},{2,0},{3,1},{4,6},{5,7},{6,4},{7,5},{8,10},{9,11},{10,... | collective-permute-start | bytes 589832 | tf_op jit(solution)/shard_map/ppermute | solution.py:348
  58.3 2.3 %collective-permute-start.9 = (f32[3,2,1024]{2,1,0:T(2,128)S(1)}, f32[3,2,1024]{2,1,0:T(2,128)S(1)}, u32[]{:S(2)}, u32[]{:S(2)}) collective-permute-start(f32[3,2,1024]{2,1,0:T(2,128)S(1)} %get-tuple-element.78), channel_id=1, source_target_pairs={{4,0},{8,4},{12,8},{16,12},{20,16},{24,20},{28,24},{0,28},{5,1},{9... | collective-permute-start | bytes 73736 | tf_op jit(solution)/shard_map/ppermute | solution.py:360
  59.1 5.0 %collective-permute-start.8 = (f32[3,2,1024]{2,1,0:T(2,128)S(1)}, f32[3,2,1024]{2,1,0:T(2,128)S(1)}, u32[]{:S(2)}, u32[]{:S(2)}) collective-permute-start(f32[3,2,1024]{2,1,0:T(2,128)S(1)} %get-tuple-element.79), channel_id=1, source_target_pairs={{0,4},{4,8},{8,12},{12,16},{16,20},{20,24},{24,28},{28,0},{1,5},{5... | collective-permute-start | bytes 73736 | tf_op jit(solution)/shard_map/ppermute | solution.py:359
  64.2 1.2 %copy-start.4 = (f32[3,16,1024]{2,1,0:T(8,128)}, f32[3,16,1024]{2,1,0:T(8,128)S(1)}, u32[]{:S(2)}) copy-start(f32[3,16,1024]{2,1,0:T(8,128)S(1)} %get-tuple-element.67) | copy-start | bytes 589828

commit v2 on v0

v2 whole, which is shorter than its diff:
```python
import functools

import jax
import jax.numpy as jnp
from jax import lax
from jax.experimental import pallas as pl
from jax.experimental.pallas import tpu as pltpu
from jax.sharding import PartitionSpec as P

coupling = 2.0
hopping = 1.0
inverse_bound = 1.0 / 6.5
time_step = 1.0

LANES = 8
REACH = 4
HALO = 2
MIB = 1 << 20


def ratios(coefs):
    step = -hopping * inverse_bound
    c = [jnp.full((LANES, 128), coefs[k], jnp.float32) for k in range(5)]
    top = c[4] * (8.0 * step**4)
    under = 1.0 / top
    return [
        (c[0] - c[2] + c[4]) * under,
        (c[1] - 3.0 * c[3]) * step * under,
        (2.0 * c[2] - 8.0 * c[4]) * step**2 * under,
        4.0 * c[3] * step**3 * under,
        top,
    ]


def block_of(width):
    return next(b for b in (512, 256, 128) if width % b == 0)


def shuffle(width, back=False):
    block = block_of(width)
    tiles = block // 128
    source = lax.broadcasted_iota(jnp.int32, (block, block), 1 if back else 0)
    target = lax.broadcasted_iota(jnp.int32, (block, block), 0 if back else 1)
    place = lax.rem(source, tiles) * 128 + lax.div(source, tiles)
    return (place == target).astype(jnp.float32).astype(jnp.bfloat16)


def moved(states, matrix):
    block = matrix.shape[0]
    out = []
    for at in range(0, states.shape[1], block):
        got = jnp.dot(states[:, at : at + block], matrix, preferred_element_type=jnp.float32)
        out += [got[:, t : t + 128] for t in range(0, block, 128)]
    return out


def moved_exactly(rows, matrix):
    parts = []
    for _ in range(3):
        parts.append(rows.astype(jnp.bfloat16))
        rows = rows - parts[-1].astype(jnp.float32)
    count = rows.shape[0]
    got = moved(jnp.concatenate(parts, axis=0), matrix)
    return [x[:count] + x[count : 2 * count] + x[2 * count :] for x in got]


def beside(tiles):
    count = len(tiles)
    group = block_of(count * 128) // 128
    blocks = count // group
    lane = lax.broadcasted_iota(jnp.int32, tiles[0].shape, 1)
    ends = [pltpu.roll(tiles[b * group + group - 1], 1, 1) for b in range(blocks)]
    starts = [pltpu.roll(tiles[b * group], 127, 1) for b in range(blocks)]
    out = []
    for b in range(blocks):
        left = ends[b] if blocks == 1 else jnp.where(lane == 0, ends[b - 1], ends[b])
        right = starts[b] if blocks == 1 else jnp.where(lane == 127, starts[(b + 1) % blocks], starts[b])
        for t in range(group):
            at = b * group + t
            out.append((left if t == 0 else tiles[at - 1]) + (right if t == group - 1 else tiles[at + 1]))
    return out


def on_site(state, spins, ratio=None):
    sx, sy, sz = spins
    ur, ui, dr, di = state
    zp, zm = (sz, sz) if ratio is None else (sz + ratio, sz - ratio)
    return [
        zp * ur + sx * dr + sy * di,
        zp * ui + sx * di - sy * dr,
        sx * ur - sy * ui - zm * dr,
        sx * ui + sy * ur - zm * di,
    ]


def density(r, w):
    return [
        r[0] * w[2] + r[1] * w[3] + r[2] * w[0] + r[3] * w[1],
        r[0] * w[3] - r[1] * w[2] - r[2] * w[1] + r[3] * w[0],
        r[0] * w[0] + r[1] * w[1] - r[2] * w[2] - r[3] * w[3],
    ]


def plus(*states):
    return [functools.reduce(lambda a, b: a + b, parts) for parts in zip(*states)]


def times(ratio, state):
    return [ratio * x for x in state]


def load(ref, at, t):
    return [ref[(*at, k, slice(None), pl.ds(t * 128, 128))] for k in range(ref.shape[len(at)])]


def save(ref, at, t, state):
    for k, x in enumerate(state):
        ref[(*at, k, slice(None), pl.ds(t * 128, 128))] = x


def by_tile(row):
    ref, at = row
    return [load(ref, at, t) for t in range(ref.shape[-1] // 128)]


def flat(row, spin, ratio=None):
    sides = [beside([x[k] for x in row]) for k in range(4)]
    for t, here in enumerate(row):
        yield t, plus([x[t] for x in sides], on_site(here, load(*spin, t), ratio))


def side_by_side(tiles):
    sub = lax.broadcasted_iota(jnp.int32, tiles[0].shape, 0)
    apart = 4
    while apart:
        first = (sub & apart) == 0
        tiles = [
            jnp.where(first, x + pltpu.roll(x, 8 - apart, 0), y + pltpu.roll(y, apart, 0))
            for x, y in zip(tiles[: len(tiles) // 2], tiles[len(tiles) // 2 :])
        ]
        apart //= 2
    return tiles[0]


def edges_kernel(v_hbm, s_hbm, low_ref, high_ref, v_ref, s_ref, rows_ref, v_sem, s_sem):
    _, count, rows, width = v_hbm.shape
    copies = {}
    for comp in range(4):
        for g in range(count // LANES):
            at = pl.ds(g * LANES, LANES)
            copies[g, comp] = pltpu.make_async_copy(v_hbm.at[comp, at], v_ref.at[g, comp], v_sem.at[g, comp])
            copies[g, comp].start()
    spins = pltpu.make_async_copy(s_hbm, s_ref, s_sem)
    spins.start()
    for (g, comp), copy in copies.items():
        copy.wait()
        states = v_ref[g, comp].astype(jnp.float32).reshape(LANES * rows, width)
        for t in range(width // 128):
            rows_ref[comp, t] = states[:, t * 128 : (t + 1) * 128]
        for i in range(HALO):
            to = pl.ds((i * 4 + comp) * count + g * LANES, LANES)
            for t in range(width // 128):
                at = pl.ds(t * 128, 128)
                low_ref[to, at] = rows_ref[comp, t, pl.ds(i, LANES, stride=rows), :]
                high_ref[to, at] = rows_ref[comp, t, pl.ds(rows - 1 - i, LANES, stride=rows), :]
    spins.wait()
    end = HALO * 4 * count
    for ref, at in ((low_ref, lambda i: i), (high_ref, lambda i: rows - 1 - i)):
        lines = [s_ref[k, at(i) : at(i) + 1] for k in range(3) for i in range(HALO)]
        ref[end:] = jnp.concatenate(lines + lines[:2], axis=0)


def edges(vectors, spins):
    _, count, rows, width = vectors.shape
    f32 = jnp.float32
    out = jax.ShapeDtypeStruct((HALO * 4 * count + 8, width), f32)
    return pl.pallas_call(
        edges_kernel,
        in_specs=[pl.BlockSpec(memory_space=pl.ANY)] * 2,
        out_shape=[out] * 2,
        scratch_shapes=[
            pltpu.VMEM((count // LANES, 4, LANES, rows, width), jnp.bfloat16),
            pltpu.VMEM(spins.shape, f32),
            pltpu.VMEM((4, width // 128, LANES * rows, 128), f32),
            pltpu.SemaphoreType.DMA((count // LANES, 4)),
            pltpu.SemaphoreType.DMA,
        ],
        compiler_params=pltpu.CompilerParams(vmem_limit_bytes=56 * MIB),
        name="edges",
    )(vectors, spins)


KEPT = REACH + 2


def inner_kernel(coef_ref, v_ref, s_ref, f_ref, kept_ref, rows_ref, r_ref, sp_ref, a_ref, b_ref, acc_ref, mat_ref):
    _, _, rows, width = v_ref.shape
    tiles = width // 128
    step = pl.program_id(0)
    last = pl.num_programs(0) - 1
    rho = ratios(coef_ref)

    @pl.when(step == 0)
    def _():
        mat_ref[...] = shuffle(width)
        acc_ref[...] = jnp.zeros_like(acc_ref)
        spins = s_ref[...].reshape(3 * rows, width) * -(coupling / hopping)
        for t, got in enumerate(moved_exactly(spins, mat_ref[...])):
            for y in range(rows):
                for k in range(3):
                    row = got[k * rows + y : k * rows + y + 1]
                    sp_ref[y, k, :, t * 128 : (t + 1) * 128] = jnp.broadcast_to(row, (LANES, 128))

    for t, got in enumerate(moved(v_ref[...].reshape(4 * LANES * rows, width), mat_ref[...])):
        rows_ref[t] = got
    for y in range(rows):
        for comp in range(4):
            for t in range(tiles):
                at = pl.ds(comp * LANES * rows + y, LANES, stride=rows)
                r_ref[y, comp, :, t * 128 : (t + 1) * 128] = rows_ref[t, at, :]

    def apply(dst, src, y, others, ratio, own):
        here = by_tile((src, (y,)))
        for t, x in flat(here, (sp_ref, (y,)), ratio if own else None):
            for o in others:
                x = plus(x, load(src, (o,), t))
            if not own:
                x = plus(x, times(ratio, load(r_ref, (y,), t)))
            dst(y, t, x)

    def pass_over(dst, src, ratio, own=False):
        apply(dst, src, 0, [1], ratio, own)
        apply(dst, src, rows - 1, [rows - 2], ratio, own)

        @pl.loop(1, rows - 1, unroll=2)
        def _(y):
            apply(dst, src, y, [y - 1, y + 1], ratio, own)

    def into(ref):
        return lambda y, t, x: save(ref, (y,), t, x)

    def fields(y, t, w):
        save(acc_ref, (y,), t, plus(density(load(r_ref, (y,), t), w), load(acc_ref, (y,), t)))

    pass_over(into(a_ref), r_ref, rho[3], own=True)
    pass_over(into(b_ref), a_ref, rho[2])
    for e in range(2):
        for i in range(REACH):
            kept_ref[0, e, i] = r_ref[rows - 1 - i if e else i]
        kept_ref[0, e, REACH] = a_ref[rows - 1 if e else 0]
        kept_ref[0, e, REACH + 1] = b_ref[rows - 1 if e else 0]
    pass_over(into(a_ref), b_ref, rho[1])
    pass_over(fields, a_ref, rho[0])

    @pl.when(step == last)
    def _():
        for k in range(3):
            for y in range(0, rows, 8):
                for t in range(tiles):
                    at = pl.ds(t * 128, 128)
                    f_ref[k, y : y + 8, at] = side_by_side([acc_ref[y + i, k, :, at] for i in range(8)])


def inner(coefficients, vectors, spins):
    _, count, rows, width = vectors.shape
    f32 = jnp.float32
    kept = (2, KEPT, 4, LANES, width)
    state = pltpu.VMEM((rows, 4, LANES, width), f32)
    return pl.pallas_call(
        inner_kernel,
        grid=(count // LANES,),
        in_specs=[
            pl.BlockSpec(memory_space=pltpu.SMEM),
            pl.BlockSpec((4, LANES, rows, width), lambda g: (0, g, 0, 0)),
            pl.BlockSpec((3, rows, width), lambda g: (0, 0, 0)),
        ],
        out_specs=[
            pl.BlockSpec((3, rows, width), lambda g: (0, 0, 0)),
            pl.BlockSpec((1, *kept), lambda g: (g, 0, 0, 0, 0, 0)),
        ],
        out_shape=[
            jax.ShapeDtypeStruct((3, rows, width), f32),
            jax.ShapeDtypeStruct((count // LANES, *kept), f32),
        ],
        scratch_shapes=[
            pltpu.VMEM((width // 128, 4 * LANES * rows, 128), f32),
            state,
            pltpu.VMEM((rows, 3, LANES, width), f32),
            state,
            state,
            pltpu.VMEM((rows, 3, LANES, width), f32),
            pltpu.VMEM((block_of(width),) * 2, jnp.bfloat16),
        ],
        compiler_params=pltpu.CompilerParams(vmem_limit_bytes=40 * MIB),
        cost_estimate=pl.CostEstimate(flops=240 * vectors.size, bytes_accessed=8 * MIB, transcendentals=0),
        name="inner",
    )(coefficients, vectors, spins)


SPINS = ("B2", "B1", "A1", "A2", "A3", "B1 to A3")


def given_kernel(coef_ref, kept_ref, low_ref, high_ref, s_ref, sp_ref, halo_ref, g_low_ref, g_high_ref):
    _, rows, width = s_ref.shape
    parts = kept_ref.shape[0]
    count = parts * LANES
    tiles = width // 128
    end = HALO * 4 * count
    rho = ratios(coef_ref)
    matrix = shuffle(width)
    lines = []
    for e, ref in enumerate((low_ref, high_ref)):
        for k in range(3):
            at = end + k * HALO
            lines += [ref[at + 1 : at + 2], ref[at : at + 1]]
            lines += [s_ref[k, y : y + 1] for y in ([rows - 1, rows - 2, rows - 3] if e else [0, 1, 2])]
    lines = jnp.concatenate(lines + lines[:2], axis=0) * -(coupling / hopping)
    for t, got in enumerate(moved_exactly(lines, matrix)):
        at = pl.ds(t * 128, 128)
        for e in range(2):
            for k in range(3):
                five = [got[(e * 3 + k) * 5 + i : (e * 3 + k) * 5 + i + 1] for i in range(5)]
                for i, row in enumerate(five + [five[1] + five[2] + five[3] + five[4]]):
                    sp_ref[e, i, k, :, at] = jnp.broadcast_to(row, (LANES, 128))
    for e, ref in enumerate((low_ref, high_ref)):
        for t, got in enumerate(moved(ref[:end].astype(jnp.bfloat16), matrix)):
            got = got.reshape(HALO, 4, parts, LANES, 128)
            for g in range(parts):
                halo_ref[g, e, :, :, :, t * 128 : (t + 1) * 128] = got[:, :, g]

    for e, ref in enumerate((g_low_ref, g_high_ref)):
        sums = [None] * tiles
        for g in range(parts):
            own = lambda i: (kept_ref, (g, e, i - 1))
            b1, b2 = (halo_ref, (g, e, 0)), (halo_ref, (g, e, 1))
            a3 = by_tile(own(3))
            sides = [beside([x[k] for x in a3]) for k in range(4)]
            for t in range(tiles):
                w = on_site(a3[t], load(sp_ref, (e, SPINS.index("B1 to A3")), t), rho[3])
                w = plus(w, times(4.0, [x[t] for x in sides]), load(*own(4), t))
                here = density(load(*b1, t), w) + density(load(*b2, t), a3[t])
                sums[t] = here if g == 0 else plus(sums[t], here)
        for t, x in enumerate(sums):
            rows_out = [x[i * 3 + k] for k in range(3) for i in range(HALO)]
            ref[:, t * 128 : (t + 1) * 128] = side_by_side(rows_out + rows_out[:2])


def given(coefficients, kept, low, high, spins):
    f32 = jnp.float32
    parts, width = kept.shape[0], spins.shape[-1]
    out = [(2, len(SPINS), 3, LANES, width), (parts, 2, HALO, 4, LANES, width), (8, width), (8, width)]
    vmem = pl.BlockSpec(memory_space=pltpu.VMEM)
    return pl.pallas_call(
        given_kernel,
        in_specs=[pl.BlockSpec(memory_space=pltpu.SMEM)] + [vmem] * 4,
        out_specs=[vmem] * len(out),
        out_shape=[jax.ShapeDtypeStruct(x, f32) for x in out],
        compiler_params=pltpu.CompilerParams(vmem_limit_bytes=32 * MIB),
        cost_estimate=pl.CostEstimate(flops=100 * low.size, bytes_accessed=4 * MIB, transcendentals=0),
        name="given",
    )(coefficients, kept, low, high, spins)


def outer_kernel(begin, end, part, coef_ref, kept_ref, sp_ref, halo_ref, *refs):
    width = halo_ref.shape[-1]
    tiles = width // 128
    rho = ratios(coef_ref)
    before = None if begin else refs[0]
    refs = refs if begin else refs[1:]
    if end:
        f_ref, below_ref, above_ref, out_ref, mid_ref, acc_ref = refs
    else:
        acc_ref, mid_ref = refs

    @pl.loop(0, 2)
    def _(e):
        spin = lambda name: (sp_ref, (e, SPINS.index(name)))
        own = lambda i: (kept_ref, (part, e, i - 1))
        a_in, b_in = (kept_ref, (part, e, REACH)), (kept_ref, (part, e, REACH + 1))
        b1, b2 = (halo_ref, (part, e, 0)), (halo_ref, (part, e, 1))
        names = ("a_b2", "a_b1", "b_b2", "b_b1", "b_a1", "c_b1", "c_a1", "c_a2")
        mid = {name: (mid_ref, (i,)) for i, name in enumerate(names)}

        def make(row, at, others, ratio=None, extra=None):
            for t, x in flat(by_tile(row), spin(at), ratio):
                for ref, place in others:
                    x = plus(x, load(ref, place, t))
                if extra is not None:
                    x = plus(x, times(extra[0], load(*extra[1], t)))
                yield t, x

        def state(name, *rest, **more):
            for t, x in make(*rest, **more):
                save(*mid[name], t, x)

        def fields(i, r, w):
            for t, x in w:
                x = density(load(*r, t), x)
                if before is not None:
                    x = plus(x, load(before, (e, i), t))
                save(acc_ref, (e, i), t, x)

        state("a_b2", b2, "B2", [b1], ratio=rho[3])
        state("a_b1", b1, "B1", [b2, own(1)], ratio=rho[3])
        state("b_b2", mid["a_b2"], "B2", [mid["a_b1"], b2], extra=(rho[2], b2))
        state("b_b1", mid["a_b1"], "B1", [mid["a_b2"], a_in, b1], extra=(rho[2], b1))
        state("b_a1", b1, "A1", [mid["a_b1"]])
        state("c_b1", mid["b_b1"], "B1", [mid["b_b2"], b_in, mid["b_a1"]], extra=(rho[1], b1))
        state("c_a1", mid["b_a1"], "A1", [mid["b_b1"], b1])
        state("c_a2", b1, "A2", [mid["b_a1"]])
        fields(0, own(1), make(mid["c_a1"], "A1", [mid["c_b1"], mid["c_a2"]]))
        fields(1, own(2), make(mid["c_a2"], "A2", [mid["c_a1"], b1]))
        fields(2, own(3), make(b1, "A3", [mid["c_a2"]]))
        fields(3, own(4), ((t, load(*b1, t)) for t in range(tiles)))

    if end:
        rows = f_ref.shape[1]
        out_ref[...] = f_ref[...]
        half = lax.broadcasted_iota(jnp.int32, (8, 128), 0) < REACH
        for t in range(tiles):
            at = pl.ds(t * 128, 128)
            for k in range(3):
                low = [acc_ref[0, i, k, :, at] for i in range(REACH)]
                high = [acc_ref[1, i, k, :, at] for i in reversed(range(REACH))]
                edge = side_by_side(low + high)
                out_ref[k, :8, at] += jnp.where(half, edge, 0.0)
                out_ref[k, rows - 8 :, at] += jnp.where(half, 0.0, edge)
        for k in range(3):
            for i in range(HALO):
                line = k * HALO + i
                out_ref[k, i : i + 1] += below_ref[line : line + 1]
                out_ref[k, rows - 1 - i : rows - i] += above_ref[line : line + 1]


def outer(coefficients, kept, sp, halo, part, so_far, rest):
    parts, width = kept.shape[0], kept.shape[-1]
    f32 = jnp.float32
    begin, end = part == 0, part == parts - 1
    acc, mid = (2, REACH, 3, LANES, width), (8, 4, LANES, width)
    more = ([] if begin else [so_far]) + (list(rest) if end else [])
    vmem = pl.BlockSpec(memory_space=pltpu.VMEM)
    return pl.pallas_call(
        functools.partial(outer_kernel, begin, end, part),
        in_specs=[pl.BlockSpec(memory_space=pltpu.SMEM)] + [vmem] * (3 + len(more)),
        out_specs=vmem,
        out_shape=jax.ShapeDtypeStruct(rest[0].shape if end else acc, f32),
        scratch_shapes=[pltpu.VMEM(mid, f32)] + ([pltpu.VMEM(acc, f32)] if end else []),
        compiler_params=pltpu.CompilerParams(vmem_limit_bytes=32 * MIB),
        cost_estimate=pl.CostEstimate(flops=300 * kept.size, bytes_accessed=3 * MIB, transcendentals=0),
        name="outer",
    )(coefficients, kept, sp, halo, *more)


def final_kernel(count_all, coef_ref, s_ref, f_ref, other_ref, rotated_ref, fields_ref):
    _, rows, width = s_ref.shape
    total = f_ref[...] + other_ref[...]
    scale = ratios(coef_ref)[4][:1, :1] * (coupling / count_all)
    got = moved_exactly(total.reshape(3 * rows, width), shuffle(width, back=True))
    for t, x in enumerate(got):
        at = pl.ds(t * 128, 128)
        field = [x[k * rows : (k + 1) * rows] * scale for k in range(3)]
        spin = [s_ref[k, :, at] for k in range(3)]
        size = jnp.sqrt(field[0] * field[0] + field[1] * field[1] + field[2] * field[2])
        half_angle = (0.5 * time_step) * size
        sine, cosine = jnp.sin(half_angle), jnp.cos(half_angle)
        some = half_angle > 0.0
        ratio = jnp.where(some, sine / jnp.where(some, half_angle, 1.0), 1.0)
        along = field[0] * spin[0] + field[1] * spin[1] + field[2] * spin[2]
        keep = 1.0 - 2.0 * sine * sine
        turn = time_step * ratio * cosine
        lift = (0.5 * time_step * time_step) * ratio * ratio * along
        for k in range(3):
            i, j = (k + 1) % 3, (k + 2) % 3
            cross = field[i] * spin[j] - field[j] * spin[i]
            rotated_ref[k, :, at] = keep * spin[k] + turn * cross + lift * field[k]
            fields_ref[k, :, at] = field[k]


def final(coefficients, spins, count_all, f, other):
    out = jax.ShapeDtypeStruct(spins.shape, jnp.float32)
    vmem = pl.BlockSpec(memory_space=pltpu.VMEM)
    return pl.pallas_call(
        functools.partial(final_kernel, count_all),
        in_specs=[pl.BlockSpec(memory_space=pltpu.SMEM)] + [vmem] * 3,
        out_specs=[vmem] * 2,
        out_shape=[out, out],
        compiler_params=pltpu.CompilerParams(vmem_limit_bytes=32 * MIB),
        name="final",
    )(coefficients, spins, f, other)


def shards(vectors, classical_spins, coefficients):
    across, number = lax.axis_size("vec"), lax.axis_size("lat")
    count_all = vectors.shape[1] * across
    parts = vectors.shape[1] // LANES

    def to_row(x, on):
        return lax.ppermute(x, "lat", [(i, (i + on) % number) for i in range(number)])

    def swap(x, step):
        steps = across.bit_length() - 1
        bit = lambda i: 1 << (step if i % 2 == 0 else steps - 1 - step)
        pairs = [(i * across + j, i * across + (j ^ bit(i))) for i in range(number) for j in range(across)]
        return lax.ppermute(x, ("lat", "vec"), pairs)

    low, high = edges(vectors, classical_spins)
    from_below, from_above = to_row(high, 1), to_row(low, -1)
    f, kept = inner(coefficients, vectors, classical_spins)
    sp, halo, g_low, g_high = given(coefficients, kept, from_below, from_above, classical_spins)
    below, above = to_row(g_high, 1), to_row(g_low, -1)
    so_far = None
    for part in range(parts):
        so_far = outer(coefficients, kept, sp, halo, part, so_far, (f, below, above))
    steps = across.bit_length() - 1
    if across != 1 << steps or steps == 0:
        return final(coefficients, classical_spins, count_all, lax.psum(so_far, "vec"), jnp.zeros_like(so_far))
    for step in range(steps - 1):
        so_far = so_far + swap(so_far, step)
    return final(coefficients, classical_spins, count_all, so_far, swap(so_far, steps - 1))


def solution(mesh):
    placed = (P(None, "vec", "lat", None), P(None, "lat", None), P())
    return jax.shard_map(
        shards,
        mesh=mesh,
        in_specs=placed,
        out_specs=(P(None, "lat", None), P(None, "lat", None)),
        check_vma=False,
    )
```

time: 149 us -> 44.4 us (0.30)
  other arithmetic: 43 us -> 0.02 us
  waiting for transfers between devices: 39.8 us -> 7.43 us
  Pallas kernels: 0 us -> 23.6 us
  local copies, waits for them, and re-layouts: 18.1 us -> 0.01 us
  blocking collectives: 16.9 us -> 0 us
  between operations: 14.7 us -> 0.73 us
  starting transfers between devices: 16.1 us -> 12.4 us
    reduce_scatter x1 -> x0, waiting for transfers between devices: 27.5 us -> none  [shards(): lax.psum_scatter(partial_value, 'vec', scatter_dimension=2, tiled=True)]
    pallas_call x0 -> x6, Pallas kernels: none -> 23.6 us  [the longest x1 12.8 us: inner(): pl.pallas_call(inner_kernel, grid=(count // LANES,), in_specs=[pl.BlockSp...]
    add x6 -> x1, other arithmetic: 19.2 us -> 0.02 us  [shards(): so_far = so_far + swap(so_far, step)]
    all_gather x2 -> x0, blocking collectives: 16.9 us -> none  [the longest x1 8.93 us: shards(): lax.all_gather(turned, 'vec', axis=2, tiled=True)]
    slice x13 -> x0, local copies, waits for them, and re-layouts: 16.8 us -> none  [the longest x6 14.1 us: apply_hamiltonian(): jnp.roll(middle, -1, 3)]
    sub x3 -> x0, other arithmetic: 11.6 us -> none  [the longest x2 10.8 us: shards(): following = 2.0 * following - previous]
    mul x2 -> x0, other arithmetic: 4.92 us -> none  [the longest x1 4.23 us: apply_hamiltonian(): inverse_bound * (coupling * exchange_term(middle, spins_here) - hopping *...]
    ppermute x8 -> x6, waiting for transfers between devices: 12.3 us -> 7.43 us  [the longest x2 7.42 us: swap(): return lax.ppermute(x, ('lat', 'vec'), pairs)]
  transfers between devices with their start and end apart: 9 -> 6, of which waited for: 7 -> 2; matrix products, arithmetic and copies ran while one was open for 3% -> 0% of each run, Pallas kernels for 0% -> 34%
where the time goes in v2:
time: 44.4 us; the launch traced here: 44.2 us
  Pallas kernels  23.6 us (53%)
  starting transfers between devices  12.4 us (28%)
  waiting for transfers between devices  7.43 us (17%)
  between operations  0.73 us (2%)
    pallas_call x1, Pallas kernels, inner(): pl.pallas_call(inner_kernel, grid=(count // LANES,), in_specs=[pl.BlockSp...  12.8 us
    ppermute x4, starting transfers between devices, to_row(): lax.ppermute(x, 'lat', [(i, (i + on) % number) for i in range(number)])  8.2 us
    ppermute x2, waiting for transfers between devices, swap(): return lax.ppermute(x, ('lat', 'vec'), pairs)  7.42 us
    pallas_call x2, Pallas kernels, outer(): pl.pallas_call(functools.partial(outer_kernel, begin, end, part), in_spec...  4.39 us
    ppermute x2, starting transfers between devices, swap(): return lax.ppermute(x, ('lat', 'vec'), pairs)  4.23 us
    pallas_call x1, Pallas kernels, edges(): pl.pallas_call(edges_kernel, in_specs=[pl.BlockSpec(memory_space=pl.ANY)]...  2.86 us
    pallas_call x1, Pallas kernels, final(): pl.pallas_call(functools.partial(final_kernel, count_all), in_specs=[pl.B...  1.88 us
    pallas_call x1, Pallas kernels, given(): pl.pallas_call(given_kernel, in_specs=[pl.BlockSpec(memory_space=pltpu.SM...  1.69 us
  transfers between devices with their start and end apart: 6, of which 2 were waited for; matrix products, arithmetic and copies ran while one was open for 0% of the time, Pallas kernels for 34%

profile of v2, /device:TPU:0, one launch (start us, length us, event | category | flops | bytes accessed | tf_op | source)
XLA Modules:
  0.0 44.2 jit_solution(14469969444538073352)
XLA Ops:
  0.6 0.0 copy-start.1
  0.6 0.0 copy-start
  0.6 0.0 copy-start.2
  0.7 2.9 %edges.1 = (f32[136,1024]{1,0:T(8,128)}, f32[136,1024]{1,0:T(8,128)}) custom-call(bf16[4,16,16,1024]{3,2,1,0:T(8,128)(2,1)} %v_hbm.1, f32[3,16,1024]{2,1,0:T(8,128)} %s_ref.5), custom_call_target="tpu_custom_call" | custom-call | tf_op jit(solution)/shard_map/edges/pallas_call | solution.py:177
  3.5 0.5 %collective-permute-start = (f32[136,1024]{1,0:T(8,128)}, f32[136,1024]{1,0:T(8,128)S(1)}, u32[]{:S(2)}, u32[]{:S(2)}) collective-permute-start(f32[136,1024]{1,0:T(8,128)} %get-tuple-element.11), channel_id=1, source_target_pairs={{0,4},{4,8},{8,12},{12,16},{16,20},{20,24},{24,28},{28,0},{1,5},{5... | collective-permute-start | bytes 1671176 | tf_op jit(solution)/shard_map/ppermute | solution.py:498
  4.0 4.1 %collective-permute-start.1 = (f32[136,1024]{1,0:T(8,128)}, f32[136,1024]{1,0:T(8,128)S(1)}, u32[]{:S(2)}, u32[]{:S(2)}) collective-permute-start(f32[136,1024]{1,0:T(8,128)} %get-tuple-element.12), channel_id=1, source_target_pairs={{0,28},{4,0},{8,4},{12,8},{16,12},{20,16},{24,20},{28,24},{1,29},{... | collective-permute-start | bytes 1671176 | tf_op jit(solution)/shard_map/ppermute | solution.py:498
  8.1 0.0 copy-done.1
  8.1 0.0 copy-done
  8.1 0.0 copy-done.2
  8.1 12.8 %inner.1 = (f32[3,16,1024]{2,1,0:T(8,128)S(1)}, f32[2,2,6,4,8,1024]{5,4,3,2,1,0:T(8,128)S(1)}) custom-call(f32[5]{0:T(128)S(1)} %copy-done.2, bf16[4,16,16,1024]{3,2,1,0:T(8,128)(2,1)S(1)} %copy-done, f32[3,16,1024]{2,1,0:T(8,128)S(1)} %copy-done.1), custom_call_target="tpu_custom_call" | custom-call | flops 251658240 | bytes 8388608 | tf_op jit(solution)/shard_map/inner/pallas_call | solution.py:269
  20.9 0.0 collective-permute-done.low_ref
  20.9 0.0 collective-permute-done.1.high_ref
  20.9 1.7 %given.1 = (f32[2,6,3,8,1024]{4,3,2,1,0:T(8,128)S(1)}, f32[2,2,2,4,8,1024]{5,4,3,2,1,0:T(8,128)S(1)}, f32[8,1024]{1,0:T(8,128)S(1)}, f32[8,1024]{1,0:T(8,128)S(1)}) custom-call(f32[5]{0:T(128)S(1)} %copy-done.2, f32[2,2,6,4,8,1024]{5,4,3,2,1,0:T(8,128)S(1)} %get-tuple-element.10.kept_ref, f32[136,1024]{1,0:T(8,128)S(1)} %collective-permute-done.low_ref, ...), custom_call_target="tpu_custom_call" | custom-call | flops 13926400 | bytes 4194304 | tf_op jit(solution)/shard_map/given/pallas_call | solution.py:353
  22.6 0.4 collective-permute-start.2
  23.0 3.2 %collective-permute-start.3 = (f32[8,1024]{1,0:T(8,128)S(1)}, f32[8,1024]{1,0:T(8,128)S(1)}, u32[]{:S(2)}, u32[]{:S(2)}) collective-permute-start(f32[8,1024]{1,0:T(8,128)S(1)} %get-tuple-element.17), channel_id=1, source_target_pairs={{0,28},{4,0},{8,4},{12,8},{16,12},{20,16},{24,20},{28,24},{1,29},{... | collective-permute-start | bytes 98312 | tf_op jit(solution)/shard_map/ppermute | solution.py:498
  26.2 2.1 %outer.2.refs_0_ = f32[2,4,3,8,1024]{4,3,2,1,0:T(8,128)S(1)} custom-call(f32[5]{0:T(128)S(1)} %copy-done.2, f32[2,2,6,4,8,1024]{5,4,3,2,1,0:T(8,128)S(1)} %get-tuple-element.10.kept_ref, f32[2,6,3,8,1024]{4,3,2,1,0:T(8,128)S(1)} %get-tuple-element.13.sp_ref, f32[2,2,2,4,8,1024]{5,4,3,2,1,0:T(8,128)S(1)} %get-tuple-element.14.halo_ref), custom_call_target="tpu_custom_call" | custom-call | flops 235929600 | bytes 3145728 | tf_op jit(solution)/shard_map/outer/pallas_call | solution.py:442
  28.3 0.0 collective-permute-done.2.refs_2_
  28.3 0.0 collective-permute-done.3.refs_3_
  28.3 2.3 %outer.3 = f32[3,16,1024]{2,1,0:T(8,128)S(1)} custom-call(f32[5]{0:T(128)S(1)} %copy-done.2, f32[2,2,6,4,8,1024]{5,4,3,2,1,0:T(8,128)S(1)} %get-tuple-element.10.kept_ref, f32[2,6,3,8,1024]{4,3,2,1,0:T(8,128)S(1)} %get-tuple-element.13.sp_ref, f32[2,2,2,4,8,1024]{5,4,3,2,1,0:T(8,128)S(1)} %get-tuple-element.14.halo_ref, ...), custom_call_target="tpu_custom_call" | custom-call | flops 235929600 | bytes 3145728 | tf_op jit(solution)/shard_map/outer/pallas_call | solution.py:442
  30.7 2.0 %collective-permute-start.4 = (f32[3,16,1024]{2,1,0:T(8,128)S(1)}, f32[3,16,1024]{2,1,0:T(8,128)S(1)}, u32[]{:S(2)}, u32[]{:S(2)}) collective-permute-start(f32[3,16,1024]{2,1,0:T(8,128)S(1)} %outer.3), channel_id=1, source_target_pairs={{0,1},{1,0},{2,3},{3,2},{4,6},{5,7},{6,4},{7,5},{8,9},{9,8},{10,11... | collective-permute-start | bytes 589832 | tf_op jit(solution)/shard_map/ppermute | solution.py:504
  32.7 3.8 %collective-permute-done.4 = f32[3,16,1024]{2,1,0:T(8,128)S(1)} collective-permute-done((f32[3,16,1024]{2,1,0:T(8,128)S(1)}, f32[3,16,1024]{2,1,0:T(8,128)S(1)}, u32[]{:S(2)}, u32[]{:S(2)}) %collective-permute-start.4) | collective-permute-done | bytes 196640 | tf_op jit(solution)/shard_map/ppermute | solution.py:504
  36.5 2.2 %collective-permute-start.5 = (f32[3,16,1024]{2,1,0:T(8,128)S(1)}, f32[3,16,1024]{2,1,0:T(8,128)S(1)}, u32[]{:S(2)}, u32[]{:S(2)}) collective-permute-start(f32[3,16,1024]{2,1,0:T(8,128)S(1)} %add.3.f_ref), channel_id=1, source_target_pairs={{0,2},{1,3},{2,0},{3,1},{4,5},{5,4},{6,7},{7,6},{8,10},{9,11},{10,... | collective-permute-start | bytes 589832 | tf_op jit(solution)/shard_map/ppermute | solution.py:504
  38.7 3.6 %collective-permute-done.5.other_ref = f32[3,16,1024]{2,1,0:T(8,128)S(1)} collective-permute-done((f32[3,16,1024]{2,1,0:T(8,128)S(1)}, f32[3,16,1024]{2,1,0:T(8,128)S(1)}, u32[]{:S(2)}, u32[]{:S(2)}) %collective-permute-start.5) | collective-permute-done | bytes 196640 | tf_op jit(solution)/shard_map/ppermute | solution.py:504
  42.3 1.9 %final.1 = (f32[3,16,1024]{2,1,0:T(8,128)}, f32[3,16,1024]{2,1,0:T(8,128)}) custom-call(f32[5]{0:T(128)S(1)} %copy-done.2, f32[3,16,1024]{2,1,0:T(8,128)S(1)} %copy-done.1, f32[3,16,1024]{2,1,0:T(8,128)S(1)} %add.3.f_ref, f32[3,16,1024]{2,1,0:T(8,128)S(1)} %collective-permute-done.5.other_ref), custom_call_target="tpu_custom_call" | custom-call | tf_op jit(solution)/shard_map/final/pallas_call | solution.py:482
  (1 shorter events, 0.0 us)
Async XLA Ops:
  0.6 7.5 %copy-start.1 = (f32[3,16,1024]{2,1,0:T(8,128)S(1)}, f32[3,16,1024]{2,1,0:T(8,128)}, u32[]{:S(2)}) copy-start(f32[3,16,1024]{2,1,0:T(8,128)} %s_ref.5) | copy-start | bytes 589828
  0.6 7.5 %copy-start = (bf16[4,16,16,1024]{3,2,1,0:T(8,128)(2,1)S(1)}, bf16[4,16,16,1024]{3,2,1,0:T(8,128)(2,1)}, u32[]{:S(2)}) copy-start(bf16[4,16,16,1024]{3,2,1,0:T(8,128)(2,1)} %v_hbm.1) | copy-start | bytes 6291460
  0.6 7.5 %copy-start.2 = (f32[5]{0:T(128)S(1)}, f32[5]{0:T(128)}, u32[]{:S(2)}) copy-start(f32[5]{0:T(128)} %coef_ref.9) | copy-start | bytes 64
  3.5 17.4 %collective-permute-start = (f32[136,1024]{1,0:T(8,128)}, f32[136,1024]{1,0:T(8,128)S(1)}, u32[]{:S(2)}, u32[]{:S(2)}) collective-permute-start(f32[136,1024]{1,0:T(8,128)} %get-tuple-element.11), channel_id=1, source_target_pairs={{0,4},{4,8},{8,12},{12,16},{16,20},{20,24},{24,28},{28,0},{1,5},{5... | collective-permute-start | bytes 1671176 | tf_op jit(solution)/shard_map/ppermute | solution.py:498
  4.0 16.9 %collective-permute-start.1 = (f32[136,1024]{1,0:T(8,128)}, f32[136,1024]{1,0:T(8,128)S(1)}, u32[]{:S(2)}, u32[]{:S(2)}) collective-permute-start(f32[136,1024]{1,0:T(8,128)} %get-tuple-element.12), channel_id=1, source_target_pairs={{0,28},{4,0},{8,4},{12,8},{16,12},{20,16},{24,20},{28,24},{1,29},{... | collective-permute-start | bytes 1671176 | tf_op jit(solution)/shard_map/ppermute | solution.py:498
  22.6 5.7 %collective-permute-start.2 = (f32[8,1024]{1,0:T(8,128)S(1)}, f32[8,1024]{1,0:T(8,128)S(1)}, u32[]{:S(2)}, u32[]{:S(2)}) collective-permute-start(f32[8,1024]{1,0:T(8,128)S(1)} %get-tuple-element.16), channel_id=1, source_target_pairs={{0,4},{4,8},{8,12},{12,16},{16,20},{20,24},{24,28},{28,0},{1,5},{5... | collective-permute-start | bytes 98312 | tf_op jit(solution)/shard_map/ppermute | solution.py:498
  23.0 5.3 %collective-permute-start.3 = (f32[8,1024]{1,0:T(8,128)S(1)}, f32[8,1024]{1,0:T(8,128)S(1)}, u32[]{:S(2)}, u32[]{:S(2)}) collective-permute-start(f32[8,1024]{1,0:T(8,128)S(1)} %get-tuple-element.17), channel_id=1, source_target_pairs={{0,28},{4,0},{8,4},{12,8},{16,12},{20,16},{24,20},{28,24},{1,29},{... | collective-permute-start | bytes 98312 | tf_op jit(solution)/shard_map/ppermute | solution.py:498
  30.7 5.8 %collective-permute-start.4 = (f32[3,16,1024]{2,1,0:T(8,128)S(1)}, f32[3,16,1024]{2,1,0:T(8,128)S(1)}, u32[]{:S(2)}, u32[]{:S(2)}) collective-permute-start(f32[3,16,1024]{2,1,0:T(8,128)S(1)} %outer.3), channel_id=1, source_target_pairs={{0,1},{1,0},{2,3},{3,2},{4,6},{5,7},{6,4},{7,5},{8,9},{9,8},{10,11... | collective-permute-start | bytes 589832 | tf_op jit(solution)/shard_map/ppermute | solution.py:504
  36.5 5.9 %collective-permute-start.5 = (f32[3,16,1024]{2,1,0:T(8,128)S(1)}, f32[3,16,1024]{2,1,0:T(8,128)S(1)}, u32[]{:S(2)}, u32[]{:S(2)}) collective-permute-start(f32[3,16,1024]{2,1,0:T(8,128)S(1)} %add.3.f_ref), channel_id=1, source_target_pairs={{0,2},{1,3},{2,0},{3,1},{4,5},{5,4},{6,7},{7,6},{8,10},{9,11},{10,... | collective-permute-start | bytes 589832 | tf_op jit(solution)/shard_map/ppermute | solution.py:504

commit v3 on v2

v3 whole, which is shorter than its diff:
```python
import functools

import jax
import jax.numpy as jnp
from jax import lax
from jax.experimental import pallas as pl
from jax.experimental.pallas import tpu as pltpu
from jax.sharding import PartitionSpec as P

coupling = 2.0
hopping = 1.0
inverse_bound = 1.0 / 6.5
time_step = 1.0

LANES = 8
REACH = 4
HALO = 2
MIB = 1 << 20


def ratios(coefs):
    step = -hopping * inverse_bound
    c = [jnp.full((LANES, 128), coefs[k], jnp.float32) for k in range(5)]
    top = c[4] * (8.0 * step**4)
    under = 1.0 / top
    return [
        (c[0] - c[2] + c[4]) * under,
        (c[1] - 3.0 * c[3]) * step * under,
        (2.0 * c[2] - 8.0 * c[4]) * step**2 * under,
        4.0 * c[3] * step**3 * under,
        top,
    ]


def block_of(width):
    return next(b for b in (512, 256, 128) if width % b == 0)


def shuffle(width, back=False):
    block = block_of(width)
    tiles = block // 128
    source = lax.broadcasted_iota(jnp.int32, (block, block), 1 if back else 0)
    target = lax.broadcasted_iota(jnp.int32, (block, block), 0 if back else 1)
    place = lax.rem(source, tiles) * 128 + lax.div(source, tiles)
    return (place == target).astype(jnp.float32).astype(jnp.bfloat16)


def moved(states, matrix):
    block = matrix.shape[0]
    out = []
    for at in range(0, states.shape[1], block):
        got = jnp.dot(states[:, at : at + block], matrix, preferred_element_type=jnp.float32)
        out += [got[:, t : t + 128] for t in range(0, block, 128)]
    return out


def moved_exactly(rows, matrix):
    parts = []
    for _ in range(3):
        parts.append(rows.astype(jnp.bfloat16))
        rows = rows - parts[-1].astype(jnp.float32)
    count = rows.shape[0]
    got = moved(jnp.concatenate(parts, axis=0), matrix)
    return [x[:count] + x[count : 2 * count] + x[2 * count :] for x in got]


def on_left(tiles):
    group = block_of(len(tiles) * 128) // 128
    lane = lax.broadcasted_iota(jnp.int32, tiles[0].shape, 1)
    ends = [pltpu.roll(x, 1, 1) for x in tiles[group - 1 :: group]]
    if len(ends) > 1:
        ends = [jnp.where(lane == 0, ends[b - 1], x) for b, x in enumerate(ends)]
    return [tiles[t - 1] if t % group else ends[t // group] for t in range(len(tiles))]


def on_right(tiles):
    group = block_of(len(tiles) * 128) // 128
    lane = lax.broadcasted_iota(jnp.int32, tiles[0].shape, 1)
    starts = [pltpu.roll(x, 127, 1) for x in tiles[::group]]
    if len(starts) > 1:
        starts = [jnp.where(lane == 127, starts[(b + 1) % len(starts)], x) for b, x in enumerate(starts)]
    return [tiles[t + 1] if (t + 1) % group else starts[t // group] for t in range(len(tiles))]


def beside(tiles):
    return [x + y for x, y in zip(on_left(tiles), on_right(tiles))]


def on_site(state, spins, ratio=None):
    sx, sy, sz = spins
    ur, ui, dr, di = state
    zp, zm = (sz, sz) if ratio is None else (sz + ratio, sz - ratio)
    return [
        zp * ur + sx * dr + sy * di,
        zp * ui + sx * di - sy * dr,
        sx * ur - sy * ui - zm * dr,
        sx * ui + sy * ur - zm * di,
    ]


def density(r, w):
    return [
        r[0] * w[2] + r[1] * w[3] + r[2] * w[0] + r[3] * w[1],
        r[0] * w[3] - r[1] * w[2] - r[2] * w[1] + r[3] * w[0],
        r[0] * w[0] + r[1] * w[1] - r[2] * w[2] - r[3] * w[3],
    ]


def plus(*states):
    return [functools.reduce(lambda a, b: a + b, parts) for parts in zip(*states)]


def times(ratio, state):
    return [ratio * x for x in state]


def load(ref, at, t):
    return [ref[(*at, k, slice(None), pl.ds(t * 128, 128))] for k in range(ref.shape[len(at)])]


def save(ref, at, t, state):
    for k, x in enumerate(state):
        ref[(*at, k, slice(None), pl.ds(t * 128, 128))] = x


def by_tile(row):
    ref, at = row
    return [load(ref, at, t) for t in range(ref.shape[-1] // 128)]


def flat(row, spin, ratio=None):
    sides = [beside([x[k] for x in row]) for k in range(4)]
    for t, here in enumerate(row):
        yield t, plus([x[t] for x in sides], on_site(here, load(*spin, t), ratio))


def side_by_side(tiles):
    sub = lax.broadcasted_iota(jnp.int32, tiles[0].shape, 0)
    apart = 4
    while apart:
        first = (sub & apart) == 0
        tiles = [
            jnp.where(first, x + pltpu.roll(x, 8 - apart, 0), y + pltpu.roll(y, apart, 0))
            for x, y in zip(tiles[: len(tiles) // 2], tiles[len(tiles) // 2 :])
        ]
        apart //= 2
    return tiles[0]


def edges_kernel(v_ref, s_ref, low_ref, high_ref, rows_ref):
    _, count, rows, width = v_ref.shape
    for comp in range(4):
        for g in range(count // LANES):
            states = v_ref[comp, g * LANES : (g + 1) * LANES].astype(jnp.float32).reshape(LANES * rows, width)
            for t in range(width // 128):
                rows_ref[comp, g, t] = states[:, t * 128 : (t + 1) * 128]
            for i in range(HALO):
                to = pl.ds((i * 4 + comp) * count + g * LANES, LANES)
                for t in range(width // 128):
                    at = pl.ds(t * 128, 128)
                    low_ref[to, at] = rows_ref[comp, g, t, pl.ds(i, LANES, stride=rows), :]
                    high_ref[to, at] = rows_ref[comp, g, t, pl.ds(rows - 1 - i, LANES, stride=rows), :]
    end = HALO * 4 * count
    low_ref[end:] = s_ref[0]
    high_ref[end:] = s_ref[1]


def edges(vectors, spin_lines):
    _, count, rows, width = vectors.shape
    f32 = jnp.float32
    out = jax.ShapeDtypeStruct((HALO * 4 * count + 8, width), f32)
    vmem = pl.BlockSpec(memory_space=pltpu.VMEM)
    return pl.pallas_call(
        edges_kernel,
        in_specs=[vmem] * 2,
        out_specs=[vmem] * 2,
        out_shape=[out, out],
        scratch_shapes=[pltpu.VMEM((4, count // LANES, width // 128, LANES * rows, 128), f32)],
        compiler_params=pltpu.CompilerParams(vmem_limit_bytes=16 * MIB),
        name="edges",
    )(vectors, spin_lines)


KEPT = REACH + 2
GROUP = 8


def inner_kernel(coef_ref, v_ref, s_ref, f_ref, kept_ref, there_ref, back_ref, rows_ref, r_ref, sp_ref, a_ref, b_ref, sum_ref, acc_ref):
    _, count, rows, width = v_ref.shape
    tiles = width // 128
    rho = ratios(coef_ref)

    there_ref[...] = shuffle(width)
    acc_ref[...] = jnp.zeros_like(acc_ref)
    for ref in (r_ref, a_ref, b_ref):
        ref[rows] = jnp.zeros(ref.shape[1:], jnp.float32)
    spins = s_ref[...].reshape(3 * rows, width) * -(coupling / hopping)
    for t, got in enumerate(moved_exactly(spins, there_ref[...])):
        for y in range(rows):
            for k in range(3):
                row = got[k * rows + y : k * rows + y + 1]
                sp_ref[y, k, :, t * 128 : (t + 1) * 128] = jnp.broadcast_to(row, (LANES, 128))

    def pass_over(dst, src, ratio, own=False):
        sum_ref[...] = src[0]

        @pl.loop(0, rows, step=GROUP)
        def _(start):
            below = [[sum_ref[k, :, t * 128 : (t + 1) * 128] for t in range(tiles)] for k in range(4)]
            for y in [start + i for i in range(GROUP)]:
                here = by_tile((src, (y,)))
                pairs = []
                for k in range(4):
                    right = on_right([x[k] for x in here])
                    pairs.append([right[t] + src[y + 1, k, :, t * 128 : (t + 1) * 128] for t in range(tiles)])
                left = [on_left(x) for x in below]
                for t in range(tiles):
                    x = plus([x[t] for x in pairs], [x[t] for x in left])
                    x = plus(x, on_site(here[t], load(sp_ref, (y,), t), ratio if own else None))
                    if not own:
                        x = plus(x, times(ratio, load(r_ref, (y,), t)))
                    dst(y, t, x)
                below = pairs
            for k in range(4):
                for t in range(tiles):
                    sum_ref[k, :, t * 128 : (t + 1) * 128] = below[k][t]

    def into(ref):
        return lambda y, t, x: save(ref, (y,), t, x)

    def fields(y, t, w):
        save(acc_ref, (y,), t, plus(density(load(r_ref, (y,), t), w), load(acc_ref, (y,), t)))

    @pl.loop(0, count // LANES)
    def _(g):
        states = v_ref[:, pl.ds(pl.multiple_of(g * LANES, LANES), LANES)]
        for t, got in enumerate(moved(states.reshape(4 * LANES * rows, width), there_ref[...])):
            rows_ref[t] = got

        for y in range(rows):
            for comp in range(4):
                for t in range(tiles):
                    at = pl.ds(comp * LANES * rows + y, LANES, stride=rows)
                    r_ref[y, comp, :, t * 128 : (t + 1) * 128] = rows_ref[t, at, :]

        pass_over(into(a_ref), r_ref, rho[3], own=True)
        pass_over(into(b_ref), a_ref, rho[2])
        for e in range(2):
            for i in range(REACH):
                kept_ref[g, e, i] = r_ref[rows - 1 - i if e else i]
            kept_ref[g, e, REACH] = a_ref[rows - 1 if e else 0]
            kept_ref[g, e, REACH + 1] = b_ref[rows - 1 if e else 0]
        pass_over(into(a_ref), b_ref, rho[1])
        pass_over(fields, a_ref, rho[0])

    for k in range(3):
        for y in range(0, rows, 8):
            for t in range(tiles):
                at = pl.ds(t * 128, 128)
                f_ref[k, y : y + 8, at] = side_by_side([acc_ref[y + i, k, :, at] for i in range(8)])
    back_ref[...] = shuffle(width, back=True)


def inner(coefficients, vectors, spins):
    _, count, rows, width = vectors.shape
    f32 = jnp.float32
    block = block_of(width)
    matrix = jax.ShapeDtypeStruct((block, block), jnp.bfloat16)
    state = pltpu.VMEM((rows + 1, 4, LANES, width), f32)
    vmem = pl.BlockSpec(memory_space=pltpu.VMEM)
    return pl.pallas_call(
        inner_kernel,
        in_specs=[pl.BlockSpec(memory_space=pltpu.SMEM), vmem, vmem],
        out_specs=[vmem] * 4,
        out_shape=[
            jax.ShapeDtypeStruct((3, rows, width), f32),
            jax.ShapeDtypeStruct((count // LANES, 2, KEPT, 4, LANES, width), f32),
            matrix,
            matrix,
        ],
        scratch_shapes=[
            pltpu.VMEM((width // 128, 4 * LANES * rows, 128), f32),
            state,
            pltpu.VMEM((rows, 3, LANES, width), f32),
            state,
            state,
            pltpu.VMEM((4, LANES, width), f32),
            pltpu.VMEM((rows, 3, LANES, width), f32),
        ],
        compiler_params=pltpu.CompilerParams(vmem_limit_bytes=40 * MIB),
        cost_estimate=pl.CostEstimate(flops=240 * vectors.size, bytes_accessed=8 * MIB, transcendentals=0),
        name="inner",
    )(coefficients, vectors, spins)


SPINS = ("B2", "B1", "A1", "A2", "A3", "B1 to A3")


def prepare(kept_ref, low_ref, high_ref, s_ref, there_ref, sp_ref, halo_ref, g_refs, ratio):
    _, rows, width = s_ref.shape
    parts = kept_ref.shape[0]
    tiles = width // 128
    end = HALO * 4 * parts * LANES
    matrix = there_ref[...]
    lines = []
    for e, ref in enumerate((low_ref, high_ref)):
        for k in range(3):
            at = end + k * HALO
            lines += [ref[at + i : at + i + 1] for i in ((1, 0) if e else (0, 1))]
            lines += [s_ref[k, y : y + 1] for y in ([rows - 1, rows - 2, rows - 3] if e else [0, 1, 2])]
    lines = jnp.concatenate(lines + lines[:2], axis=0) * -(coupling / hopping)
    for t, got in enumerate(moved_exactly(lines, matrix)):
        at = pl.ds(t * 128, 128)
        for e in range(2):
            for k in range(3):
                five = [got[(e * 3 + k) * 5 + i : (e * 3 + k) * 5 + i + 1] for i in range(5)]
                for i, row in enumerate(five + [five[1] + five[2] + five[3] + five[4]]):
                    sp_ref[e, i, k, :, at] = jnp.broadcast_to(row, (LANES, 128))
    for e, ref in enumerate((low_ref, high_ref)):
        for t, got in enumerate(moved(ref[:end].astype(jnp.bfloat16), matrix)):
            got = got.reshape(HALO, 4, parts, LANES, 128)
            for g in range(parts):
                halo_ref[g, e, :, :, :, t * 128 : (t + 1) * 128] = got[:, :, g]

    for e, ref in enumerate(g_refs):
        sums = [None] * tiles
        for g in range(parts):
            own = lambda i: (kept_ref, (g, e, i - 1))
            b1, b2 = (halo_ref, (g, e, 0)), (halo_ref, (g, e, 1))
            a3 = by_tile(own(3))
            sides = [beside([x[k] for x in a3]) for k in range(4)]
            for t in range(tiles):
                w = on_site(a3[t], load(sp_ref, (e, SPINS.index("B1 to A3")), t), ratio)
                w = plus(w, times(4.0, [x[t] for x in sides]), load(*own(4), t))
                here = density(load(*b1, t), w) + density(load(*b2, t), a3[t])
                sums[t] = here if g == 0 else plus(sums[t], here)
        for t, x in enumerate(sums):
            rows_out = [x[i * 3 + k] for k in range(3) for i in (range(HALO) if e else reversed(range(HALO)))]
            ref[:, t * 128 : (t + 1) * 128] = side_by_side(rows_out + rows_out[:2])


def cross(part, kept_ref, sp_ref, halo_ref, mid_ref, acc_ref, old_ref, rho):
    tiles = halo_ref.shape[-1] // 128

    @pl.loop(0, 2)
    def _(e):
        spin = lambda name: (sp_ref, (e, SPINS.index(name)))
        own = lambda i: (kept_ref, (part, e, i - 1))
        a_in, b_in = (kept_ref, (part, e, REACH)), (kept_ref, (part, e, REACH + 1))
        b1, b2 = (halo_ref, (part, e, 0)), (halo_ref, (part, e, 1))
        names = ("a_b2", "a_b1", "b_b2", "b_b1", "b_a1", "c_b1", "c_a1", "c_a2")
        mid = {name: (mid_ref, (i,)) for i, name in enumerate(names)}

        def make(row, at, others, ratio=None, extra=None):
            for t, x in flat(by_tile(row), spin(at), ratio):
                for ref, place in others:
                    x = plus(x, load(ref, place, t))
                if extra is not None:
                    x = plus(x, times(extra[0], load(*extra[1], t)))
                yield t, x

        def state(name, *rest, **more):
            for t, x in make(*rest, **more):
                save(*mid[name], t, x)

        def fields(i, r, w):
            for t, x in w:
                x = density(load(*r, t), x)
                if old_ref is not None:
                    x = plus(x, load(old_ref, (e, i), t))
                save(acc_ref, (e, i), t, x)

        state("a_b2", b2, "B2", [b1], ratio=rho[3])
        state("a_b1", b1, "B1", [b2, own(1)], ratio=rho[3])
        state("b_b2", mid["a_b2"], "B2", [mid["a_b1"], b2], extra=(rho[2], b2))
        state("b_b1", mid["a_b1"], "B1", [mid["a_b2"], a_in, b1], extra=(rho[2], b1))
        state("b_a1", b1, "A1", [mid["a_b1"]])
        state("c_b1", mid["b_b1"], "B1", [mid["b_b2"], b_in, mid["b_a1"]], extra=(rho[1], b1))
        state("c_a1", mid["b_a1"], "A1", [mid["b_b1"], b1])
        state("c_a2", b1, "A2", [mid["b_a1"]])
        fields(0, own(1), make(mid["c_a1"], "A1", [mid["c_b1"], mid["c_a2"]]))
        fields(1, own(2), make(mid["c_a2"], "A2", [mid["c_a1"], b1]))
        fields(2, own(3), make(b1, "A3", [mid["c_a2"]]))
        fields(3, own(4), ((t, load(*b1, t)) for t in range(tiles)))


def begin_kernel(coef_ref, kept_ref, low_ref, high_ref, s_ref, there_ref, sp_ref, halo_ref, g_low_ref, g_high_ref, acc_ref, mid_ref):
    rho = ratios(coef_ref)
    prepare(kept_ref, low_ref, high_ref, s_ref, there_ref, sp_ref, halo_ref, (g_low_ref, g_high_ref), rho[3])
    cross(0, kept_ref, sp_ref, halo_ref, mid_ref, acc_ref, None, rho)


def begin(coefficients, kept, low, high, spins, there):
    f32 = jnp.float32
    parts, width = kept.shape[0], spins.shape[-1]
    out = [
        (2, len(SPINS), 3, LANES, width),
        (parts, 2, HALO, 4, LANES, width),
        (8, width),
        (8, width),
        (2, REACH, 3, LANES, width),
    ]
    vmem = pl.BlockSpec(memory_space=pltpu.VMEM)
    return pl.pallas_call(
        begin_kernel,
        in_specs=[pl.BlockSpec(memory_space=pltpu.SMEM)] + [vmem] * 5,
        out_specs=[vmem] * len(out),
        out_shape=[jax.ShapeDtypeStruct(x, f32) for x in out],
        scratch_shapes=[pltpu.VMEM((8, 4, LANES, width), f32)],
        compiler_params=pltpu.CompilerParams(vmem_limit_bytes=32 * MIB),
        cost_estimate=pl.CostEstimate(flops=500 * low.size, bytes_accessed=4 * MIB, transcendentals=0),
        name="begin",
    )(coefficients, kept, low, high, spins, there)


def end_kernel(coef_ref, kept_ref, sp_ref, halo_ref, old_ref, f_ref, out_ref, mid_ref, acc_ref):
    _, rows, width = f_ref.shape
    parts = kept_ref.shape[0]
    rho = ratios(coef_ref)
    for part in range(1, parts):
        cross(part, kept_ref, sp_ref, halo_ref, mid_ref, acc_ref, old_ref if part == 1 else acc_ref, rho)
    last_ref = acc_ref if parts > 1 else old_ref
    out_ref[...] = f_ref[...]
    half = lax.broadcasted_iota(jnp.int32, (8, 128), 0) < REACH
    for t in range(width // 128):
        at = pl.ds(t * 128, 128)
        for k in range(3):
            low = [last_ref[0, i, k, :, at] for i in range(REACH)]
            high = [last_ref[1, i, k, :, at] for i in reversed(range(REACH))]
            edge = side_by_side(low + high)
            out_ref[k, :8, at] += jnp.where(half, edge, 0.0)
            out_ref[k, rows - 8 :, at] += jnp.where(half, 0.0, edge)


def end(coefficients, kept, sp, halo, old, f):
    f32 = jnp.float32
    vmem = pl.BlockSpec(memory_space=pltpu.VMEM)
    return pl.pallas_call(
        end_kernel,
        in_specs=[pl.BlockSpec(memory_space=pltpu.SMEM)] + [vmem] * 5,
        out_specs=vmem,
        out_shape=jax.ShapeDtypeStruct(f.shape, f32),
        scratch_shapes=[pltpu.VMEM((8, 4, LANES, f.shape[-1]), f32), pltpu.VMEM(old.shape, f32)],
        compiler_params=pltpu.CompilerParams(vmem_limit_bytes=32 * MIB),
        cost_estimate=pl.CostEstimate(flops=300 * kept.size, bytes_accessed=3 * MIB, transcendentals=0),
        name="end",
    )(coefficients, kept, sp, halo, old, f)


def sine_and_cosine(x):
    quarters = jnp.floor(x * (2.0 / jnp.pi) + 0.5)
    for part in (1.5703125, 4.837512969970703125e-4, 7.54978995489188216e-8):
        x = x - quarters * part
    z = x * x
    sine = ((-1.9515295891e-4 * z + 8.3321608736e-3) * z - 1.6666654611e-1) * z * x + x
    cosine = ((2.443315711809948e-5 * z - 1.388731625493765e-3) * z + 4.166664568298827e-2) * z * z - 0.5 * z + 1.0
    turns = quarters.astype(jnp.int32)
    odd, half = (turns & 1) == 1, (turns & 2) == 2
    sine, cosine = jnp.where(odd, cosine, sine), jnp.where(odd, -sine, cosine)
    return jnp.where(half, -sine, sine), jnp.where(half, -cosine, cosine)


def final_kernel(count_all, coef_ref, s_ref, back_ref, f_ref, other_ref, rotated_ref, fields_ref):
    _, rows, width = s_ref.shape
    total = f_ref[...] + other_ref[...]
    scale = ratios(coef_ref)[4][:1, :1] * (coupling / count_all)
    got = moved_exactly(total.reshape(3 * rows, width), back_ref[...])
    for t, x in enumerate(got):
        at = pl.ds(t * 128, 128)
        field = [x[k * rows : (k + 1) * rows] * scale for k in range(3)]
        spin = [s_ref[k, :, at] for k in range(3)]
        size = jnp.sqrt(field[0] * field[0] + field[1] * field[1] + field[2] * field[2])
        half_angle = (0.5 * time_step) * size
        sine, cosine = sine_and_cosine(half_angle)
        some = half_angle > 0.0
        ratio = jnp.where(some, sine / jnp.where(some, half_angle, 1.0), 1.0)
        along = field[0] * spin[0] + field[1] * spin[1] + field[2] * spin[2]
        keep = 1.0 - 2.0 * sine * sine
        turn = time_step * ratio * cosine
        lift = (0.5 * time_step * time_step) * ratio * ratio * along
        for k in range(3):
            i, j = (k + 1) % 3, (k + 2) % 3
            cross = field[i] * spin[j] - field[j] * spin[i]
            rotated_ref[k, :, at] = keep * spin[k] + turn * cross + lift * field[k]
            fields_ref[k, :, at] = field[k]


def final(coefficients, spins, back, count_all, f, other):
    out = jax.ShapeDtypeStruct(spins.shape, jnp.float32)
    vmem = pl.BlockSpec(memory_space=pltpu.VMEM)
    return pl.pallas_call(
        functools.partial(final_kernel, count_all),
        in_specs=[pl.BlockSpec(memory_space=pltpu.SMEM)] + [vmem] * 4,
        out_specs=[vmem] * 2,
        out_shape=[out, out],
        compiler_params=pltpu.CompilerParams(vmem_limit_bytes=32 * MIB),
        name="final",
    )(coefficients, spins, back, f, other)


def shards(vectors, classical_spins, coefficients):
    across, number = lax.axis_size("vec"), lax.axis_size("lat")
    count_all = vectors.shape[1] * across

    def to_row(x, on):
        return lax.ppermute(x, "lat", [(i, (i + on) % number) for i in range(number)])

    def swap(x, step):
        steps = across.bit_length() - 1
        bit = lambda i: 1 << (step if i % 2 == 0 else steps - 1 - step)
        pairs = [(i * across + j, i * across + (j ^ bit(i))) for i in range(number) for j in range(across)]
        return lax.ppermute(x, ("lat", "vec"), pairs)

    spins = classical_spins
    rows, width = spins.shape[1:]
    ends = jnp.stack([spins[:, :HALO], spins[:, rows - HALO :]]).reshape(2, 3 * HALO, width)
    low, high = edges(vectors, jnp.pad(ends, ((0, 0), (0, 8 - 3 * HALO), (0, 0))))
    from_below, from_above = to_row(high, 1), to_row(low, -1)
    f, kept, there, back = inner(coefficients, vectors, spins)
    sp, halo, g_low, g_high, crossed = begin(coefficients, kept, from_below, from_above, spins, there)
    below, above = to_row(g_high, 1), to_row(g_low, -1)
    fields = end(coefficients, kept, sp, halo, crossed, f)
    lines = lambda x: x[: 3 * HALO].reshape(3, HALO, width)
    fields = fields.at[:, :HALO].add(lines(below)).at[:, rows - HALO :].add(lines(above))
    steps = across.bit_length() - 1
    if across != 1 << steps or steps == 0:
        return final(coefficients, spins, back, count_all, lax.psum(fields, "vec"), jnp.zeros_like(fields))
    for step in range(steps - 1):
        fields = fields + swap(fields, step)
    return final(coefficients, spins, back, count_all, fields, swap(fields, steps - 1))


def solution(mesh):
    placed = (P(None, "vec", "lat", None), P(None, "lat", None), P())
    return jax.shard_map(
        shards,
        mesh=mesh,
        in_specs=placed,
        out_specs=(P(None, "lat", None), P(None, "lat", None)),
        check_vma=False,
    )
```

time: 44.4 us -> 43.1 us (0.971)
  Pallas kernels: 23.6 us -> 19.7 us
  local copies, waits for them, and re-layouts: 0.01 us -> 2.67 us
    pallas_call x5 -> x4, Pallas kernels: 21.7 us -> 18 us  [the longest x1 12 us: inner(): pl.pallas_call(inner_kernel, in_specs=[pl.BlockSpec(memory_space=pltpu.SM...]
    unnamed x6 -> x8, local copies, waits for them, and re-layouts: 0.01 us -> 1.6 us
    slice x0 -> x1, local copies, waits for them, and re-layouts: none -> 1 us  [shards(): spins[:, :HALO]]
  transfers between devices with their start and end apart: 6 -> 6, of which waited for: 2 -> 2; matrix products, arithmetic and copies ran while one was open for 0% -> 0% of each run, Pallas kernels for 34% -> 33%
where the time goes in v3:
time: 43.1 us; the launch traced here: 42.9 us
  Pallas kernels  19.7 us (46%)
  starting transfers between devices  12.2 us (28%)
  waiting for transfers between devices  7.49 us (17%)
  local copies, waits for them, and re-layouts  2.67 us (6%)
  between operations  0.77 us (2%)
    pallas_call x1, Pallas kernels, inner(): pl.pallas_call(inner_kernel, in_specs=[pl.BlockSpec(memory_space=pltpu.SM...  12 us
    ppermute x4, starting transfers between devices, to_row(): lax.ppermute(x, 'lat', [(i, (i + on) % number) for i in range(number)])  8.2 us
    ppermute x2, waiting for transfers between devices, swap(): return lax.ppermute(x, ('lat', 'vec'), pairs)  7.47 us
    ppermute x2, starting transfers between devices, swap(): return lax.ppermute(x, ('lat', 'vec'), pairs)  3.99 us
    pallas_call x1, Pallas kernels, begin(): pl.pallas_call(begin_kernel, in_specs=[pl.BlockSpec(memory_space=pltpu.SM...  3.13 us
    pallas_call x1, Pallas kernels, end(): pl.pallas_call(end_kernel, in_specs=[pl.BlockSpec(memory_space=pltpu.SMEM...  2.27 us
    pallas_call x1, Pallas kernels, final(): pl.pallas_call(functools.partial(final_kernel, count_all), in_specs=[pl.B...  1.7 us
    unnamed x8, local copies, waits for them, and re-layouts  1.6 us
  transfers between devices with their start and end apart: 6, of which 2 were waited for; matrix products, arithmetic and copies ran while one was open for 0% of the time, Pallas kernels for 33%

profile of v3, /device:TPU:0, one launch (start us, length us, event | category | flops | bytes accessed | tf_op | source)
XLA Modules:
  0.0 42.9 jit_solution(15041537900051499135)
XLA Ops:
  0.6 0.0 copy-start.2
  0.6 0.0 copy-start.3
  0.6 1.0 %fusion.2 = (f32[3,2,1024]{2,1,0:T(2,128)S(1)}, f32[3,2,1024]{2,1,0:T(2,128)S(1)}) fusion(f32[3,16,1024]{2,1,0:T(8,128)} %s_ref.5), kind=kLoop, calls=%fused_computation.6 | loop fusion | bytes 98304 | tf_op jit(solution)/shard_map/slice | solution.py:516
  1.7 0.0 copy-start
  1.7 1.6 %copy-done = bf16[4,16,16,1024]{3,2,1,0:T(8,128)(2,1)S(1)} copy-done((bf16[4,16,16,1024]{3,2,1,0:T(8,128)(2,1)S(1)}, bf16[4,16,16,1024]{3,2,1,0:T(8,128)(2,1)}, u32[]{:S(2)}) %copy-start) | copy-done | bytes 2097176
  3.3 0.0 copy-start.1
  3.3 0.6 %edges.1 = (f32[136,1024]{1,0:T(8,128)S(1)}, f32[136,1024]{1,0:T(8,128)S(1)}) custom-call(bf16[4,16,16,1024]{3,2,1,0:T(8,128)(2,1)S(1)} %copy-done, f32[2,8,1024]{2,1,0:T(8,128)S(1)} %select_maximum_fusion.s_ref), custom_call_target="tpu_custom_call" | custom-call | tf_op jit(solution)/shard_map/edges/pallas_call | solution.py:173
  3.9 0.5 %collective-permute-start = (f32[136,1024]{1,0:T(8,128)S(1)}, f32[136,1024]{1,0:T(8,128)S(1)}, u32[]{:S(2)}, u32[]{:S(2)}) collective-permute-start(f32[136,1024]{1,0:T(8,128)S(1)} %get-tuple-element.39), channel_id=1, source_target_pairs={{0,4},{4,8},{8,12},{12,16},{16,20},{20,24},{24,28},{28,0},{1,5},{5... | collective-permute-start | bytes 1671176 | tf_op jit(solution)/shard_map/ppermute | solution.py:506
  4.4 4.1 %collective-permute-start.1 = (f32[136,1024]{1,0:T(8,128)S(1)}, f32[136,1024]{1,0:T(8,128)S(1)}, u32[]{:S(2)}, u32[]{:S(2)}) collective-permute-start(f32[136,1024]{1,0:T(8,128)S(1)} %get-tuple-element.40), channel_id=1, source_target_pairs={{0,28},{4,0},{8,4},{12,8},{16,12},{20,16},{24,20},{28,24},{1,29},{... | collective-permute-start | bytes 1671176 | tf_op jit(solution)/shard_map/ppermute | solution.py:506
  8.5 0.0 copy-done.2
  8.5 0.0 copy-done.3
  8.5 0.0 copy-done.1
  8.5 12.0 %inner.1 = (f32[3,16,1024]{2,1,0:T(8,128)S(1)}, f32[2,2,6,4,8,1024]{5,4,3,2,1,0:T(8,128)S(1)}, bf16[512,512]{1,0:T(8,128)(2,1)S(1)}, bf16[512,512]{1,0:T(8,128)(2,1)S(1)}) custom-call(f32[5]{0:T(128)S(1)} %copy-done.3, bf16[4,16,16,1024]{3,2,1,0:T(8,128)(2,1)S(1)} %copy-done.1, f32[3,16,1024]{2,1,0:T(8,128)S(1)} %copy-done.2), custom_call_target="tpu_custom_call" | custom-call | flops 251658240 | bytes 8388608 | tf_op jit(solution)/shard_map/inner/pallas_call | solution.py:271
  20.6 0.0 collective-permute-done.low_ref
  20.6 0.0 collective-permute-done.1.high_ref
  20.6 3.1 %begin.1 = (f32[2,6,3,8,1024]{4,3,2,1,0:T(8,128)S(1)}, f32[2,2,2,4,8,1024]{5,4,3,2,1,0:T(8,128)S(1)}, f32[8,1024]{1,0:T(8,128)S(1)}, f32[8,1024]{1,0:T(8,128)S(1)}, f32[2,4,3,8,1024]{4,3,2,1,0:T(8,128)S(1)}) custom-call(f32[5]{0:T(128)S(1)} %copy-done.3, f32[2,2,6,4,8,1024]{5,4,3,2,1,0:T(8,128)S(1)} %get-tuple-element.38.kept_ref, ...), custom_call_target="tpu_custom_call" | custom-call | flops 69632000 | bytes 4194304 | tf_op jit(solution)/shard_map/begin/pallas_call | solution.py:404
  23.7 0.9 %collective-permute-start.2 = (f32[8,1024]{1,0:T(8,128)S(1)}, f32[8,1024]{1,0:T(8,128)S(1)}, u32[]{:S(2)}, u32[]{:S(2)}) collective-permute-start(f32[8,1024]{1,0:T(8,128)S(1)} %get-tuple-element.46), channel_id=1, source_target_pairs={{0,4},{4,8},{8,12},{12,16},{16,20},{20,24},{24,28},{28,0},{1,5},{5... | collective-permute-start | bytes 98312 | tf_op jit(solution)/shard_map/ppermute | solution.py:506
  24.6 2.7 %collective-permute-start.3 = (f32[8,1024]{1,0:T(8,128)S(1)}, f32[8,1024]{1,0:T(8,128)S(1)}, u32[]{:S(2)}, u32[]{:S(2)}) collective-permute-start(f32[8,1024]{1,0:T(8,128)S(1)} %get-tuple-element.47), channel_id=1, source_target_pairs={{0,28},{4,0},{8,4},{12,8},{16,12},{20,16},{24,20},{28,24},{1,29},{... | collective-permute-start | bytes 98312 | tf_op jit(solution)/shard_map/ppermute | solution.py:506
  27.3 2.3 %end.1 = f32[3,16,1024]{2,1,0:T(8,128)S(1)} custom-call(f32[5]{0:T(128)S(1)} %copy-done.3, f32[2,2,6,4,8,1024]{5,4,3,2,1,0:T(8,128)S(1)} %get-tuple-element.38.kept_ref, f32[2,6,3,8,1024]{4,3,2,1,0:T(8,128)S(1)} %get-tuple-element.42.sp_ref, f32[2,2,2,4,8,1024]{5,4,3,2,1,0:T(8,128)S(1)} %get-tuple-element.43.halo_ref, ...), custom_call_target="tpu_custom_call" | custom-call | flops 235929600 | bytes 3145728 | tf_op jit(solution)/shard_map/end/pallas_call | solution.py:438
  29.6 0.0 collective-permute-done.2
  29.6 0.0 collective-permute-done.3
  29.7 2.0 %collective-permute-start.4 = (f32[3,16,1024]{2,1,0:T(8,128)S(1)}, f32[3,16,1024]{2,1,0:T(8,128)S(1)}, u32[]{:S(2)}, u32[]{:S(2)}) collective-permute-start(f32[3,16,1024]{2,1,0:T(8,128)S(1)} %fusion), channel_id=1, source_target_pairs={{0,1},{1,0},{2,3},{3,2},{4,6},{5,7},{6,4},{7,5},{8,9},{9,8},{10,11... | collective-permute-start | bytes 589832 | tf_op jit(solution)/shard_map/ppermute | solution.py:512
  31.7 3.8 %collective-permute-done.4 = f32[3,16,1024]{2,1,0:T(8,128)S(1)} collective-permute-done((f32[3,16,1024]{2,1,0:T(8,128)S(1)}, f32[3,16,1024]{2,1,0:T(8,128)S(1)}, u32[]{:S(2)}, u32[]{:S(2)}) %collective-permute-start.4) | collective-permute-done | bytes 196640 | tf_op jit(solution)/shard_map/ppermute | solution.py:512
  35.5 2.0 %collective-permute-start.5 = (f32[3,16,1024]{2,1,0:T(8,128)S(1)}, f32[3,16,1024]{2,1,0:T(8,128)S(1)}, u32[]{:S(2)}, u32[]{:S(2)}) collective-permute-start(f32[3,16,1024]{2,1,0:T(8,128)S(1)} %add.21.f_ref), channel_id=1, source_target_pairs={{0,2},{1,3},{2,0},{3,1},{4,5},{5,4},{6,7},{7,6},{8,10},{9,11},{10,... | collective-permute-start | bytes 589832 | tf_op jit(solution)/shard_map/ppermute | solution.py:512
  37.5 3.7 %collective-permute-done.5.other_ref = f32[3,16,1024]{2,1,0:T(8,128)S(1)} collective-permute-done((f32[3,16,1024]{2,1,0:T(8,128)S(1)}, f32[3,16,1024]{2,1,0:T(8,128)S(1)}, u32[]{:S(2)}, u32[]{:S(2)}) %collective-permute-start.5) | collective-permute-done | bytes 196640 | tf_op jit(solution)/shard_map/ppermute | solution.py:512
  41.2 1.7 %final.1 = (f32[3,16,1024]{2,1,0:T(8,128)}, f32[3,16,1024]{2,1,0:T(8,128)}) custom-call(f32[5]{0:T(128)S(1)} %copy-done.3, f32[3,16,1024]{2,1,0:T(8,128)S(1)} %copy-done.2, bf16[512,512]{1,0:T(8,128)(2,1)S(1)} %get-tuple-element.37.back_ref, f32[3,16,1024]{2,1,0:T(8,128)S(1)} %add.21.f_ref, f32[3,16,1024]{2,1,0:T(8,128)S(1)} %collective-permute-done.5.other_ref), custom_call_target="tpu_custom_call" | custom-call | tf_op jit(solution)/shard_map/final/pallas_call | solution.py:491
  (8 shorter events, 0.2 us)
Async XLA Ops:
  0.6 7.9 %copy-start.2 = (f32[3,16,1024]{2,1,0:T(8,128)S(1)}, f32[3,16,1024]{2,1,0:T(8,128)}, u32[]{:S(2)}) copy-start(f32[3,16,1024]{2,1,0:T(8,128)} %s_ref.5) | copy-start | bytes 589828
  0.6 7.9 %copy-start.3 = (f32[5]{0:T(128)S(1)}, f32[5]{0:T(128)}, u32[]{:S(2)}) copy-start(f32[5]{0:T(128)} %coef_ref.7) | copy-start | bytes 64
  1.7 1.6 %copy-start = (bf16[4,16,16,1024]{3,2,1,0:T(8,128)(2,1)S(1)}, bf16[4,16,16,1024]{3,2,1,0:T(8,128)(2,1)}, u32[]{:S(2)}) copy-start(bf16[4,16,16,1024]{3,2,1,0:T(8,128)(2,1)} %v_ref.3) | copy-start | bytes 6291460
  3.3 5.2 %copy-start.1 = (bf16[4,16,16,1024]{3,2,1,0:T(8,128)(2,1)S(1)}, bf16[4,16,16,1024]{3,2,1,0:T(8,128)(2,1)}, u32[]{:S(2)}) copy-start(bf16[4,16,16,1024]{3,2,1,0:T(8,128)(2,1)} %v_ref.3) | copy-start | bytes 6291460
  3.9 16.7 %collective-permute-start = (f32[136,1024]{1,0:T(8,128)S(1)}, f32[136,1024]{1,0:T(8,128)S(1)}, u32[]{:S(2)}, u32[]{:S(2)}) collective-permute-start(f32[136,1024]{1,0:T(8,128)S(1)} %get-tuple-element.39), channel_id=1, source_target_pairs={{0,4},{4,8},{8,12},{12,16},{16,20},{20,24},{24,28},{28,0},{1,5},{5... | collective-permute-start | bytes 1671176 | tf_op jit(solution)/shard_map/ppermute | solution.py:506
  4.4 16.2 %collective-permute-start.1 = (f32[136,1024]{1,0:T(8,128)S(1)}, f32[136,1024]{1,0:T(8,128)S(1)}, u32[]{:S(2)}, u32[]{:S(2)}) collective-permute-start(f32[136,1024]{1,0:T(8,128)S(1)} %get-tuple-element.40), channel_id=1, source_target_pairs={{0,28},{4,0},{8,4},{12,8},{16,12},{20,16},{24,20},{28,24},{1,29},{... | collective-permute-start | bytes 1671176 | tf_op jit(solution)/shard_map/ppermute | solution.py:506
  23.7 5.9 %collective-permute-start.2 = (f32[8,1024]{1,0:T(8,128)S(1)}, f32[8,1024]{1,0:T(8,128)S(1)}, u32[]{:S(2)}, u32[]{:S(2)}) collective-permute-start(f32[8,1024]{1,0:T(8,128)S(1)} %get-tuple-element.46), channel_id=1, source_target_pairs={{0,4},{4,8},{8,12},{12,16},{16,20},{20,24},{24,28},{28,0},{1,5},{5... | collective-permute-start | bytes 98312 | tf_op jit(solution)/shard_map/ppermute | solution.py:506
  24.6 5.0 %collective-permute-start.3 = (f32[8,1024]{1,0:T(8,128)S(1)}, f32[8,1024]{1,0:T(8,128)S(1)}, u32[]{:S(2)}, u32[]{:S(2)}) collective-permute-start(f32[8,1024]{1,0:T(8,128)S(1)} %get-tuple-element.47), channel_id=1, source_target_pairs={{0,28},{4,0},{8,4},{12,8},{16,12},{20,16},{24,20},{28,24},{1,29},{... | collective-permute-start | bytes 98312 | tf_op jit(solution)/shard_map/ppermute | solution.py:506
  29.7 5.7 %collective-permute-start.4 = (f32[3,16,1024]{2,1,0:T(8,128)S(1)}, f32[3,16,1024]{2,1,0:T(8,128)S(1)}, u32[]{:S(2)}, u32[]{:S(2)}) collective-permute-start(f32[3,16,1024]{2,1,0:T(8,128)S(1)} %fusion), channel_id=1, source_target_pairs={{0,1},{1,0},{2,3},{3,2},{4,6},{5,7},{6,4},{7,5},{8,9},{9,8},{10,11... | collective-permute-start | bytes 589832 | tf_op jit(solution)/shard_map/ppermute | solution.py:512
  35.5 5.7 %collective-permute-start.5 = (f32[3,16,1024]{2,1,0:T(8,128)S(1)}, f32[3,16,1024]{2,1,0:T(8,128)S(1)}, u32[]{:S(2)}, u32[]{:S(2)}) collective-permute-start(f32[3,16,1024]{2,1,0:T(8,128)S(1)} %add.21.f_ref), channel_id=1, source_target_pairs={{0,2},{1,3},{2,0},{3,1},{4,5},{5,4},{6,7},{7,6},{8,10},{9,11},{10,... | collective-permute-start | bytes 589832 | tf_op jit(solution)/shard_map/ppermute | solution.py:512

commit v4 on v3

--- a/solution.py
+++ b/solution.py
@@ -147,8 +147,10 @@
     return tiles[0]
 
 
-def edges_kernel(v_ref, s_ref, low_ref, high_ref, rows_ref):
+def edges_kernel(v_ref, s_hbm, low_ref, high_ref, s_ref, rows_ref, s_sem):
     _, count, rows, width = v_ref.shape
+    spins = pltpu.make_async_copy(s_hbm, s_ref, s_sem)
+    spins.start()
     for comp in range(4):
         for g in range(count // LANES):
             states = v_ref[comp, g * LANES : (g + 1) * LANES].astype(jnp.float32).reshape(LANES * rows, width)
@@ -160,25 +162,30 @@
                     at = pl.ds(t * 128, 128)
                     low_ref[to, at] = rows_ref[comp, g, t, pl.ds(i, LANES, stride=rows), :]
                     high_ref[to, at] = rows_ref[comp, g, t, pl.ds(rows - 1 - i, LANES, stride=rows), :]
+    spins.wait()
     end = HALO * 4 * count
-    low_ref[end:] = s_ref[0]
-    high_ref[end:] = s_ref[1]
-
-
-def edges(vectors, spin_lines):
+    for ref, first in ((low_ref, 0), (high_ref, rows - HALO)):
+        lines = [s_ref[k, first + i : first + i + 1] for k in range(3) for i in range(HALO)]
+        ref[end:] = jnp.concatenate(lines + lines[: 8 - 3 * HALO], axis=0)
+
+
+def edges(vectors, spins):
     _, count, rows, width = vectors.shape
     f32 = jnp.float32
-    out = jax.ShapeDtypeStruct((HALO * 4 * count + 8, width), f32)
+    out = pltpu.VMEM((HALO * 4 * count + 8, width), f32)
     vmem = pl.BlockSpec(memory_space=pltpu.VMEM)
     return pl.pallas_call(
         edges_kernel,
-        in_specs=[vmem] * 2,
-        out_specs=[vmem] * 2,
-        out_shape=[out, out],
-        scratch_shapes=[pltpu.VMEM((4, count // LANES, width // 128, LANES * rows, 128), f32)],
+        in_specs=[vmem, pl.BlockSpec(memory_space=pltpu.HBM)],
+        out_specs=[vmem] * 3,
+        out_shape=[out, out, pltpu.VMEM(spins.shape, f32)],
+        scratch_shapes=[
+            pltpu.VMEM((4, count // LANES, width // 128, LANES * rows, 128), f32),
+            pltpu.SemaphoreType.DMA,
+        ],
         compiler_params=pltpu.CompilerParams(vmem_limit_bytes=16 * MIB),
         name="edges",
-    )(vectors, spin_lines)
+    )(vectors, pltpu.with_memory_space_constraint(spins, pltpu.HBM))
 
 
 KEPT = REACH + 2
@@ -511,10 +518,8 @@
         pairs = [(i * across + j, i * across + (j ^ bit(i))) for i in range(number) for j in range(across)]
         return lax.ppermute(x, ("lat", "vec"), pairs)
 
-    spins = classical_spins
-    rows, width = spins.shape[1:]
-    ends = jnp.stack([spins[:, :HALO], spins[:, rows - HALO :]]).reshape(2, 3 * HALO, width)
-    low, high = edges(vectors, jnp.pad(ends, ((0, 0), (0, 8 - 3 * HALO), (0, 0))))
+    rows, width = classical_spins.shape[1:]
+    low, high, spins = edges(vectors, classical_spins)
     from_below, from_above = to_row(high, 1), to_row(low, -1)
     f, kept, there, back = inner(coefficients, vectors, spins)
     sp, halo, g_low, g_high, crossed = begin(coefficients, kept, from_below, from_above, spins, there)

time: 43.1 us -> 42.5 us (0.986)
  local copies, waits for them, and re-layouts: 2.67 us -> 1.63 us
  Pallas kernels: 19.7 us -> 20.2 us
    slice x1 -> x0, local copies, waits for them, and re-layouts: 1 us -> none  [shards(): spins[:, :HALO]]
    pallas_call x1, Pallas kernels: 0.57 us -> 1.12 us  [edges(): pl.pallas_call(edges_kernel, in_specs=[vmem, pl.BlockSpec(memory_space=pl...]
    unnamed x8 -> x6, local copies, waits for them, and re-layouts: 1.6 us -> 1.59 us
  transfers between devices with their start and end apart: 6 -> 6, of which waited for: 2 -> 2; matrix products, arithmetic and copies ran while one was open for 0% -> 0% of each run, Pallas kernels for 33% -> 34%
where the time goes in v4:
time: 42.5 us; the launch traced here: 42.3 us
  Pallas kernels  20.2 us (48%)
  starting transfers between devices  12.2 us (29%)
  waiting for transfers between devices  7.46 us (18%)
  local copies, waits for them, and re-layouts  1.63 us (4%)
  between operations  0.73 us (2%)
    pallas_call x1, Pallas kernels, inner(): pl.pallas_call(inner_kernel, in_specs=[pl.BlockSpec(memory_space=pltpu.SM...  12 us
    ppermute x4, starting transfers between devices, to_row(): lax.ppermute(x, 'lat', [(i, (i + on) % number) for i in range(number)])  8.2 us
    ppermute x2, waiting for transfers between devices, swap(): return lax.ppermute(x, ('lat', 'vec'), pairs)  7.45 us
    ppermute x2, starting transfers between devices, swap(): return lax.ppermute(x, ('lat', 'vec'), pairs)  4.02 us
    pallas_call x1, Pallas kernels, begin(): pl.pallas_call(begin_kernel, in_specs=[pl.BlockSpec(memory_space=pltpu.SM...  3.13 us
    pallas_call x1, Pallas kernels, end(): pl.pallas_call(end_kernel, in_specs=[pl.BlockSpec(memory_space=pltpu.SMEM...  2.27 us
    pallas_call x1, Pallas kernels, final(): pl.pallas_call(functools.partial(final_kernel, count_all), in_specs=[pl.B...  1.69 us
    unnamed x6, local copies, waits for them, and re-layouts  1.59 us
  transfers between devices with their start and end apart: 6, of which 2 were waited for; matrix products, arithmetic and copies ran while one was open for 0% of the time, Pallas kernels for 34%

profile of v4, /device:TPU:0, one launch (start us, length us, event | category | flops | bytes accessed | tf_op | source)
XLA Modules:
  0.0 42.3 jit_solution(7238801460857180627)
XLA Ops:
  0.6 0.0 copy-start
  0.6 1.6 %copy-done = bf16[4,16,16,1024]{3,2,1,0:T(8,128)(2,1)S(1)} copy-done((bf16[4,16,16,1024]{3,2,1,0:T(8,128)(2,1)S(1)}, bf16[4,16,16,1024]{3,2,1,0:T(8,128)(2,1)}, u32[]{:S(2)}) %copy-start) | copy-done | bytes 2097176
  2.2 0.0 copy-start.1
  2.2 0.0 copy-start.2
  2.2 1.1 %edges.1 = (f32[136,1024]{1,0:T(8,128)S(1)}, f32[136,1024]{1,0:T(8,128)S(1)}, f32[3,16,1024]{2,1,0:T(8,128)S(1)}) custom-call(bf16[4,16,16,1024]{3,2,1,0:T(8,128)(2,1)S(1)} %copy-done, f32[3,16,1024]{2,1,0:T(8,128)} %s_hbm.1), custom_call_target="tpu_custom_call" | custom-call | tf_op jit(solution)/shard_map/edges/pallas_call | solution.py:177
  3.4 0.5 %collective-permute-start = (f32[136,1024]{1,0:T(8,128)S(1)}, f32[136,1024]{1,0:T(8,128)S(1)}, u32[]{:S(2)}, u32[]{:S(2)}) collective-permute-start(f32[136,1024]{1,0:T(8,128)S(1)} %get-tuple-element.41), channel_id=1, source_target_pairs={{0,4},{4,8},{8,12},{12,16},{16,20},{20,24},{24,28},{28,0},{1,5},{5... | collective-permute-start | bytes 1671176 | tf_op jit(solution)/shard_map/ppermute | solution.py:513
  3.9 4.1 %collective-permute-start.1 = (f32[136,1024]{1,0:T(8,128)S(1)}, f32[136,1024]{1,0:T(8,128)S(1)}, u32[]{:S(2)}, u32[]{:S(2)}) collective-permute-start(f32[136,1024]{1,0:T(8,128)S(1)} %get-tuple-element.42), channel_id=1, source_target_pairs={{0,28},{4,0},{8,4},{12,8},{16,12},{20,16},{24,20},{28,24},{1,29},{... | collective-permute-start | bytes 1671176 | tf_op jit(solution)/shard_map/ppermute | solution.py:513
  8.0 0.0 copy-done.1
  8.0 0.0 copy-done.2
  8.0 12.0 %inner.1 = (f32[3,16,1024]{2,1,0:T(8,128)S(1)}, f32[2,2,6,4,8,1024]{5,4,3,2,1,0:T(8,128)S(1)}, bf16[512,512]{1,0:T(8,128)(2,1)S(1)}, bf16[512,512]{1,0:T(8,128)(2,1)S(1)}) custom-call(f32[5]{0:T(128)S(1)} %copy-done.2, bf16[4,16,16,1024]{3,2,1,0:T(8,128)(2,1)S(1)} %copy-done.1, f32[3,16,1024]{2,1,0:T(8,128)S(1)} %get-tuple-element.38.s_ref), custom_call_target="tpu_custom_call" | custom-call | flops 251658240 | bytes 8388608 | tf_op jit(solution)/shard_map/inner/pallas_call | solution.py:278
  20.0 0.0 collective-permute-done.low_ref
  20.0 0.0 collective-permute-done.1.high_ref
  20.0 3.1 %begin.1 = (f32[2,6,3,8,1024]{4,3,2,1,0:T(8,128)S(1)}, f32[2,2,2,4,8,1024]{5,4,3,2,1,0:T(8,128)S(1)}, f32[8,1024]{1,0:T(8,128)S(1)}, f32[8,1024]{1,0:T(8,128)S(1)}, f32[2,4,3,8,1024]{4,3,2,1,0:T(8,128)S(1)}) custom-call(f32[5]{0:T(128)S(1)} %copy-done.2, f32[2,2,6,4,8,1024]{5,4,3,2,1,0:T(8,128)S(1)} %get-tuple-element.40.kept_ref, ...), custom_call_target="tpu_custom_call" | custom-call | flops 69632000 | bytes 4194304 | tf_op jit(solution)/shard_map/begin/pallas_call | solution.py:411
  23.1 0.9 %collective-permute-start.2 = (f32[8,1024]{1,0:T(8,128)S(1)}, f32[8,1024]{1,0:T(8,128)S(1)}, u32[]{:S(2)}, u32[]{:S(2)}) collective-permute-start(f32[8,1024]{1,0:T(8,128)S(1)} %get-tuple-element.48), channel_id=1, source_target_pairs={{0,4},{4,8},{8,12},{12,16},{16,20},{20,24},{24,28},{28,0},{1,5},{5... | collective-permute-start | bytes 98312 | tf_op jit(solution)/shard_map/ppermute | solution.py:513
  24.1 2.7 %collective-permute-start.3 = (f32[8,1024]{1,0:T(8,128)S(1)}, f32[8,1024]{1,0:T(8,128)S(1)}, u32[]{:S(2)}, u32[]{:S(2)}) collective-permute-start(f32[8,1024]{1,0:T(8,128)S(1)} %get-tuple-element.49), channel_id=1, source_target_pairs={{0,28},{4,0},{8,4},{12,8},{16,12},{20,16},{24,20},{28,24},{1,29},{... | collective-permute-start | bytes 98312 | tf_op jit(solution)/shard_map/ppermute | solution.py:513
  26.7 2.3 %end.1 = f32[3,16,1024]{2,1,0:T(8,128)S(1)} custom-call(f32[5]{0:T(128)S(1)} %copy-done.2, f32[2,2,6,4,8,1024]{5,4,3,2,1,0:T(8,128)S(1)} %get-tuple-element.40.kept_ref, f32[2,6,3,8,1024]{4,3,2,1,0:T(8,128)S(1)} %get-tuple-element.44.sp_ref, f32[2,2,2,4,8,1024]{5,4,3,2,1,0:T(8,128)S(1)} %get-tuple-element.45.halo_ref, ...), custom_call_target="tpu_custom_call" | custom-call | flops 235929600 | bytes 3145728 | tf_op jit(solution)/shard_map/end/pallas_call | solution.py:445
  29.0 0.0 collective-permute-done.2
  29.0 0.0 collective-permute-done.3
  29.1 2.0 %collective-permute-start.4 = (f32[3,16,1024]{2,1,0:T(8,128)S(1)}, f32[3,16,1024]{2,1,0:T(8,128)S(1)}, u32[]{:S(2)}, u32[]{:S(2)}) collective-permute-start(f32[3,16,1024]{2,1,0:T(8,128)S(1)} %fusion), channel_id=1, source_target_pairs={{0,1},{1,0},{2,3},{3,2},{4,6},{5,7},{6,4},{7,5},{8,9},{9,8},{10,11... | collective-permute-start | bytes 589832 | tf_op jit(solution)/shard_map/ppermute | solution.py:519
  31.1 3.7 %collective-permute-done.4 = f32[3,16,1024]{2,1,0:T(8,128)S(1)} collective-permute-done((f32[3,16,1024]{2,1,0:T(8,128)S(1)}, f32[3,16,1024]{2,1,0:T(8,128)S(1)}, u32[]{:S(2)}, u32[]{:S(2)}) %collective-permute-start.4) | collective-permute-done | bytes 196640 | tf_op jit(solution)/shard_map/ppermute | solution.py:519
  34.9 2.0 %collective-permute-start.5 = (f32[3,16,1024]{2,1,0:T(8,128)S(1)}, f32[3,16,1024]{2,1,0:T(8,128)S(1)}, u32[]{:S(2)}, u32[]{:S(2)}) collective-permute-start(f32[3,16,1024]{2,1,0:T(8,128)S(1)} %add.19.f_ref), channel_id=1, source_target_pairs={{0,2},{1,3},{2,0},{3,1},{4,5},{5,4},{6,7},{7,6},{8,10},{9,11},{10,... | collective-permute-start | bytes 589832 | tf_op jit(solution)/shard_map/ppermute | solution.py:519
  36.9 3.7 %collective-permute-done.5.other_ref = f32[3,16,1024]{2,1,0:T(8,128)S(1)} collective-permute-done((f32[3,16,1024]{2,1,0:T(8,128)S(1)}, f32[3,16,1024]{2,1,0:T(8,128)S(1)}, u32[]{:S(2)}, u32[]{:S(2)}) %collective-permute-start.5) | collective-permute-done | bytes 196640 | tf_op jit(solution)/shard_map/ppermute | solution.py:519
  40.6 1.7 %final.1 = (f32[3,16,1024]{2,1,0:T(8,128)}, f32[3,16,1024]{2,1,0:T(8,128)}) custom-call(f32[5]{0:T(128)S(1)} %copy-done.2, f32[3,16,1024]{2,1,0:T(8,128)S(1)} %get-tuple-element.38.s_ref, bf16[512,512]{1,0:T(8,128)(2,1)S(1)} %get-tuple-element.39.back_ref, f32[3,16,1024]{2,1,0:T(8,128)S(1)} %add.19.f_ref, f32[3,16,1024]{2,1,0:T(8,128)S(1)} %collective-permute-done.5.other_ref), custom_call_target="tpu_custom_call" | custom-call | tf_op jit(solution)/shard_map/final/pallas_call | solution.py:498
  (5 shorter events, 0.1 us)
Async XLA Ops:
  0.6 1.6 %copy-start = (bf16[4,16,16,1024]{3,2,1,0:T(8,128)(2,1)S(1)}, bf16[4,16,16,1024]{3,2,1,0:T(8,128)(2,1)}, u32[]{:S(2)}) copy-start(bf16[4,16,16,1024]{3,2,1,0:T(8,128)(2,1)} %v_ref.3) | copy-start | bytes 6291460
  2.2 5.7 %copy-start.1 = (bf16[4,16,16,1024]{3,2,1,0:T(8,128)(2,1)S(1)}, bf16[4,16,16,1024]{3,2,1,0:T(8,128)(2,1)}, u32[]{:S(2)}) copy-start(bf16[4,16,16,1024]{3,2,1,0:T(8,128)(2,1)} %v_ref.3) | copy-start | bytes 6291460
  2.2 5.7 %copy-start.2 = (f32[5]{0:T(128)S(1)}, f32[5]{0:T(128)}, u32[]{:S(2)}) copy-start(f32[5]{0:T(128)} %coef_ref.7) | copy-start | bytes 64
  3.4 16.6 %collective-permute-start = (f32[136,1024]{1,0:T(8,128)S(1)}, f32[136,1024]{1,0:T(8,128)S(1)}, u32[]{:S(2)}, u32[]{:S(2)}) collective-permute-start(f32[136,1024]{1,0:T(8,128)S(1)} %get-tuple-element.41), channel_id=1, source_target_pairs={{0,4},{4,8},{8,12},{12,16},{16,20},{20,24},{24,28},{28,0},{1,5},{5... | collective-permute-start | bytes 1671176 | tf_op jit(solution)/shard_map/ppermute | solution.py:513
  3.9 16.1 %collective-permute-start.1 = (f32[136,1024]{1,0:T(8,128)S(1)}, f32[136,1024]{1,0:T(8,128)S(1)}, u32[]{:S(2)}, u32[]{:S(2)}) collective-permute-start(f32[136,1024]{1,0:T(8,128)S(1)} %get-tuple-element.42), channel_id=1, source_target_pairs={{0,28},{4,0},{8,4},{12,8},{16,12},{20,16},{24,20},{28,24},{1,29},{... | collective-permute-start | bytes 1671176 | tf_op jit(solution)/shard_map/ppermute | solution.py:513
  23.1 5.9 %collective-permute-start.2 = (f32[8,1024]{1,0:T(8,128)S(1)}, f32[8,1024]{1,0:T(8,128)S(1)}, u32[]{:S(2)}, u32[]{:S(2)}) collective-permute-start(f32[8,1024]{1,0:T(8,128)S(1)} %get-tuple-element.48), channel_id=1, source_target_pairs={{0,4},{4,8},{8,12},{12,16},{16,20},{20,24},{24,28},{28,0},{1,5},{5... | collective-permute-start | bytes 98312 | tf_op jit(solution)/shard_map/ppermute | solution.py:513
  24.1 5.0 %collective-permute-start.3 = (f32[8,1024]{1,0:T(8,128)S(1)}, f32[8,1024]{1,0:T(8,128)S(1)}, u32[]{:S(2)}, u32[]{:S(2)}) collective-permute-start(f32[8,1024]{1,0:T(8,128)S(1)} %get-tuple-element.49), channel_id=1, source_target_pairs={{0,28},{4,0},{8,4},{12,8},{16,12},{20,16},{24,20},{28,24},{1,29},{... | collective-permute-start | bytes 98312 | tf_op jit(solution)/shard_map/ppermute | solution.py:513
  29.1 5.7 %collective-permute-start.4 = (f32[3,16,1024]{2,1,0:T(8,128)S(1)}, f32[3,16,1024]{2,1,0:T(8,128)S(1)}, u32[]{:S(2)}, u32[]{:S(2)}) collective-permute-start(f32[3,16,1024]{2,1,0:T(8,128)S(1)} %fusion), channel_id=1, source_target_pairs={{0,1},{1,0},{2,3},{3,2},{4,6},{5,7},{6,4},{7,5},{8,9},{9,8},{10,11... | collective-permute-start | bytes 589832 | tf_op jit(solution)/shard_map/ppermute | solution.py:519
  34.9 5.7 %collective-permute-start.5 = (f32[3,16,1024]{2,1,0:T(8,128)S(1)}, f32[3,16,1024]{2,1,0:T(8,128)S(1)}, u32[]{:S(2)}, u32[]{:S(2)}) collective-permute-start(f32[3,16,1024]{2,1,0:T(8,128)S(1)} %add.19.f_ref), channel_id=1, source_target_pairs={{0,2},{1,3},{2,0},{3,1},{4,5},{5,4},{6,7},{7,6},{8,10},{9,11},{10,... | collective-permute-start | bytes 589832 | tf_op jit(solution)/shard_map/ppermute | solution.py:519

commit v5 on v4

--- a/solution.py
+++ b/solution.py
@@ -147,11 +147,15 @@
     return tiles[0]
 
 
-def edges_kernel(v_ref, s_hbm, low_ref, high_ref, s_ref, rows_ref, s_sem):
-    _, count, rows, width = v_ref.shape
+def edges_kernel(v_hbm, s_hbm, low_ref, high_ref, v_ref, s_ref, rows_ref, v_sem, s_sem):
+    _, count, rows, width = v_hbm.shape
+    copies = [pltpu.make_async_copy(v_hbm.at[comp], v_ref.at[comp], v_sem.at[comp]) for comp in range(4)]
+    for copy in copies:
+        copy.start()
     spins = pltpu.make_async_copy(s_hbm, s_ref, s_sem)
     spins.start()
     for comp in range(4):
+        copies[comp].wait()
         for g in range(count // LANES):
             states = v_ref[comp, g * LANES : (g + 1) * LANES].astype(jnp.float32).reshape(LANES * rows, width)
             for t in range(width // 128):
@@ -173,19 +177,20 @@
     _, count, rows, width = vectors.shape
     f32 = jnp.float32
     out = pltpu.VMEM((HALO * 4 * count + 8, width), f32)
-    vmem = pl.BlockSpec(memory_space=pltpu.VMEM)
+    hbm, vmem = pl.BlockSpec(memory_space=pltpu.HBM), pl.BlockSpec(memory_space=pltpu.VMEM)
     return pl.pallas_call(
         edges_kernel,
-        in_specs=[vmem, pl.BlockSpec(memory_space=pltpu.HBM)],
-        out_specs=[vmem] * 3,
-        out_shape=[out, out, pltpu.VMEM(spins.shape, f32)],
+        in_specs=[hbm] * 2,
+        out_specs=[vmem] * 4,
+        out_shape=[out, out, pltpu.VMEM(vectors.shape, vectors.dtype), pltpu.VMEM(spins.shape, f32)],
         scratch_shapes=[
             pltpu.VMEM((4, count // LANES, width // 128, LANES * rows, 128), f32),
+            pltpu.SemaphoreType.DMA((4,)),
             pltpu.SemaphoreType.DMA,
         ],
         compiler_params=pltpu.CompilerParams(vmem_limit_bytes=16 * MIB),
         name="edges",
-    )(vectors, pltpu.with_memory_space_constraint(spins, pltpu.HBM))
+    )(*[pltpu.with_memory_space_constraint(x, pltpu.HBM) for x in (vectors, spins)])
 
 
 KEPT = REACH + 2
@@ -519,7 +524,7 @@
         return lax.ppermute(x, ("lat", "vec"), pairs)
 
     rows, width = classical_spins.shape[1:]
-    low, high, spins = edges(vectors, classical_spins)
+    low, high, vectors, spins = edges(vectors, classical_spins)
     from_below, from_above = to_row(high, 1), to_row(low, -1)
     f, kept, there, back = inner(coefficients, vectors, spins)
     sp, halo, g_low, g_high, crossed = begin(coefficients, kept, from_below, from_above, spins, there)

time: 42.5 us -> 41.5 us (0.976)
  local copies, waits for them, and re-layouts: 1.63 us -> 0.04 us
  Pallas kernels: 20.2 us -> 20.8 us
    unnamed x6 -> x2, local copies, waits for them, and re-layouts: 1.59 us -> 0.01 us
    pallas_call x1, Pallas kernels: 1.12 us -> 1.75 us  [edges(): pl.pallas_call(edges_kernel, in_specs=[hbm] * 2, out_specs=[vmem] * 4, ou...]
where the time goes in v5:
time: 41.5 us; the launch traced here: 41.4 us
  Pallas kernels  20.8 us (50%)
  starting transfers between devices  12.2 us (29%)
  waiting for transfers between devices  7.45 us (18%)
  between operations  0.72 us (2%)
    pallas_call x1, Pallas kernels, inner(): pl.pallas_call(inner_kernel, in_specs=[pl.BlockSpec(memory_space=pltpu.SM...  12 us
    ppermute x4, starting transfers between devices, to_row(): lax.ppermute(x, 'lat', [(i, (i + on) % number) for i in range(number)])  8.2 us
    ppermute x2, waiting for transfers between devices, swap(): return lax.ppermute(x, ('lat', 'vec'), pairs)  7.44 us
    ppermute x2, starting transfers between devices, swap(): return lax.ppermute(x, ('lat', 'vec'), pairs)  4.03 us
    pallas_call x1, Pallas kernels, begin(): pl.pallas_call(begin_kernel, in_specs=[pl.BlockSpec(memory_space=pltpu.SM...  3.13 us
    pallas_call x1, Pallas kernels, end(): pl.pallas_call(end_kernel, in_specs=[pl.BlockSpec(memory_space=pltpu.SMEM...  2.27 us
    pallas_call x1, Pallas kernels, edges(): pl.pallas_call(edges_kernel, in_specs=[hbm] * 2, out_specs=[vmem] * 4, ou...  1.75 us
    pallas_call x1, Pallas kernels, final(): pl.pallas_call(functools.partial(final_kernel, count_all), in_specs=[pl.B...  1.69 us
  transfers between devices with their start and end apart: 6, of which 2 were waited for; matrix products, arithmetic and copies ran while one was open for 0% of the time, Pallas kernels for 34%

profile of v5, /device:TPU:0, one launch (start us, length us, event | category | flops | bytes accessed | tf_op | source)
XLA Modules:
  0.0 41.4 jit_solution(13812522234664738494)
XLA Ops:
  0.6 0.0 copy-start
  0.6 1.8 %edges.1 = (f32[136,1024]{1,0:T(8,128)S(1)}, f32[136,1024]{1,0:T(8,128)S(1)}, bf16[4,16,16,1024]{3,2,1,0:T(8,128)(2,1)S(1)}, f32[3,16,1024]{2,1,0:T(8,128)S(1)}) custom-call(bf16[4,16,16,1024]{3,2,1,0:T(8,128)(2,1)} %v_hbm.1, f32[3,16,1024]{2,1,0:T(8,128)} %s_hbm.1), custom_call_target="tpu_custom_call" | custom-call | tf_op jit(solution)/shard_map/edges/pallas_call | solution.py:181
  2.4 0.5 %collective-permute-start = (f32[136,1024]{1,0:T(8,128)S(1)}, f32[136,1024]{1,0:T(8,128)S(1)}, u32[]{:S(2)}, u32[]{:S(2)}) collective-permute-start(f32[136,1024]{1,0:T(8,128)S(1)} %get-tuple-element.43), channel_id=1, source_target_pairs={{0,4},{4,8},{8,12},{12,16},{16,20},{20,24},{24,28},{28,0},{1,5},{5... | collective-permute-start | bytes 1671176 | tf_op jit(solution)/shard_map/ppermute | solution.py:518
  2.9 4.1 %collective-permute-start.1 = (f32[136,1024]{1,0:T(8,128)S(1)}, f32[136,1024]{1,0:T(8,128)S(1)}, u32[]{:S(2)}, u32[]{:S(2)}) collective-permute-start(f32[136,1024]{1,0:T(8,128)S(1)} %get-tuple-element.44), channel_id=1, source_target_pairs={{0,28},{4,0},{8,4},{12,8},{16,12},{20,16},{24,20},{28,24},{1,29},{... | collective-permute-start | bytes 1671176 | tf_op jit(solution)/shard_map/ppermute | solution.py:518
  7.0 0.0 copy-done
  7.0 12.0 %inner.1 = (f32[3,16,1024]{2,1,0:T(8,128)S(1)}, f32[2,2,6,4,8,1024]{5,4,3,2,1,0:T(8,128)S(1)}, bf16[512,512]{1,0:T(8,128)(2,1)S(1)}, bf16[512,512]{1,0:T(8,128)(2,1)S(1)}) custom-call(f32[5]{0:T(128)S(1)} %copy-done, bf16[4,16,16,1024]{3,2,1,0:T(8,128)(2,1)S(1)} %get-tuple-element.40.v_ref, f32[3,16,1024]{2,1,0:T(8,128)S(1)} %get-tuple-element.39.s_ref), custom_call_target="tpu_custom_call" | custom-call | flops 251658240 | bytes 8388608 | tf_op jit(solution)/shard_map/inner/pallas_call | solution.py:283
  19.0 0.0 collective-permute-done.low_ref
  19.0 0.0 collective-permute-done.1.high_ref
  19.0 3.1 %begin.1 = (f32[2,6,3,8,1024]{4,3,2,1,0:T(8,128)S(1)}, f32[2,2,2,4,8,1024]{5,4,3,2,1,0:T(8,128)S(1)}, f32[8,1024]{1,0:T(8,128)S(1)}, f32[8,1024]{1,0:T(8,128)S(1)}, f32[2,4,3,8,1024]{4,3,2,1,0:T(8,128)S(1)}) custom-call(f32[5]{0:T(128)S(1)} %copy-done, f32[2,2,6,4,8,1024]{5,4,3,2,1,0:T(8,128)S(1)} %get-tuple-element.42.kept_ref, ...), custom_call_target="tpu_custom_call" | custom-call | flops 69632000 | bytes 4194304 | tf_op jit(solution)/shard_map/begin/pallas_call | solution.py:416
  22.2 1.0 %collective-permute-start.2 = (f32[8,1024]{1,0:T(8,128)S(1)}, f32[8,1024]{1,0:T(8,128)S(1)}, u32[]{:S(2)}, u32[]{:S(2)}) collective-permute-start(f32[8,1024]{1,0:T(8,128)S(1)} %get-tuple-element.50), channel_id=1, source_target_pairs={{0,4},{4,8},{8,12},{12,16},{16,20},{20,24},{24,28},{28,0},{1,5},{5... | collective-permute-start | bytes 98312 | tf_op jit(solution)/shard_map/ppermute | solution.py:518
  23.1 2.6 %collective-permute-start.3 = (f32[8,1024]{1,0:T(8,128)S(1)}, f32[8,1024]{1,0:T(8,128)S(1)}, u32[]{:S(2)}, u32[]{:S(2)}) collective-permute-start(f32[8,1024]{1,0:T(8,128)S(1)} %get-tuple-element.51), channel_id=1, source_target_pairs={{0,28},{4,0},{8,4},{12,8},{16,12},{20,16},{24,20},{28,24},{1,29},{... | collective-permute-start | bytes 98312 | tf_op jit(solution)/shard_map/ppermute | solution.py:518
  25.8 2.3 %end.1 = f32[3,16,1024]{2,1,0:T(8,128)S(1)} custom-call(f32[5]{0:T(128)S(1)} %copy-done, f32[2,2,6,4,8,1024]{5,4,3,2,1,0:T(8,128)S(1)} %get-tuple-element.42.kept_ref, f32[2,6,3,8,1024]{4,3,2,1,0:T(8,128)S(1)} %get-tuple-element.46.sp_ref, f32[2,2,2,4,8,1024]{5,4,3,2,1,0:T(8,128)S(1)} %get-tuple-element.47.halo_ref, ...), custom_call_target="tpu_custom_call" | custom-call | flops 235929600 | bytes 3145728 | tf_op jit(solution)/shard_map/end/pallas_call | solution.py:450
  28.1 0.0 collective-permute-done.2
  28.1 0.0 collective-permute-done.3
  28.2 2.0 %collective-permute-start.4 = (f32[3,16,1024]{2,1,0:T(8,128)S(1)}, f32[3,16,1024]{2,1,0:T(8,128)S(1)}, u32[]{:S(2)}, u32[]{:S(2)}) collective-permute-start(f32[3,16,1024]{2,1,0:T(8,128)S(1)} %fusion), channel_id=1, source_target_pairs={{0,1},{1,0},{2,3},{3,2},{4,6},{5,7},{6,4},{7,5},{8,9},{9,8},{10,11... | collective-permute-start | bytes 589832 | tf_op jit(solution)/shard_map/ppermute | solution.py:524
  30.2 3.7 %collective-permute-done.4 = f32[3,16,1024]{2,1,0:T(8,128)S(1)} collective-permute-done((f32[3,16,1024]{2,1,0:T(8,128)S(1)}, f32[3,16,1024]{2,1,0:T(8,128)S(1)}, u32[]{:S(2)}, u32[]{:S(2)}) %collective-permute-start.4) | collective-permute-done | bytes 196640 | tf_op jit(solution)/shard_map/ppermute | solution.py:524
  34.0 2.0 %collective-permute-start.5 = (f32[3,16,1024]{2,1,0:T(8,128)S(1)}, f32[3,16,1024]{2,1,0:T(8,128)S(1)}, u32[]{:S(2)}, u32[]{:S(2)}) collective-permute-start(f32[3,16,1024]{2,1,0:T(8,128)S(1)} %add.19.f_ref), channel_id=1, source_target_pairs={{0,2},{1,3},{2,0},{3,1},{4,5},{5,4},{6,7},{7,6},{8,10},{9,11},{10,... | collective-permute-start | bytes 589832 | tf_op jit(solution)/shard_map/ppermute | solution.py:524
  36.0 3.7 %collective-permute-done.5.other_ref = f32[3,16,1024]{2,1,0:T(8,128)S(1)} collective-permute-done((f32[3,16,1024]{2,1,0:T(8,128)S(1)}, f32[3,16,1024]{2,1,0:T(8,128)S(1)}, u32[]{:S(2)}, u32[]{:S(2)}) %collective-permute-start.5) | collective-permute-done | bytes 196640 | tf_op jit(solution)/shard_map/ppermute | solution.py:524
  39.7 1.7 %final.1 = (f32[3,16,1024]{2,1,0:T(8,128)}, f32[3,16,1024]{2,1,0:T(8,128)}) custom-call(f32[5]{0:T(128)S(1)} %copy-done, f32[3,16,1024]{2,1,0:T(8,128)S(1)} %get-tuple-element.39.s_ref, bf16[512,512]{1,0:T(8,128)(2,1)S(1)} %get-tuple-element.41.back_ref, f32[3,16,1024]{2,1,0:T(8,128)S(1)} %add.19.f_ref, f32[3,16,1024]{2,1,0:T(8,128)S(1)} %collective-permute-done.5.other_ref), custom_call_target="tpu_custom_call" | custom-call | tf_op jit(solution)/shard_map/final/pallas_call | solution.py:503
  (5 shorter events, 0.1 us)
Async XLA Ops:
  0.6 6.4 %copy-start = (f32[5]{0:T(128)S(1)}, f32[5]{0:T(128)}, u32[]{:S(2)}) copy-start(f32[5]{0:T(128)} %coef_ref.7) | copy-start | bytes 64
  2.4 16.6 %collective-permute-start = (f32[136,1024]{1,0:T(8,128)S(1)}, f32[136,1024]{1,0:T(8,128)S(1)}, u32[]{:S(2)}, u32[]{:S(2)}) collective-permute-start(f32[136,1024]{1,0:T(8,128)S(1)} %get-tuple-element.43), channel_id=1, source_target_pairs={{0,4},{4,8},{8,12},{12,16},{16,20},{20,24},{24,28},{28,0},{1,5},{5... | collective-permute-start | bytes 1671176 | tf_op jit(solution)/shard_map/ppermute | solution.py:518
  2.9 16.1 %collective-permute-start.1 = (f32[136,1024]{1,0:T(8,128)S(1)}, f32[136,1024]{1,0:T(8,128)S(1)}, u32[]{:S(2)}, u32[]{:S(2)}) collective-permute-start(f32[136,1024]{1,0:T(8,128)S(1)} %get-tuple-element.44), channel_id=1, source_target_pairs={{0,28},{4,0},{8,4},{12,8},{16,12},{20,16},{24,20},{28,24},{1,29},{... | collective-permute-start | bytes 1671176 | tf_op jit(solution)/shard_map/ppermute | solution.py:518
  22.2 5.9 %collective-permute-start.2 = (f32[8,1024]{1,0:T(8,128)S(1)}, f32[8,1024]{1,0:T(8,128)S(1)}, u32[]{:S(2)}, u32[]{:S(2)}) collective-permute-start(f32[8,1024]{1,0:T(8,128)S(1)} %get-tuple-element.50), channel_id=1, source_target_pairs={{0,4},{4,8},{8,12},{12,16},{16,20},{20,24},{24,28},{28,0},{1,5},{5... | collective-permute-start | bytes 98312 | tf_op jit(solution)/shard_map/ppermute | solution.py:518
  23.1 5.0 %collective-permute-start.3 = (f32[8,1024]{1,0:T(8,128)S(1)}, f32[8,1024]{1,0:T(8,128)S(1)}, u32[]{:S(2)}, u32[]{:S(2)}) collective-permute-start(f32[8,1024]{1,0:T(8,128)S(1)} %get-tuple-element.51), channel_id=1, source_target_pairs={{0,28},{4,0},{8,4},{12,8},{16,12},{20,16},{24,20},{28,24},{1,29},{... | collective-permute-start | bytes 98312 | tf_op jit(solution)/shard_map/ppermute | solution.py:518
  28.2 5.7 %collective-permute-start.4 = (f32[3,16,1024]{2,1,0:T(8,128)S(1)}, f32[3,16,1024]{2,1,0:T(8,128)S(1)}, u32[]{:S(2)}, u32[]{:S(2)}) collective-permute-start(f32[3,16,1024]{2,1,0:T(8,128)S(1)} %fusion), channel_id=1, source_target_pairs={{0,1},{1,0},{2,3},{3,2},{4,6},{5,7},{6,4},{7,5},{8,9},{9,8},{10,11... | collective-permute-start | bytes 589832 | tf_op jit(solution)/shard_map/ppermute | solution.py:524
  34.0 5.7 %collective-permute-start.5 = (f32[3,16,1024]{2,1,0:T(8,128)S(1)}, f32[3,16,1024]{2,1,0:T(8,128)S(1)}, u32[]{:S(2)}, u32[]{:S(2)}) collective-permute-start(f32[3,16,1024]{2,1,0:T(8,128)S(1)} %add.19.f_ref), channel_id=1, source_target_pairs={{0,2},{1,3},{2,0},{3,1},{4,5},{5,4},{6,7},{7,6},{8,10},{9,11},{10,... | collective-permute-start | bytes 589832 | tf_op jit(solution)/shard_map/ppermute | solution.py:524

commit v6 on v5

--- a/solution.py
+++ b/solution.py
@@ -16,6 +16,11 @@
 REACH = 4
 HALO = 2
 MIB = 1 << 20
+
+
+def inwards(odd, side, i, rows):
+    high = odd if side == 0 else 1 - odd
+    return i + high * (rows - 1 - 2 * i)
 
 
 def ratios(coefs):
@@ -128,8 +133,12 @@
     return [load(ref, at, t) for t in range(ref.shape[-1] // 128)]
 
 
-def flat(row, spin, ratio=None):
-    sides = [beside([x[k] for x in row]) for k in range(4)]
+def lateral(row):
+    return [beside([x[k] for x in row]) for k in range(4)]
+
+
+def flat(row, spin, ratio=None, sides=None):
+    sides = sides or lateral(row)
     for t, here in enumerate(row):
         yield t, plus([x[t] for x in sides], on_site(here, load(*spin, t), ratio))
 
@@ -147,8 +156,9 @@
     return tiles[0]
 
 
-def edges_kernel(v_hbm, s_hbm, low_ref, high_ref, v_ref, s_ref, rows_ref, v_sem, s_sem):
+def edges_kernel(odd_ref, v_hbm, s_hbm, far_ref, near_ref, v_ref, s_ref, rows_ref, v_sem, s_sem):
     _, count, rows, width = v_hbm.shape
+    odd = odd_ref[0]
     copies = [pltpu.make_async_copy(v_hbm.at[comp], v_ref.at[comp], v_sem.at[comp]) for comp in range(4)]
     for copy in copies:
         copy.start()
@@ -164,23 +174,23 @@
                 to = pl.ds((i * 4 + comp) * count + g * LANES, LANES)
                 for t in range(width // 128):
                     at = pl.ds(t * 128, 128)
-                    low_ref[to, at] = rows_ref[comp, g, t, pl.ds(i, LANES, stride=rows), :]
-                    high_ref[to, at] = rows_ref[comp, g, t, pl.ds(rows - 1 - i, LANES, stride=rows), :]
+                    for side, ref in enumerate((far_ref, near_ref)):
+                        ref[to, at] = rows_ref[comp, g, t, pl.ds(inwards(odd, side, i, rows), LANES, stride=rows), :]
     spins.wait()
     end = HALO * 4 * count
-    for ref, first in ((low_ref, 0), (high_ref, rows - HALO)):
-        lines = [s_ref[k, first + i : first + i + 1] for k in range(3) for i in range(HALO)]
+    for side, ref in enumerate((far_ref, near_ref)):
+        lines = [s_ref[k, pl.ds(inwards(odd, side, i, rows), 1)] for k in range(3) for i in range(HALO)]
         ref[end:] = jnp.concatenate(lines + lines[: 8 - 3 * HALO], axis=0)
 
 
-def edges(vectors, spins):
+def edges(odd, vectors, spins):
     _, count, rows, width = vectors.shape
     f32 = jnp.float32
     out = pltpu.VMEM((HALO * 4 * count + 8, width), f32)
     hbm, vmem = pl.BlockSpec(memory_space=pltpu.HBM), pl.BlockSpec(memory_space=pltpu.VMEM)
     return pl.pallas_call(
         edges_kernel,
-        in_specs=[hbm] * 2,
+        in_specs=[pl.BlockSpec(memory_space=pltpu.SMEM)] + [hbm] * 2,
         out_specs=[vmem] * 4,
         out_shape=[out, out, pltpu.VMEM(vectors.shape, vectors.dtype), pltpu.VMEM(spins.shape, f32)],
         scratch_shapes=[
@@ -190,16 +200,17 @@
         ],
         compiler_params=pltpu.CompilerParams(vmem_limit_bytes=16 * MIB),
         name="edges",
-    )(*[pltpu.with_memory_space_constraint(x, pltpu.HBM) for x in (vectors, spins)])
+    )(odd, *[pltpu.with_memory_space_constraint(x, pltpu.HBM) for x in (vectors, spins)])
 
 
 KEPT = REACH + 2
 GROUP = 8
 
 
-def inner_kernel(coef_ref, v_ref, s_ref, f_ref, kept_ref, there_ref, back_ref, rows_ref, r_ref, sp_ref, a_ref, b_ref, sum_ref, acc_ref):
+def inner_kernel(odd_ref, coef_ref, v_ref, s_ref, f_ref, kept_ref, there_ref, back_ref, rows_ref, r_ref, sp_ref, a_ref, b_ref, sum_ref, acc_ref):
     _, count, rows, width = v_ref.shape
     tiles = width // 128
+    odd = odd_ref[0]
     rho = ratios(coef_ref)
 
     there_ref[...] = shuffle(width)
@@ -257,11 +268,11 @@
 
         pass_over(into(a_ref), r_ref, rho[3], own=True)
         pass_over(into(b_ref), a_ref, rho[2])
-        for e in range(2):
+        for side in range(2):
             for i in range(REACH):
-                kept_ref[g, e, i] = r_ref[rows - 1 - i if e else i]
-            kept_ref[g, e, REACH] = a_ref[rows - 1 if e else 0]
-            kept_ref[g, e, REACH + 1] = b_ref[rows - 1 if e else 0]
+                kept_ref[g, side, i] = r_ref[inwards(odd, side, i, rows)]
+            kept_ref[g, side, REACH] = a_ref[inwards(odd, side, 0, rows)]
+            kept_ref[g, side, REACH + 1] = b_ref[inwards(odd, side, 0, rows)]
         pass_over(into(a_ref), b_ref, rho[1])
         pass_over(fields, a_ref, rho[0])
 
@@ -273,7 +284,7 @@
     back_ref[...] = shuffle(width, back=True)
 
 
-def inner(coefficients, vectors, spins):
+def inner(odd, coefficients, vectors, spins):
     _, count, rows, width = vectors.shape
     f32 = jnp.float32
     block = block_of(width)
@@ -282,7 +293,7 @@
     vmem = pl.BlockSpec(memory_space=pltpu.VMEM)
     return pl.pallas_call(
         inner_kernel,
-        in_specs=[pl.BlockSpec(memory_space=pltpu.SMEM), vmem, vmem],
+        in_specs=[pl.BlockSpec(memory_space=pltpu.SMEM)] * 2 + [vmem] * 2,
         out_specs=[vmem] * 4,
         out_shape=[
             jax.ShapeDtypeStruct((3, rows, width), f32),
@@ -302,24 +313,24 @@
         compiler_params=pltpu.CompilerParams(vmem_limit_bytes=40 * MIB),
         cost_estimate=pl.CostEstimate(flops=240 * vectors.size, bytes_accessed=8 * MIB, transcendentals=0),
         name="inner",
-    )(coefficients, vectors, spins)
+    )(odd, coefficients, vectors, spins)
 
 
 SPINS = ("B2", "B1", "A1", "A2", "A3", "B1 to A3")
 
 
-def prepare(kept_ref, low_ref, high_ref, s_ref, there_ref, sp_ref, halo_ref, g_refs, ratio):
+def prepare(odd, kept_ref, far_ref, near_ref, s_ref, there_ref, sp_ref, halo_ref, g_refs, ratio):
     _, rows, width = s_ref.shape
     parts = kept_ref.shape[0]
     tiles = width // 128
     end = HALO * 4 * parts * LANES
     matrix = there_ref[...]
     lines = []
-    for e, ref in enumerate((low_ref, high_ref)):
+    for e, ref in enumerate((far_ref, near_ref)):
         for k in range(3):
             at = end + k * HALO
-            lines += [ref[at + i : at + i + 1] for i in ((1, 0) if e else (0, 1))]
-            lines += [s_ref[k, y : y + 1] for y in ([rows - 1, rows - 2, rows - 3] if e else [0, 1, 2])]
+            lines += [ref[at + i : at + i + 1] for i in (1, 0)]
+            lines += [s_ref[k, pl.ds(inwards(odd, e, i, rows), 1)] for i in range(3)]
     lines = jnp.concatenate(lines + lines[:2], axis=0) * -(coupling / hopping)
     for t, got in enumerate(moved_exactly(lines, matrix)):
         at = pl.ds(t * 128, 128)
@@ -328,7 +339,7 @@
                 five = [got[(e * 3 + k) * 5 + i : (e * 3 + k) * 5 + i + 1] for i in range(5)]
                 for i, row in enumerate(five + [five[1] + five[2] + five[3] + five[4]]):
                     sp_ref[e, i, k, :, at] = jnp.broadcast_to(row, (LANES, 128))
-    for e, ref in enumerate((low_ref, high_ref)):
+    for e, ref in enumerate((far_ref, near_ref)):
         for t, got in enumerate(moved(ref[:end].astype(jnp.bfloat16), matrix)):
             got = got.reshape(HALO, 4, parts, LANES, 128)
             for g in range(parts):
@@ -346,9 +357,12 @@
                 w = plus(w, times(4.0, [x[t] for x in sides]), load(*own(4), t))
                 here = density(load(*b1, t), w) + density(load(*b2, t), a3[t])
                 sums[t] = here if g == 0 else plus(sums[t], here)
+        low = (odd if e == 0 else 1 - odd).astype(jnp.float32)
+        zero = jnp.zeros((LANES, 128), jnp.float32)
         for t, x in enumerate(sums):
-            rows_out = [x[i * 3 + k] for k in range(3) for i in (range(HALO) if e else reversed(range(HALO)))]
-            ref[:, t * 128 : (t + 1) * 128] = side_by_side(rows_out + rows_out[:2])
+            at = pl.ds(t * 128, 128)
+            ref[:8, at] = low * side_by_side([x[i * 3 + k] for k in range(3) for i in range(HALO)] + [zero] * 2)
+            ref[8:, at] = (1.0 - low) * side_by_side([x[i * 3 + k] for k in range(3) for i in (1, 0)] + [zero] * 2)
 
 
 def cross(part, kept_ref, sp_ref, halo_ref, mid_ref, acc_ref, old_ref, rho):
@@ -360,11 +374,20 @@
         own = lambda i: (kept_ref, (part, e, i - 1))
         a_in, b_in = (kept_ref, (part, e, REACH)), (kept_ref, (part, e, REACH + 1))
         b1, b2 = (halo_ref, (part, e, 0)), (halo_ref, (part, e, 1))
-        names = ("a_b2", "a_b1", "b_b2", "b_b1", "b_a1", "c_b1", "c_a1", "c_a2")
+        names = ("a_b2", "a_b1", "b_b2", "b_b1", "b_a1", "c_b1", "c_a1", "c_a2", "b1_sides")
         mid = {name: (mid_ref, (i,)) for i, name in enumerate(names)}
+        b1_sides = mid["b1_sides"]
+
+        b1_tiles = by_tile(b1)
+        for t, x in enumerate(zip(*lateral(b1_tiles))):
+            save(*b1_sides, t, x)
 
         def make(row, at, others, ratio=None, extra=None):
-            for t, x in flat(by_tile(row), spin(at), ratio):
+            if row is b1:
+                made = ((t, plus(load(*b1_sides, t), on_site(load(*b1, t), load(*spin(at), t), ratio))) for t in range(tiles))
+            else:
+                made = flat(by_tile(row), spin(at), ratio)
+            for t, x in made:
                 for ref, place in others:
                     x = plus(x, load(ref, place, t))
                 if extra is not None:
@@ -396,67 +419,63 @@
         fields(3, own(4), ((t, load(*b1, t)) for t in range(tiles)))
 
 
-def begin_kernel(coef_ref, kept_ref, low_ref, high_ref, s_ref, there_ref, sp_ref, halo_ref, g_low_ref, g_high_ref, acc_ref, mid_ref):
+def begin_kernel(odd_ref, coef_ref, kept_ref, far_ref, near_ref, s_ref, there_ref, sp_ref, halo_ref, g_far_ref, g_near_ref):
     rho = ratios(coef_ref)
-    prepare(kept_ref, low_ref, high_ref, s_ref, there_ref, sp_ref, halo_ref, (g_low_ref, g_high_ref), rho[3])
-    cross(0, kept_ref, sp_ref, halo_ref, mid_ref, acc_ref, None, rho)
-
-
-def begin(coefficients, kept, low, high, spins, there):
+    prepare(odd_ref[0], kept_ref, far_ref, near_ref, s_ref, there_ref, sp_ref, halo_ref, (g_far_ref, g_near_ref), rho[3])
+
+
+def begin(odd, coefficients, kept, far, near, spins, there):
     f32 = jnp.float32
     parts, width = kept.shape[0], spins.shape[-1]
     out = [
         (2, len(SPINS), 3, LANES, width),
         (parts, 2, HALO, 4, LANES, width),
-        (8, width),
-        (8, width),
-        (2, REACH, 3, LANES, width),
+        (16, width),
+        (16, width),
     ]
     vmem = pl.BlockSpec(memory_space=pltpu.VMEM)
     return pl.pallas_call(
         begin_kernel,
-        in_specs=[pl.BlockSpec(memory_space=pltpu.SMEM)] + [vmem] * 5,
+        in_specs=[pl.BlockSpec(memory_space=pltpu.SMEM)] * 2 + [vmem] * 5,
         out_specs=[vmem] * len(out),
         out_shape=[jax.ShapeDtypeStruct(x, f32) for x in out],
-        scratch_shapes=[pltpu.VMEM((8, 4, LANES, width), f32)],
         compiler_params=pltpu.CompilerParams(vmem_limit_bytes=32 * MIB),
-        cost_estimate=pl.CostEstimate(flops=500 * low.size, bytes_accessed=4 * MIB, transcendentals=0),
+        cost_estimate=pl.CostEstimate(flops=500 * far.size, bytes_accessed=4 * MIB, transcendentals=0),
         name="begin",
-    )(coefficients, kept, low, high, spins, there)
-
-
-def end_kernel(coef_ref, kept_ref, sp_ref, halo_ref, old_ref, f_ref, out_ref, mid_ref, acc_ref):
+    )(odd, coefficients, kept, far, near, spins, there)
+
+
+def end_kernel(odd_ref, coef_ref, kept_ref, sp_ref, halo_ref, f_ref, out_ref, mid_ref, acc_ref):
     _, rows, width = f_ref.shape
     parts = kept_ref.shape[0]
     rho = ratios(coef_ref)
-    for part in range(1, parts):
-        cross(part, kept_ref, sp_ref, halo_ref, mid_ref, acc_ref, old_ref if part == 1 else acc_ref, rho)
-    last_ref = acc_ref if parts > 1 else old_ref
+    for part in range(parts):
+        cross(part, kept_ref, sp_ref, halo_ref, mid_ref, acc_ref, acc_ref if part else None, rho)
     out_ref[...] = f_ref[...]
     half = lax.broadcasted_iota(jnp.int32, (8, 128), 0) < REACH
     for t in range(width // 128):
         at = pl.ds(t * 128, 128)
         for k in range(3):
-            low = [last_ref[0, i, k, :, at] for i in range(REACH)]
-            high = [last_ref[1, i, k, :, at] for i in reversed(range(REACH))]
+            low = [acc_ref[odd_ref[0], i, k, :, at] for i in range(REACH)]
+            high = [acc_ref[1 - odd_ref[0], i, k, :, at] for i in reversed(range(REACH))]
             edge = side_by_side(low + high)
             out_ref[k, :8, at] += jnp.where(half, edge, 0.0)
             out_ref[k, rows - 8 :, at] += jnp.where(half, 0.0, edge)
 
 
-def end(coefficients, kept, sp, halo, old, f):
+def end(odd, coefficients, kept, sp, halo, f):
     f32 = jnp.float32
     vmem = pl.BlockSpec(memory_space=pltpu.VMEM)
     return pl.pallas_call(
         end_kernel,
-        in_specs=[pl.BlockSpec(memory_space=pltpu.SMEM)] + [vmem] * 5,
+        in_specs=[pl.BlockSpec(memory_space=pltpu.SMEM)] * 2 + [vmem] * 4,
         out_specs=vmem,
         out_shape=jax.ShapeDtypeStruct(f.shape, f32),
-        scratch_shapes=[pltpu.VMEM((8, 4, LANES, f.shape[-1]), f32), pltpu.VMEM(old.shape, f32)],
+        scratch_shapes=[pltpu.VMEM((9, 4, LANES, f.shape[-1]), f32), pltpu.VMEM((2, REACH, 3, LANES, f.shape[-1]), f32)],
         compiler_params=pltpu.CompilerParams(vmem_limit_bytes=32 * MIB),
         cost_estimate=pl.CostEstimate(flops=300 * kept.size, bytes_accessed=3 * MIB, transcendentals=0),
         name="end",
-    )(coefficients, kept, sp, halo, old, f)
+    )(odd, coefficients, kept, sp, halo, f)
 
 
 def sine_and_cosine(x):
@@ -514,8 +533,8 @@
     across, number = lax.axis_size("vec"), lax.axis_size("lat")
     count_all = vectors.shape[1] * across
 
-    def to_row(x, on):
-        return lax.ppermute(x, "lat", [(i, (i + on) % number) for i in range(number)])
+    def trade(x, side):
+        return lax.ppermute(x, "lat", [(i, (i + (1 if i % 2 != side else -1)) % number) for i in range(number)])
 
     def swap(x, step):
         steps = across.bit_length() - 1
@@ -524,14 +543,16 @@
         return lax.ppermute(x, ("lat", "vec"), pairs)
 
     rows, width = classical_spins.shape[1:]
-    low, high, vectors, spins = edges(vectors, classical_spins)
-    from_below, from_above = to_row(high, 1), to_row(low, -1)
-    f, kept, there, back = inner(coefficients, vectors, spins)
-    sp, halo, g_low, g_high, crossed = begin(coefficients, kept, from_below, from_above, spins, there)
-    below, above = to_row(g_high, 1), to_row(g_low, -1)
-    fields = end(coefficients, kept, sp, halo, crossed, f)
+    odd = jnp.full((1,), lax.rem(lax.axis_index("lat"), 2), jnp.int32)
+    far, near, vectors, spins = edges(odd, vectors, classical_spins)
+    far, near = trade(far, 0), trade(near, 1)
+    f, kept, there, back = inner(odd, coefficients, vectors, spins)
+    sp, halo, g_far, g_near = begin(odd, coefficients, kept, far, near, spins, there)
+    g_far, g_near = trade(g_far, 0), trade(g_near, 1)
+    fields = end(odd, coefficients, kept, sp, halo, f)
     lines = lambda x: x[: 3 * HALO].reshape(3, HALO, width)
-    fields = fields.at[:, :HALO].add(lines(below)).at[:, rows - HALO :].add(lines(above))
+    given = g_far + g_near
+    fields = fields.at[:, :HALO].add(lines(given)).at[:, rows - HALO :].add(lines(given[8:]))
     steps = across.bit_length() - 1
     if across != 1 << steps or steps == 0:
         return final(coefficients, spins, back, count_all, lax.psum(fields, "vec"), jnp.zeros_like(fields))

time: 41.5 us -> 40.8 us (0.983)
  starting transfers between devices: 12.2 us -> 11.1 us
    pallas_call x1, Pallas kernels: 3.13 us -> 1.61 us  [begin(): pl.pallas_call(begin_kernel, in_specs=[pl.BlockSpec(memory_space=pltpu.SM...]
    pallas_call x1, Pallas kernels: 2.27 us -> 3.62 us  [end(): pl.pallas_call(end_kernel, in_specs=[pl.BlockSpec(memory_space=pltpu.SMEM...]
    ppermute x4, starting transfers between devices: 8.2 us -> 7.12 us  [trade(): lax.ppermute(x, 'lat', [(i, (i + (1 if i % 2 != side else -1)) % number)...]
  transfers between devices with their start and end apart: 6 -> 6, of which waited for: 2 -> 3; matrix products, arithmetic and copies ran while one was open for 0% -> 0% of each run, Pallas kernels for 34% -> 39%
where the time goes in v6:
time: 40.8 us; the launch traced here: 40.7 us
  Pallas kernels  20.9 us (51%)
  starting transfers between devices  11.1 us (27%)
  waiting for transfers between devices  7.8 us (19%)
  between operations  0.73 us (2%)
    pallas_call x1, Pallas kernels, inner(): pl.pallas_call(inner_kernel, in_specs=[pl.BlockSpec(memory_space=pltpu.SM...  12.1 us
    ppermute x2, waiting for transfers between devices, swap(): return lax.ppermute(x, ('lat', 'vec'), pairs)  7.51 us
    ppermute x4, starting transfers between devices, trade(): lax.ppermute(x, 'lat', [(i, (i + (1 if i % 2 != side else -1)) % number)...  7.12 us
    ppermute x2, starting transfers between devices, swap(): return lax.ppermute(x, ('lat', 'vec'), pairs)  3.95 us
    pallas_call x1, Pallas kernels, end(): pl.pallas_call(end_kernel, in_specs=[pl.BlockSpec(memory_space=pltpu.SMEM...  3.62 us
    pallas_call x1, Pallas kernels, edges(): pl.pallas_call(edges_kernel, in_specs=[pl.BlockSpec(memory_space=pltpu.SM...  1.96 us
    pallas_call x1, Pallas kernels, final(): pl.pallas_call(functools.partial(final_kernel, count_all), in_specs=[pl.B...  1.69 us
    pallas_call x1, Pallas kernels, begin(): pl.pallas_call(begin_kernel, in_specs=[pl.BlockSpec(memory_space=pltpu.SM...  1.61 us
  transfers between devices with their start and end apart: 6, of which 3 were waited for; matrix products, arithmetic and copies ran while one was open for 0% of the time, Pallas kernels for 39%

profile of v6, /device:TPU:0, one launch (start us, length us, event | category | flops | bytes accessed | tf_op | source)
XLA Modules:
  0.0 40.7 jit_solution(16920330227641120155)
XLA Ops:
  0.6 0.0 copy-start
  0.6 2.0 %edges.1 = (f32[136,1024]{1,0:T(8,128)S(1)}, f32[136,1024]{1,0:T(8,128)S(1)}, bf16[4,16,16,1024]{3,2,1,0:T(8,128)(2,1)S(1)}, f32[3,16,1024]{2,1,0:T(8,128)S(1)}) custom-call(s32[1]{0:T(128)} %bitcast.odd_ref, bf16[4,16,16,1024]{3,2,1,0:T(8,128)(2,1)} %v_hbm.1, f32[3,16,1024]{2,1,0:T(8,128)} %s_hbm.1), custom_call_target="tpu_custom_call" | custom-call | tf_op jit(solution)/shard_map/edges/pallas_call | solution.py:191
  2.6 4.5 %collective-permute-start = (f32[136,1024]{1,0:T(8,128)S(1)}, f32[136,1024]{1,0:T(8,128)S(1)}, u32[]{:S(2)}, u32[]{:S(2)}) collective-permute-start(f32[136,1024]{1,0:T(8,128)S(1)} %get-tuple-element.42), channel_id=1, source_target_pairs={{0,28},{4,8},{8,4},{12,16},{16,12},{20,24},{24,20},{28,0},{1,29},{... | collective-permute-start | bytes 1671176 | tf_op jit(solution)/shard_map/ppermute | solution.py:537
  7.2 0.0 collective-permute-start.1
  7.2 0.0 copy-done
  7.2 12.1 %inner.1 = (f32[3,16,1024]{2,1,0:T(8,128)S(1)}, f32[2,2,6,4,8,1024]{5,4,3,2,1,0:T(8,128)S(1)}, bf16[512,512]{1,0:T(8,128)(2,1)S(1)}, bf16[512,512]{1,0:T(8,128)(2,1)S(1)}) custom-call(s32[1]{0:T(128)} %bitcast.odd_ref, f32[5]{0:T(128)S(1)} %copy-done, bf16[4,16,16,1024]{3,2,1,0:T(8,128)(2,1)S(1)} %get-tuple-element.39.v_ref, ...), custom_call_target="tpu_custom_call" | custom-call | flops 251658240 | bytes 8388608 | tf_op jit(solution)/shard_map/inner/pallas_call | solution.py:294
  19.2 0.3 collective-permute-done.far_ref
  19.5 0.0 collective-permute-done.1.near_ref
  19.5 1.6 %begin.1 = (f32[2,6,3,8,1024]{4,3,2,1,0:T(8,128)S(1)}, f32[2,2,2,4,8,1024]{5,4,3,2,1,0:T(8,128)S(1)}, f32[16,1024]{1,0:T(8,128)S(1)}, f32[16,1024]{1,0:T(8,128)S(1)}) custom-call(s32[1]{0:T(128)} %bitcast.odd_ref, f32[5]{0:T(128)S(1)} %copy-done, f32[2,2,6,4,8,1024]{5,4,3,2,1,0:T(8,128)S(1)} %get-tuple-element.41.kept_ref, ...), custom_call_target="tpu_custom_call" | custom-call | flops 69632000 | bytes 4194304 | tf_op jit(solution)/shard_map/begin/pallas_call | solution.py:437
  21.1 2.6 %collective-permute-start.2 = (f32[16,1024]{1,0:T(8,128)S(1)}, f32[16,1024]{1,0:T(8,128)S(1)}, u32[]{:S(2)}, u32[]{:S(2)}) collective-permute-start(f32[16,1024]{1,0:T(8,128)S(1)} %get-tuple-element.48), channel_id=1, source_target_pairs={{0,28},{4,8},{8,4},{12,16},{16,12},{20,24},{24,20},{28,0},{1,29},{... | collective-permute-start | bytes 196616 | tf_op jit(solution)/shard_map/ppermute | solution.py:537
  23.7 0.0 collective-permute-start.3
  23.7 3.6 %end.1 = f32[3,16,1024]{2,1,0:T(8,128)S(1)} custom-call(s32[1]{0:T(128)} %bitcast.odd_ref, f32[5]{0:T(128)S(1)} %copy-done, f32[2,2,6,4,8,1024]{5,4,3,2,1,0:T(8,128)S(1)} %get-tuple-element.41.kept_ref, f32[2,6,3,8,1024]{4,3,2,1,0:T(8,128)S(1)} %get-tuple-element.45.sp_ref, f32[2,2,2,4,8,1024]{5,4,3,2,1,0:T(8,128)S(1)} %get-tuple-element.46.halo_ref, ...), custom_call_target="tpu_custom_call" | custom-call | flops 235929600 | bytes 3145728 | tf_op jit(solution)/shard_map/end/pallas_call | solution.py:469
  27.3 0.0 collective-permute-done.2
  27.3 0.0 collective-permute-done.3
  27.5 2.0 %collective-permute-start.4 = (f32[3,16,1024]{2,1,0:T(8,128)S(1)}, f32[3,16,1024]{2,1,0:T(8,128)S(1)}, u32[]{:S(2)}, u32[]{:S(2)}) collective-permute-start(f32[3,16,1024]{2,1,0:T(8,128)S(1)} %fusion), channel_id=1, source_target_pairs={{0,1},{1,0},{2,3},{3,2},{4,6},{5,7},{6,4},{7,5},{8,9},{9,8},{10,11... | collective-permute-start | bytes 589832 | tf_op jit(solution)/shard_map/ppermute | solution.py:543
  29.5 3.8 %collective-permute-done.4 = f32[3,16,1024]{2,1,0:T(8,128)S(1)} collective-permute-done((f32[3,16,1024]{2,1,0:T(8,128)S(1)}, f32[3,16,1024]{2,1,0:T(8,128)S(1)}, u32[]{:S(2)}, u32[]{:S(2)}) %collective-permute-start.4) | collective-permute-done | bytes 196640 | tf_op jit(solution)/shard_map/ppermute | solution.py:543
  33.3 2.0 %collective-permute-start.5 = (f32[3,16,1024]{2,1,0:T(8,128)S(1)}, f32[3,16,1024]{2,1,0:T(8,128)S(1)}, u32[]{:S(2)}, u32[]{:S(2)}) collective-permute-start(f32[3,16,1024]{2,1,0:T(8,128)S(1)} %add.23.f_ref), channel_id=1, source_target_pairs={{0,2},{1,3},{2,0},{3,1},{4,5},{5,4},{6,7},{7,6},{8,10},{9,11},{10,... | collective-permute-start | bytes 589832 | tf_op jit(solution)/shard_map/ppermute | solution.py:543
  35.3 3.7 %collective-permute-done.5.other_ref = f32[3,16,1024]{2,1,0:T(8,128)S(1)} collective-permute-done((f32[3,16,1024]{2,1,0:T(8,128)S(1)}, f32[3,16,1024]{2,1,0:T(8,128)S(1)}, u32[]{:S(2)}, u32[]{:S(2)}) %collective-permute-start.5) | collective-permute-done | bytes 196640 | tf_op jit(solution)/shard_map/ppermute | solution.py:543
  39.0 1.7 %final.1 = (f32[3,16,1024]{2,1,0:T(8,128)}, f32[3,16,1024]{2,1,0:T(8,128)}) custom-call(f32[5]{0:T(128)S(1)} %copy-done, f32[3,16,1024]{2,1,0:T(8,128)S(1)} %get-tuple-element.38.s_ref, bf16[512,512]{1,0:T(8,128)(2,1)S(1)} %get-tuple-element.40.back_ref, f32[3,16,1024]{2,1,0:T(8,128)S(1)} %add.23.f_ref, f32[3,16,1024]{2,1,0:T(8,128)S(1)} %collective-permute-done.5.other_ref), custom_call_target="tpu_custom_call" | custom-call | tf_op jit(solution)/shard_map/final/pallas_call | solution.py:522
  (7 shorter events, 0.1 us)
Async XLA Ops:
  0.6 6.5 %copy-start = (f32[5]{0:T(128)S(1)}, f32[5]{0:T(128)}, u32[]{:S(2)}) copy-start(f32[5]{0:T(128)} %coef_ref.7) | copy-start | bytes 64
  2.6 16.9 %collective-permute-start = (f32[136,1024]{1,0:T(8,128)S(1)}, f32[136,1024]{1,0:T(8,128)S(1)}, u32[]{:S(2)}, u32[]{:S(2)}) collective-permute-start(f32[136,1024]{1,0:T(8,128)S(1)} %get-tuple-element.42), channel_id=1, source_target_pairs={{0,28},{4,8},{8,4},{12,16},{16,12},{20,24},{24,20},{28,0},{1,29},{... | collective-permute-start | bytes 1671176 | tf_op jit(solution)/shard_map/ppermute | solution.py:537
  7.2 12.3 %collective-permute-start.1 = (f32[136,1024]{1,0:T(8,128)S(1)}, f32[136,1024]{1,0:T(8,128)S(1)}, u32[]{:S(2)}, u32[]{:S(2)}) collective-permute-start(f32[136,1024]{1,0:T(8,128)S(1)} %get-tuple-element.43), channel_id=1, source_target_pairs={{0,4},{4,0},{8,12},{12,8},{16,20},{20,16},{24,28},{28,24},{1,5},{5... | collective-permute-start | bytes 1671176 | tf_op jit(solution)/shard_map/ppermute | solution.py:537
  21.1 6.2 %collective-permute-start.2 = (f32[16,1024]{1,0:T(8,128)S(1)}, f32[16,1024]{1,0:T(8,128)S(1)}, u32[]{:S(2)}, u32[]{:S(2)}) collective-permute-start(f32[16,1024]{1,0:T(8,128)S(1)} %get-tuple-element.48), channel_id=1, source_target_pairs={{0,28},{4,8},{8,4},{12,16},{16,12},{20,24},{24,20},{28,0},{1,29},{... | collective-permute-start | bytes 196616 | tf_op jit(solution)/shard_map/ppermute | solution.py:537
  23.7 3.6 %collective-permute-start.3 = (f32[16,1024]{1,0:T(8,128)S(1)}, f32[16,1024]{1,0:T(8,128)S(1)}, u32[]{:S(2)}, u32[]{:S(2)}) collective-permute-start(f32[16,1024]{1,0:T(8,128)S(1)} %get-tuple-element.49), channel_id=1, source_target_pairs={{0,4},{4,0},{8,12},{12,8},{16,20},{20,16},{24,28},{28,24},{1,5},{5... | collective-permute-start | bytes 196616 | tf_op jit(solution)/shard_map/ppermute | solution.py:537
  27.5 5.7 %collective-permute-start.4 = (f32[3,16,1024]{2,1,0:T(8,128)S(1)}, f32[3,16,1024]{2,1,0:T(8,128)S(1)}, u32[]{:S(2)}, u32[]{:S(2)}) collective-permute-start(f32[3,16,1024]{2,1,0:T(8,128)S(1)} %fusion), channel_id=1, source_target_pairs={{0,1},{1,0},{2,3},{3,2},{4,6},{5,7},{6,4},{7,5},{8,9},{9,8},{10,11... | collective-permute-start | bytes 589832 | tf_op jit(solution)/shard_map/ppermute | solution.py:543
  33.3 5.7 %collective-permute-start.5 = (f32[3,16,1024]{2,1,0:T(8,128)S(1)}, f32[3,16,1024]{2,1,0:T(8,128)S(1)}, u32[]{:S(2)}, u32[]{:S(2)}) collective-permute-start(f32[3,16,1024]{2,1,0:T(8,128)S(1)} %add.23.f_ref), channel_id=1, source_target_pairs={{0,2},{1,3},{2,0},{3,1},{4,5},{5,4},{6,7},{7,6},{8,10},{9,11},{10,... | collective-permute-start | bytes 589832 | tf_op jit(solution)/shard_map/ppermute | solution.py:543

commit v7 on v6

--- a/solution.py
+++ b/solution.py
@@ -368,14 +368,13 @@
 def cross(part, kept_ref, sp_ref, halo_ref, mid_ref, acc_ref, old_ref, rho):
     tiles = halo_ref.shape[-1] // 128
 
-    @pl.loop(0, 2)
-    def _(e):
+    def one_edge(e):
         spin = lambda name: (sp_ref, (e, SPINS.index(name)))
         own = lambda i: (kept_ref, (part, e, i - 1))
         a_in, b_in = (kept_ref, (part, e, REACH)), (kept_ref, (part, e, REACH + 1))
         b1, b2 = (halo_ref, (part, e, 0)), (halo_ref, (part, e, 1))
         names = ("a_b2", "a_b1", "b_b2", "b_b1", "b_a1", "c_b1", "c_a1", "c_a2", "b1_sides")
-        mid = {name: (mid_ref, (i,)) for i, name in enumerate(names)}
+        mid = {name: (mid_ref, (e, i)) for i, name in enumerate(names)}
         b1_sides = mid["b1_sides"]
 
         b1_tiles = by_tile(b1)
@@ -417,6 +416,9 @@
         fields(1, own(2), make(mid["c_a2"], "A2", [mid["c_a1"], b1]))
         fields(2, own(3), make(b1, "A3", [mid["c_a2"]]))
         fields(3, own(4), ((t, load(*b1, t)) for t in range(tiles)))
+
+    for e in range(2):
+        one_edge(e)
 
 
 def begin_kernel(odd_ref, coef_ref, kept_ref, far_ref, near_ref, s_ref, there_ref, sp_ref, halo_ref, g_far_ref, g_near_ref):
@@ -471,7 +473,7 @@
         in_specs=[pl.BlockSpec(memory_space=pltpu.SMEM)] * 2 + [vmem] * 4,
         out_specs=vmem,
         out_shape=jax.ShapeDtypeStruct(f.shape, f32),
-        scratch_shapes=[pltpu.VMEM((9, 4, LANES, f.shape[-1]), f32), pltpu.VMEM((2, REACH, 3, LANES, f.shape[-1]), f32)],
+        scratch_shapes=[pltpu.VMEM((2, 9, 4, LANES, f.shape[-1]), f32), pltpu.VMEM((2, REACH, 3, LANES, f.shape[-1]), f32)],
         compiler_params=pltpu.CompilerParams(vmem_limit_bytes=32 * MIB),
         cost_estimate=pl.CostEstimate(flops=300 * kept.size, bytes_accessed=3 * MIB, transcendentals=0),
         name="end",

time: 40.8 us -> 40.8 us (level)
  transfers between devices with their start and end apart: 6 -> 6, of which waited for: 3 -> 3; matrix products, arithmetic and copies ran while one was open for 0% -> 0% of each run, Pallas kernels for 39% -> 38%
where the time goes in v7:
time: 40.8 us; the launch traced here: 40.7 us
  Pallas kernels  20.9 us (51%)
  starting transfers between devices  11.1 us (27%)
  waiting for transfers between devices  7.76 us (19%)
  between operations  0.73 us (2%)
    pallas_call x1, Pallas kernels, inner(): pl.pallas_call(inner_kernel, in_specs=[pl.BlockSpec(memory_space=pltpu.SM...  12.1 us
    ppermute x2, waiting for transfers between devices, swap(): return lax.ppermute(x, ('lat', 'vec'), pairs)  7.48 us
    ppermute x4, starting transfers between devices, trade(): lax.ppermute(x, 'lat', [(i, (i + (1 if i % 2 != side else -1)) % number)...  7.12 us
    ppermute x2, starting transfers between devices, swap(): return lax.ppermute(x, ('lat', 'vec'), pairs)  3.99 us
    pallas_call x1, Pallas kernels, end(): pl.pallas_call(end_kernel, in_specs=[pl.BlockSpec(memory_space=pltpu.SMEM...  3.6 us
    pallas_call x1, Pallas kernels, edges(): pl.pallas_call(edges_kernel, in_specs=[pl.BlockSpec(memory_space=pltpu.SM...  1.96 us
    pallas_call x1, Pallas kernels, final(): pl.pallas_call(functools.partial(final_kernel, count_all), in_specs=[pl.B...  1.69 us
    pallas_call x1, Pallas kernels, begin(): pl.pallas_call(begin_kernel, in_specs=[pl.BlockSpec(memory_space=pltpu.SM...  1.61 us
  transfers between devices with their start and end apart: 6, of which 3 were waited for; matrix products, arithmetic and copies ran while one was open for 0% of the time, Pallas kernels for 38%

profile of v7, /device:TPU:0, one launch (start us, length us, event | category | flops | bytes accessed | tf_op | source)
XLA Modules:
  0.0 40.7 jit_solution(6145715452202312432)
XLA Ops:
  0.6 0.0 copy-start
  0.6 2.0 %edges.1 = (f32[136,1024]{1,0:T(8,128)S(1)}, f32[136,1024]{1,0:T(8,128)S(1)}, bf16[4,16,16,1024]{3,2,1,0:T(8,128)(2,1)S(1)}, f32[3,16,1024]{2,1,0:T(8,128)S(1)}) custom-call(s32[1]{0:T(128)} %bitcast.odd_ref, bf16[4,16,16,1024]{3,2,1,0:T(8,128)(2,1)} %v_hbm.1, f32[3,16,1024]{2,1,0:T(8,128)} %s_hbm.1), custom_call_target="tpu_custom_call" | custom-call | tf_op jit(solution)/shard_map/edges/pallas_call | solution.py:191
  2.6 4.5 %collective-permute-start = (f32[136,1024]{1,0:T(8,128)S(1)}, f32[136,1024]{1,0:T(8,128)S(1)}, u32[]{:S(2)}, u32[]{:S(2)}) collective-permute-start(f32[136,1024]{1,0:T(8,128)S(1)} %get-tuple-element.42), channel_id=1, source_target_pairs={{0,28},{4,8},{8,4},{12,16},{16,12},{20,24},{24,20},{28,0},{1,29},{... | collective-permute-start | bytes 1671176 | tf_op jit(solution)/shard_map/ppermute | solution.py:539
  7.2 0.0 collective-permute-start.1
  7.2 0.0 copy-done
  7.2 12.1 %inner.1 = (f32[3,16,1024]{2,1,0:T(8,128)S(1)}, f32[2,2,6,4,8,1024]{5,4,3,2,1,0:T(8,128)S(1)}, bf16[512,512]{1,0:T(8,128)(2,1)S(1)}, bf16[512,512]{1,0:T(8,128)(2,1)S(1)}) custom-call(s32[1]{0:T(128)} %bitcast.odd_ref, f32[5]{0:T(128)S(1)} %copy-done, bf16[4,16,16,1024]{3,2,1,0:T(8,128)(2,1)S(1)} %get-tuple-element.39.v_ref, ...), custom_call_target="tpu_custom_call" | custom-call | flops 251658240 | bytes 8388608 | tf_op jit(solution)/shard_map/inner/pallas_call | solution.py:294
  19.2 0.3 collective-permute-done.far_ref
  19.5 0.0 collective-permute-done.1.near_ref
  19.5 1.6 %begin.1 = (f32[2,6,3,8,1024]{4,3,2,1,0:T(8,128)S(1)}, f32[2,2,2,4,8,1024]{5,4,3,2,1,0:T(8,128)S(1)}, f32[16,1024]{1,0:T(8,128)S(1)}, f32[16,1024]{1,0:T(8,128)S(1)}) custom-call(s32[1]{0:T(128)} %bitcast.odd_ref, f32[5]{0:T(128)S(1)} %copy-done, f32[2,2,6,4,8,1024]{5,4,3,2,1,0:T(8,128)S(1)} %get-tuple-element.41.kept_ref, ...), custom_call_target="tpu_custom_call" | custom-call | flops 69632000 | bytes 4194304 | tf_op jit(solution)/shard_map/begin/pallas_call | solution.py:439
  21.1 2.6 %collective-permute-start.2 = (f32[16,1024]{1,0:T(8,128)S(1)}, f32[16,1024]{1,0:T(8,128)S(1)}, u32[]{:S(2)}, u32[]{:S(2)}) collective-permute-start(f32[16,1024]{1,0:T(8,128)S(1)} %get-tuple-element.48), channel_id=1, source_target_pairs={{0,28},{4,8},{8,4},{12,16},{16,12},{20,24},{24,20},{28,0},{1,29},{... | collective-permute-start | bytes 196616 | tf_op jit(solution)/shard_map/ppermute | solution.py:539
  23.7 0.0 collective-permute-start.3
  23.7 3.6 %end.1 = f32[3,16,1024]{2,1,0:T(8,128)S(1)} custom-call(s32[1]{0:T(128)} %bitcast.odd_ref, f32[5]{0:T(128)S(1)} %copy-done, f32[2,2,6,4,8,1024]{5,4,3,2,1,0:T(8,128)S(1)} %get-tuple-element.41.kept_ref, f32[2,6,3,8,1024]{4,3,2,1,0:T(8,128)S(1)} %get-tuple-element.45.sp_ref, f32[2,2,2,4,8,1024]{5,4,3,2,1,0:T(8,128)S(1)} %get-tuple-element.46.halo_ref, ...), custom_call_target="tpu_custom_call" | custom-call | flops 235929600 | bytes 3145728 | tf_op jit(solution)/shard_map/end/pallas_call | solution.py:471
  27.3 0.0 collective-permute-done.2
  27.3 0.0 collective-permute-done.3
  27.5 2.0 %collective-permute-start.4 = (f32[3,16,1024]{2,1,0:T(8,128)S(1)}, f32[3,16,1024]{2,1,0:T(8,128)S(1)}, u32[]{:S(2)}, u32[]{:S(2)}) collective-permute-start(f32[3,16,1024]{2,1,0:T(8,128)S(1)} %fusion), channel_id=1, source_target_pairs={{0,1},{1,0},{2,3},{3,2},{4,6},{5,7},{6,4},{7,5},{8,9},{9,8},{10,11... | collective-permute-start | bytes 589832 | tf_op jit(solution)/shard_map/ppermute | solution.py:545
  29.5 3.8 %collective-permute-done.4 = f32[3,16,1024]{2,1,0:T(8,128)S(1)} collective-permute-done((f32[3,16,1024]{2,1,0:T(8,128)S(1)}, f32[3,16,1024]{2,1,0:T(8,128)S(1)}, u32[]{:S(2)}, u32[]{:S(2)}) %collective-permute-start.4) | collective-permute-done | bytes 196640 | tf_op jit(solution)/shard_map/ppermute | solution.py:545
  33.2 2.0 %collective-permute-start.5 = (f32[3,16,1024]{2,1,0:T(8,128)S(1)}, f32[3,16,1024]{2,1,0:T(8,128)S(1)}, u32[]{:S(2)}, u32[]{:S(2)}) collective-permute-start(f32[3,16,1024]{2,1,0:T(8,128)S(1)} %add.23.f_ref), channel_id=1, source_target_pairs={{0,2},{1,3},{2,0},{3,1},{4,5},{5,4},{6,7},{7,6},{8,10},{9,11},{10,... | collective-permute-start | bytes 589832 | tf_op jit(solution)/shard_map/ppermute | solution.py:545
  35.3 3.7 %collective-permute-done.5.other_ref = f32[3,16,1024]{2,1,0:T(8,128)S(1)} collective-permute-done((f32[3,16,1024]{2,1,0:T(8,128)S(1)}, f32[3,16,1024]{2,1,0:T(8,128)S(1)}, u32[]{:S(2)}, u32[]{:S(2)}) %collective-permute-start.5) | collective-permute-done | bytes 196640 | tf_op jit(solution)/shard_map/ppermute | solution.py:545
  39.0 1.7 %final.1 = (f32[3,16,1024]{2,1,0:T(8,128)}, f32[3,16,1024]{2,1,0:T(8,128)}) custom-call(f32[5]{0:T(128)S(1)} %copy-done, f32[3,16,1024]{2,1,0:T(8,128)S(1)} %get-tuple-element.38.s_ref, bf16[512,512]{1,0:T(8,128)(2,1)S(1)} %get-tuple-element.40.back_ref, f32[3,16,1024]{2,1,0:T(8,128)S(1)} %add.23.f_ref, f32[3,16,1024]{2,1,0:T(8,128)S(1)} %collective-permute-done.5.other_ref), custom_call_target="tpu_custom_call" | custom-call | tf_op jit(solution)/shard_map/final/pallas_call | solution.py:524
  (7 shorter events, 0.1 us)
Async XLA Ops:
  0.6 6.5 %copy-start = (f32[5]{0:T(128)S(1)}, f32[5]{0:T(128)}, u32[]{:S(2)}) copy-start(f32[5]{0:T(128)} %coef_ref.7) | copy-start | bytes 64
  2.6 16.9 %collective-permute-start = (f32[136,1024]{1,0:T(8,128)S(1)}, f32[136,1024]{1,0:T(8,128)S(1)}, u32[]{:S(2)}, u32[]{:S(2)}) collective-permute-start(f32[136,1024]{1,0:T(8,128)S(1)} %get-tuple-element.42), channel_id=1, source_target_pairs={{0,28},{4,8},{8,4},{12,16},{16,12},{20,24},{24,20},{28,0},{1,29},{... | collective-permute-start | bytes 1671176 | tf_op jit(solution)/shard_map/ppermute | solution.py:539
  7.2 12.3 %collective-permute-start.1 = (f32[136,1024]{1,0:T(8,128)S(1)}, f32[136,1024]{1,0:T(8,128)S(1)}, u32[]{:S(2)}, u32[]{:S(2)}) collective-permute-start(f32[136,1024]{1,0:T(8,128)S(1)} %get-tuple-element.43), channel_id=1, source_target_pairs={{0,4},{4,0},{8,12},{12,8},{16,20},{20,16},{24,28},{28,24},{1,5},{5... | collective-permute-start | bytes 1671176 | tf_op jit(solution)/shard_map/ppermute | solution.py:539
  21.1 6.2 %collective-permute-start.2 = (f32[16,1024]{1,0:T(8,128)S(1)}, f32[16,1024]{1,0:T(8,128)S(1)}, u32[]{:S(2)}, u32[]{:S(2)}) collective-permute-start(f32[16,1024]{1,0:T(8,128)S(1)} %get-tuple-element.48), channel_id=1, source_target_pairs={{0,28},{4,8},{8,4},{12,16},{16,12},{20,24},{24,20},{28,0},{1,29},{... | collective-permute-start | bytes 196616 | tf_op jit(solution)/shard_map/ppermute | solution.py:539
  23.7 3.6 %collective-permute-start.3 = (f32[16,1024]{1,0:T(8,128)S(1)}, f32[16,1024]{1,0:T(8,128)S(1)}, u32[]{:S(2)}, u32[]{:S(2)}) collective-permute-start(f32[16,1024]{1,0:T(8,128)S(1)} %get-tuple-element.49), channel_id=1, source_target_pairs={{0,4},{4,0},{8,12},{12,8},{16,20},{20,16},{24,28},{28,24},{1,5},{5... | collective-permute-start | bytes 196616 | tf_op jit(solution)/shard_map/ppermute | solution.py:539
  27.5 5.7 %collective-permute-start.4 = (f32[3,16,1024]{2,1,0:T(8,128)S(1)}, f32[3,16,1024]{2,1,0:T(8,128)S(1)}, u32[]{:S(2)}, u32[]{:S(2)}) collective-permute-start(f32[3,16,1024]{2,1,0:T(8,128)S(1)} %fusion), channel_id=1, source_target_pairs={{0,1},{1,0},{2,3},{3,2},{4,6},{5,7},{6,4},{7,5},{8,9},{9,8},{10,11... | collective-permute-start | bytes 589832 | tf_op jit(solution)/shard_map/ppermute | solution.py:545
  33.2 5.7 %collective-permute-start.5 = (f32[3,16,1024]{2,1,0:T(8,128)S(1)}, f32[3,16,1024]{2,1,0:T(8,128)S(1)}, u32[]{:S(2)}, u32[]{:S(2)}) collective-permute-start(f32[3,16,1024]{2,1,0:T(8,128)S(1)} %add.23.f_ref), channel_id=1, source_target_pairs={{0,2},{1,3},{2,0},{3,1},{4,5},{5,4},{6,7},{7,6},{8,10},{9,11},{10,... | collective-permute-start | bytes 589832 | tf_op jit(solution)/shard_map/ppermute | solution.py:545
